TPU v7x, 32 devices: a whole 2x2x4 slice. The times are simulated.
32 devices in a mesh: dp: 8 (over y, x, core), tensor: 4 (over z).
Axes of the slice: x: 2, y: 2, z: 4, core: 2. Of those that a mesh axis runs over, the one named last changes fastest.
Arguments:
- inputs: bfloat16 [8192, 1536], P(('dp', 'tensor')), may hold values from -6 to 6
- segment_ids: int32 [8192], P('dp'), may hold values from 0 to 255, as said below
- first_gain: bfloat16 [1536], P('dp'), may hold values from 0.5 to 1.5
- query_weight: bfloat16 [1536, 1536], P('dp', 'tensor'), may hold values from -0.15625 to 0.15625
- query_bias: bfloat16 [1536], P(('tensor', 'dp')), may hold values from -3 to 3
- key_value_weight: bfloat16 [1536, 512], P('dp'), may hold values from -0.15625 to 0.15625
- key_value_bias: bfloat16 [512], P('dp'), may hold values from -3 to 3
- output_weight: bfloat16 [1536, 1536], P('tensor', 'dp'), may hold values from -0.625 to 0.625
- second_gain: bfloat16 [1536], P('dp'), may hold values from 0.5 to 1.5
- gateup_weight: bfloat16 [2, 1536, 8960], P(None, 'dp', 'tensor'), may hold values from -0.15625 to 0.15625
- down_weight: bfloat16 [8960, 1536], P('tensor', 'dp'), may hold values from -0.0625 to 0.0625
- cotangent: bfloat16 [8192, 1536], P(('dp', 'tensor')), may hold values from -6 to 6
Outputs:
- output: bfloat16 [8192, 1536], P(('dp', 'tensor'))
- input_grad: bfloat16 [8192, 1536], P(('dp', 'tensor'))
- first_gain_grad: float32 [1536], P('dp')
- query_weight_grad: float32 [1536, 1536], P('dp', 'tensor')
- query_bias_grad: float32 [1536], P(('tensor', 'dp'))
- keyval_weight_grad: float32 [1536, 512], P('dp')
- keyval_bias_grad: float32 [512], P('dp')
- output_weight_grad: float32 [1536, 1536], P('tensor', 'dp')
- second_gain_grad: float32 [1536], P('dp')
- gateup_weight_grad: float32 [2, 1536, 8960], P(None, 'dp', 'tensor')
- down_weight_grad: float32 [8960, 1536], P('tensor', 'dp')
Inputs may be any that keep to these rules, and one draw needn't show every extreme that they name: `segment_ids`: within each group of 1024 tokens the ids start at 0 and never fall; each group has one segment that begins among its first 256 tokens and ends among its last 256; in every draw some group is a single segment of all 1024 tokens, and some group reaches the largest id.
All inputs are finite; a program needn't handle non-finite values.
Results may differ from a plain program's by a relative error of at most 0.02.
Values may be sent and summed in bfloat16 or wider, within the bound.
A program may use at most 192 MiB of HBM per device.

v0:
```python
import math

import jax
import jax.numpy as jnp
from jax import lax
from jax.sharding import PartitionSpec as P

QUERY_HEADS = 12
KEYVALUE_HEADS = 2
HEAD_DIMENSION = 128


EPSILON = 1e-06
THETA = 1000000.0
NEGATIVE = -1e30


def rms_scale(rows):
    return lax.rsqrt(jnp.mean(rows * rows, axis=-1, keepdims=True) + EPSILON)


def norm_back(rows, gain, grad):
    scale = rms_scale(rows)
    normed = rows * scale
    weighted = grad * gain
    inner = jnp.mean(weighted * normed, axis=-1, keepdims=True)
    return (scale * (weighted - normed * inner), jnp.sum(grad * normed, axis=0))


def rope_tables(segments, head_extent):
    index = jnp.arange(segments.shape[0], dtype=jnp.int32)
    starts = jnp.concatenate([jnp.ones((1,), dtype=bool), segments[1:] != segments[:-1]])
    first = lax.cummax(jnp.where(starts, index, jnp.zeros_like(index)), axis=0)
    placed = (index - first).astype(jnp.float32)
    freqs = jnp.exp(
        jnp.arange(head_extent // 2, dtype=jnp.float32) * (-2.0 * math.log(THETA) / head_extent)
    )
    angles = placed[:, None] * freqs[None, :]
    return (jnp.cos(angles)[:, None, :], jnp.sin(angles)[:, None, :])


def apply_rotation(value_rows, cosine_table, sine_table):
    half = value_rows.shape[-1] // 2
    former = value_rows[..., :half]
    latter = value_rows[..., half:]
    return jnp.concatenate(
        [former * cosine_table - latter * sine_table, latter * cosine_table + former * sine_table],
        axis=-1,
    )


def unrotate(grads, cosine_table, sine_table):
    half = grads.shape[-1] // 2
    former = grads[..., :half]
    latter = grads[..., half:]
    return jnp.concatenate(
        [former * cosine_table + latter * sine_table, latter * cosine_table - former * sine_table],
        axis=-1,
    )


def allowed_block(segments, begin, end):
    rows = jnp.arange(begin, end, dtype=jnp.int32)
    columns = jnp.arange(end, dtype=jnp.int32)
    same = segments[begin:end][:, None] == segments[:end][None, :]
    return same & (columns[None, :] <= rows[:, None])


def block_scores(queries, keys, segments, begin, end, scale):
    scores = (
        jnp.einsum(
            "qhd,kd->hqk", queries[begin:end], keys[:end], preferred_element_type=jnp.float32
        )
        * scale
    )
    return jnp.where(allowed_block(segments, begin, end)[None], scores, NEGATIVE)


def attend(queries, keys, value_rows, segments, scale):
    item_count = queries.shape[0]
    block = min(512, item_count)
    outputs = []
    totals = []
    for begin in range(0, item_count, block):
        end = begin + block
        scores = block_scores(queries, keys, segments, begin, end, scale)
        top = jnp.max(scores, axis=-1, keepdims=True)
        weights = jnp.exp(scores - top)
        total = jnp.sum(weights, axis=-1, keepdims=True)
        probs = (weights / total).astype(jnp.bfloat16)
        outputs.append(
            jnp.einsum("hqk,kd->qhd", probs, value_rows[:end], preferred_element_type=jnp.float32)
        )
        totals.append(top[..., 0] + jnp.log(total[..., 0]))
    return (jnp.concatenate(outputs, axis=0), jnp.concatenate(totals, axis=1))


def attend_back(queries, keys, value_rows, segments, totals, d_out, scale):
    item_count = queries.shape[0]
    block = min(512, item_count)
    query_parts = []
    key_grad = jnp.zeros(keys.shape, jnp.float32)
    value_grad = jnp.zeros(value_rows.shape, jnp.float32)
    for begin in range(0, item_count, block):
        end = begin + block
        scores = block_scores(queries, keys, segments, begin, end, scale)
        probs = jnp.exp(scores - totals[:, begin:end, None])
        probs_low = probs.astype(jnp.bfloat16)
        d_probs = jnp.einsum(
            "qhd,kd->hqk", d_out[begin:end], value_rows[:end], preferred_element_type=jnp.float32
        )
        inner = jnp.sum(probs * d_probs, axis=-1, keepdims=True)
        d_scores = (scale * probs * (d_probs - inner)).astype(jnp.bfloat16)
        query_parts.append(
            jnp.einsum("hqk,kd->qhd", d_scores, keys[:end], preferred_element_type=jnp.float32)
        )
        key_grad = key_grad.at[:end].add(
            jnp.einsum(
                "hqk,qhd->kd", d_scores, queries[begin:end], preferred_element_type=jnp.float32
            )
        )
        value_grad = value_grad.at[:end].add(
            jnp.einsum(
                "hqk,qhd->kd", probs_low, d_out[begin:end], preferred_element_type=jnp.float32
            )
        )
    return (jnp.concatenate(query_parts, axis=0), key_grad, value_grad)


def local(
    inputs,
    segment_ids,
    first_gain,
    query_weight,
    query_bias,
    key_value_weight,
    key_value_bias,
    output_weight,
    second_gain,
    gateup_weight,
    down_weight,
    cotangent,
):
    gathered_weights = (
        lax.all_gather(first_gain, "dp", axis=0, tiled=True),
        lax.all_gather(query_weight, "dp", axis=0, tiled=True),
        lax.all_gather(query_bias, "dp", axis=0, tiled=True),
        lax.all_gather(key_value_weight, "dp", axis=0, tiled=True),
        lax.all_gather(key_value_bias, "dp", axis=0, tiled=True),
        lax.all_gather(output_weight, "dp", axis=1, tiled=True),
        lax.all_gather(second_gain, "dp", axis=0, tiled=True),
        lax.all_gather(gateup_weight, "dp", axis=1, tiled=True),
        lax.all_gather(down_weight, "dp", axis=1, tiled=True),
    )
    (
        gain_one,
        query_full,
        qbias_full,
        keyval_full,
        kvbias_full,
        output_full,
        gain_two,
        gateup_full,
        down_full,
    ) = gathered_weights
    head_extent = HEAD_DIMENSION
    local_heads = query_full.shape[1] // head_extent
    scale = 1.0 / math.sqrt(head_extent)
    shared_key_head = lax.axis_index("tensor") * local_heads // (QUERY_HEADS // KEYVALUE_HEADS)
    key_start = shared_key_head * head_extent
    value_offset = (KEYVALUE_HEADS + shared_key_head) * head_extent
    own_inputs = inputs.astype(jnp.float32)
    normed_own = (own_inputs * rms_scale(own_inputs) * gain_one.astype(jnp.float32)).astype(
        jnp.bfloat16
    )
    normed_rows = lax.all_gather(normed_own, "tensor", axis=0, tiled=True)
    item_count = normed_rows.shape[0]
    cosine_table, sine_table = rope_tables(segment_ids, head_extent)
    query = jnp.dot(
        normed_rows, query_full, preferred_element_type=jnp.float32
    ) + qbias_full.astype(jnp.float32)
    rot_query = apply_rotation(
        query.reshape(item_count, local_heads, head_extent), cosine_table, sine_table
    ).astype(jnp.bfloat16)
    pair_weight = jnp.concatenate(
        [
            lax.dynamic_slice_in_dim(keyval_full, key_start, head_extent, 1),
            lax.dynamic_slice_in_dim(keyval_full, value_offset, head_extent, 1),
        ],
        axis=1,
    )
    pair_bias = jnp.concatenate(
        [
            lax.dynamic_slice_in_dim(kvbias_full, key_start, head_extent, 0),
            lax.dynamic_slice_in_dim(kvbias_full, value_offset, head_extent, 0),
        ],
        axis=0,
    )
    pair = jnp.dot(normed_rows, pair_weight, preferred_element_type=jnp.float32) + pair_bias.astype(
        jnp.float32
    )
    rotated_key = apply_rotation(pair[:, None, :head_extent], cosine_table, sine_table)[
        :, 0
    ].astype(jnp.bfloat16)
    value_rows = pair[:, head_extent:].astype(jnp.bfloat16)
    attended, totals = attend(rot_query, rotated_key, value_rows, segment_ids, scale)
    attended = attended.reshape(item_count, local_heads * head_extent).astype(jnp.bfloat16)
    branch_terms = jnp.dot(attended, output_full, preferred_element_type=jnp.float32)
    branch_own = lax.psum_scatter(branch_terms, "tensor", scatter_dimension=0, tiled=True)
    residual = own_inputs + branch_own
    gain_two32 = gain_two.astype(jnp.float32)
    second_own = (residual * rms_scale(residual) * gain_two32).astype(jnp.bfloat16)
    second_rows = lax.all_gather(second_own, "tensor", axis=0, tiled=True)
    gate = jnp.dot(second_rows, gateup_full[0], preferred_element_type=jnp.float32)
    upper = jnp.dot(second_rows, gateup_full[1], preferred_element_type=jnp.float32)
    sigmoid = jax.nn.sigmoid(gate)
    swish = gate * sigmoid
    hidden = (swish * upper).astype(jnp.bfloat16)
    mlp_terms = jnp.dot(hidden, down_full, preferred_element_type=jnp.float32)
    mlp_own = lax.psum_scatter(
        mlp_terms.astype(jnp.bfloat16), "tensor", scatter_dimension=0, tiled=True
    ).astype(jnp.float32)
    output = (residual + mlp_own).astype(jnp.bfloat16)
    again = (
        lax.all_gather(first_gain, "dp", axis=0, tiled=True),
        lax.all_gather(query_weight, "dp", axis=0, tiled=True),
        lax.all_gather(query_bias, "dp", axis=0, tiled=True),
        lax.all_gather(key_value_weight, "dp", axis=0, tiled=True),
        lax.all_gather(key_value_bias, "dp", axis=0, tiled=True),
        lax.all_gather(output_weight, "dp", axis=1, tiled=True),
        lax.all_gather(second_gain, "dp", axis=0, tiled=True),
        lax.all_gather(gateup_weight, "dp", axis=1, tiled=True),
        lax.all_gather(down_weight, "dp", axis=1, tiled=True),
    )
    (
        gain_one_b,
        query_back,
        qbias_back,
        keyval_back,
        kvbias_back,
        output_back,
        gain_two_b,
        gateup_back,
        down_back,
    ) = again
    grad_rows = lax.all_gather(cotangent, "tensor", axis=0, tiled=True)
    d_hidden = jnp.einsum("td,fd->tf", grad_rows, down_back, preferred_element_type=jnp.float32)
    down_grad = jnp.einsum("tf,td->fd", hidden, grad_rows, preferred_element_type=jnp.float32)
    d_gate = (d_hidden * upper * sigmoid * (1.0 + gate * (1.0 - sigmoid))).astype(jnp.bfloat16)
    d_up = (d_hidden * swish).astype(jnp.bfloat16)
    gateup_grad = jnp.stack(
        [
            jnp.einsum("td,tf->df", second_rows, d_gate, preferred_element_type=jnp.float32),
            jnp.einsum("td,tf->df", second_rows, d_up, preferred_element_type=jnp.float32),
        ]
    )
    second_terms = jnp.einsum(
        "tf,df->td", d_gate, gateup_back[0], preferred_element_type=jnp.float32
    ) + jnp.einsum("tf,df->td", d_up, gateup_back[1], preferred_element_type=jnp.float32)
    d_second = lax.psum_scatter(second_terms, "tensor", scatter_dimension=0, tiled=True)
    residual_part, gain_two_grad = norm_back(residual, gain_two_b.astype(jnp.float32), d_second)
    d_residual = cotangent.astype(jnp.float32) + residual_part
    d_branch = d_residual.astype(jnp.bfloat16)
    branch_rows = lax.all_gather(d_branch, "tensor", axis=0, tiled=True)
    output_grad = jnp.einsum("th,td->hd", attended, branch_rows, preferred_element_type=jnp.float32)
    d_attended = jnp.einsum(
        "td,hd->th", branch_rows, output_back, preferred_element_type=jnp.float32
    ).astype(jnp.bfloat16)
    d_rot_query, d_rot_key, d_values = attend_back(
        rot_query,
        rotated_key,
        value_rows,
        segment_ids,
        totals,
        d_attended.reshape(item_count, local_heads, head_extent),
        scale,
    )
    d_query = (
        unrotate(d_rot_query, cosine_table, sine_table)
        .reshape(item_count, local_heads * head_extent)
        .astype(jnp.bfloat16)
    )
    d_key = unrotate(d_rot_key[:, None, :], cosine_table, sine_table)[:, 0]
    query_grad = jnp.einsum("td,th->dh", normed_rows, d_query, preferred_element_type=jnp.float32)
    qbias_grad = jnp.sum(d_query.astype(jnp.float32), axis=0)
    normed_terms = jnp.einsum("th,dh->td", d_query, query_back, preferred_element_type=jnp.float32)
    keyval_terms = jnp.zeros((item_count, keyval_back.shape[1]), jnp.float32)
    keyval_terms = lax.dynamic_update_slice_in_dim(keyval_terms, d_key, key_start, 1)
    keyval_terms = lax.dynamic_update_slice_in_dim(keyval_terms, d_values, value_offset, 1)
    d_normed_own, keyval_own = (
        lax.psum_scatter(
            normed_terms.astype(jnp.bfloat16), "tensor", scatter_dimension=0, tiled=True
        ).astype(jnp.float32),
        lax.psum_scatter(
            keyval_terms.astype(jnp.bfloat16), "tensor", scatter_dimension=0, tiled=True
        ).astype(jnp.float32),
    )
    keyval_low = keyval_own.astype(jnp.bfloat16)
    d_normed_own = d_normed_own + jnp.einsum(
        "tc,dc->td", keyval_low, keyval_back, preferred_element_type=jnp.float32
    )
    keyval_grad = jnp.einsum(
        "td,tc->dc", normed_own, keyval_low, preferred_element_type=jnp.float32
    )
    kvbias_grad = jnp.sum(keyval_low.astype(jnp.float32), axis=0)
    input_part, gain_one_grad = norm_back(own_inputs, gain_one_b.astype(jnp.float32), d_normed_own)
    input_grad = (d_residual + input_part).astype(jnp.bfloat16)
    summed = (
        lax.psum_scatter(
            gain_one_grad.astype(jnp.bfloat16), "dp", scatter_dimension=0, tiled=True
        ).astype(jnp.float32),
        lax.psum_scatter(
            query_grad.astype(jnp.bfloat16), "dp", scatter_dimension=0, tiled=True
        ).astype(jnp.float32),
        lax.psum_scatter(
            qbias_grad.astype(jnp.bfloat16), "dp", scatter_dimension=0, tiled=True
        ).astype(jnp.float32),
        lax.psum_scatter(
            keyval_grad.astype(jnp.bfloat16), "dp", scatter_dimension=0, tiled=True
        ).astype(jnp.float32),
        lax.psum_scatter(
            kvbias_grad.astype(jnp.bfloat16), "dp", scatter_dimension=0, tiled=True
        ).astype(jnp.float32),
        lax.psum_scatter(
            output_grad.astype(jnp.bfloat16), "dp", scatter_dimension=1, tiled=True
        ).astype(jnp.float32),
        lax.psum_scatter(
            gain_two_grad.astype(jnp.bfloat16), "dp", scatter_dimension=0, tiled=True
        ).astype(jnp.float32),
        lax.psum_scatter(
            gateup_grad.astype(jnp.bfloat16), "dp", scatter_dimension=1, tiled=True
        ).astype(jnp.float32),
        lax.psum_scatter(
            down_grad.astype(jnp.bfloat16), "dp", scatter_dimension=1, tiled=True
        ).astype(jnp.float32),
    )
    (
        gain_one_sh,
        query_sh,
        qbias_sh,
        keyval_sh,
        kvbias_sh,
        output_sh,
        gain_two_sh,
        gateup_sh,
        down_sh,
    ) = summed
    gain_one_sh, keyval_sh, kvbias_sh, gain_two_sh = (
        lax.psum(gain_one_sh.astype(jnp.bfloat16), "tensor").astype(jnp.float32),
        lax.psum(keyval_sh.astype(jnp.bfloat16), "tensor").astype(jnp.float32),
        lax.psum(kvbias_sh.astype(jnp.bfloat16), "tensor").astype(jnp.float32),
        lax.psum(gain_two_sh.astype(jnp.bfloat16), "tensor").astype(jnp.float32),
    )
    return (
        output,
        input_grad,
        gain_one_sh,
        query_sh,
        qbias_sh,
        keyval_sh,
        kvbias_sh,
        output_sh,
        gain_two_sh,
        gateup_sh,
        down_sh,
    )


def solution(mesh):
    in_specs = (
        P(("dp", "tensor"), None),
        P("dp"),
        P("dp"),
        P("dp", "tensor"),
        P(("tensor", "dp")),
        P("dp", None),
        P("dp"),
        P("tensor", "dp"),
        P("dp"),
        P(None, "dp", "tensor"),
        P("tensor", "dp"),
        P(("dp", "tensor"), None),
    )
    out_specs = (
        P(("dp", "tensor"), None),
        P(("dp", "tensor"), None),
        P("dp"),
        P("dp", "tensor"),
        P(("tensor", "dp")),
        P("dp", None),
        P("dp"),
        P("tensor", "dp"),
        P("dp"),
        P(None, "dp", "tensor"),
        P("tensor", "dp"),
    )
    return jax.shard_map(local, mesh=mesh, in_specs=in_specs, out_specs=out_specs, check_vma=False)
```

profile of v0, /device:TPU:24, one launch (start us, length us, event | category | flops | bytes accessed | tf_op | source)
XLA Modules:
  0.0 1380.9 jit_solution(4146943633883394250)
XLA Ops:
  14.7 24.3 %all-reduce.12 = (bf16[1536]{0:T(1024)(128)(2,1)S(1)}, bf16[384]{0:T(512)(128)(2,1)S(1)}, bf16[512]{0:T(512)(128)(2,1)S(1)}, bf16[1536]{0:T(1024)(128)(2,1)S(1)}) all-reduce(bf16[1536]{0:T(1024)(128)(2,1)S(1)} %dynamic-update-slice.10, bf16[384]{0:T(512)(128)(2,1)S(1)} %dynamic-update-slice.12, ...), channel_id=1, replica_groups=mesh['dp'=8,'tensor'=4] {'dp'}, use_global_device_ids=true, to_apply=%add.2 | all-reduce | flops 3968 | bytes 15872
  52.5 50.9 %all-gather.10.cloned.1.call-done = bf16[1024,1536]{1,0:T(8,128)(2,1)} async-done(((bf16[256,1536]{1,0:T(8,128)(2,1)}), bf16[1024,1536]{1,0:T(8,128)(2,1)}) %all-gather.10.cloned.1.call-update) | async-done | bytes 3145744 | tf_op jit(solution)/shard_map/all_gather | solution.py:176
  108.3 22.3 %all-gather.14.cloned.1.call-done = bf16[1536,384]{1,0:T(8,128)(2,1)} async-done(((bf16[192,384]{1,0:T(8,128)(2,1)}), bf16[1536,384]{1,0:T(8,128)(2,1)}) %all-gather.14.cloned.1.call-update) | async-done | bytes 1179664 | tf_op jit(solution)/shard_map/all_gather | solution.py:146
  162.8 109.9 %reduce-scatter.10.cloned.1.call-done = f32[256,1536]{1,0:T(8,128)} async-done(((f32[1024,1536]{1,0:T(8,128)}), f32[256,1536]{1,0:T(8,128)}) %reduce-scatter.10.cloned.1.call-update) | async-done | bytes 1572880 | tf_op jit(solution)/shard_map/reduce_scatter | solution.py:209
  279.2 60.0 %all-gather.18.cloned.1.call-done = bf16[1024,1536]{1,0:T(8,128)(2,1)} async-done(((bf16[256,1536]{1,0:T(8,128)(2,1)}), bf16[1024,1536]{1,0:T(8,128)(2,1)}) %all-gather.18.cloned.1.call-update) | async-done | bytes 3145744 | tf_op jit(solution)/shard_map/all_gather | solution.py:213
  339.2 82.0 %all-gather.20.cloned.1.call-done = bf16[2,1536,2240]{2,1,0:T(8,128)(2,1)} async-done(((bf16[2,192,2240]{2,1,0:T(8,128)(2,1)}), bf16[2,1536,2240]{2,1,0:T(8,128)(2,1)}) %all-gather.20.cloned.1.call-update) | async-done | bytes 13762576 | tf_op jit(solution)/shard_map/all_gather | solution.py:152
  421.2 13.3 fusion.9
  446.0 37.7 %all-gather.24.cloned.1.call-done = bf16[1024,1536]{1,0:T(8,128)(2,1)} async-done(((bf16[256,1536]{1,0:T(8,128)(2,1)}), bf16[1024,1536]{1,0:T(8,128)(2,1)}) %all-gather.24.cloned.1.call-update) | async-done | bytes 3145744 | tf_op jit(solution)/shard_map/all_gather | solution.py:246
  483.7 52.0 %all-gather.22.cloned.1.call-done = bf16[2240,1536]{0,1:T(8,128)(2,1)} async-done(((bf16[2240,192]{0,1:T(8,128)(2,1)}), bf16[2240,1536]{0,1:T(8,128)(2,1)}) %all-gather.22.cloned.1.call-update) | async-done | bytes 6881296 | tf_op jit(solution)/shard_map/all_gather | solution.py:153
  535.8 20.3 %multiply_convert_fusion = (bf16[1024,2240]{0,1:T(8,128)(2,1)}, bf16[1024,2240]{0,1:T(8,128)(2,1)}, bf16[1024,2240]{0,1:T(8,128)(2,1)}) fusion(f32[1024,2240]{0,1:T(8,128)} %fusion.7, f32[1024,2240]{0,1:T(8,128)} %fusion.9, bf16[1024,1536]{1,0:T(8,128)(2,1)} %all-gather.24.cloned.1.call-done, bf16[2240,1536]{0,1:T(8,128)(2,1)} %all-gather.22.cloned.1.call-done), kind=kOutput, calls=%fused_computation.6 | convolution fusion | flops 7080837120 | bytes 42139648 | tf_op jit(solution)/shard_map/td,fd->tf/dot_general | solution.py:247
  567.4 12.2 fusion.12
  579.7 110.1 %reduce-scatter.14.cloned.1.call-done = f32[256,1536]{1,0:T(8,128)} async-done(((f32[1024,1536]{1,0:T(8,128)}), f32[256,1536]{1,0:T(8,128)}) %reduce-scatter.14.cloned.1.call-update) | async-done | bytes 1572880 | tf_op jit(solution)/shard_map/reduce_scatter | solution.py:260
  695.2 62.2 %all-gather.26.cloned.1.call-done = bf16[1024,1536]{1,0:T(8,128)(2,1)} async-done(((bf16[256,1536]{1,0:T(8,128)(2,1)}), bf16[1024,1536]{1,0:T(8,128)(2,1)}) %all-gather.26.cloned.1.call-update) | async-done | bytes 3145744 | tf_op jit(solution)/shard_map/all_gather | solution.py:264
  797.3 13.9 %reduce-scatter.18.cloned.1.call-done = bf16[256,512]{0,1:T(8,128)(2,1)} async-done(((bf16[1024,512]{0,1:T(8,128)(2,1)}), bf16[256,512]{0,1:T(8,128)(2,1)}) %reduce-scatter.18.cloned.1.call-update) | async-done | bytes 262160 | tf_op jit(solution)/shard_map/reduce_scatter | solution.py:294
  833.6 35.5 %copy.90 = bf16[2,1536,2240]{2,0,1:T(2,128)(2,1)} copy(bf16[2,1536,2240]{1,2,0:T(8,128)(2,1)} %pad_maximum_fusion) | data formatting | bytes 27525120 | tf_op jit(solution)/shard_map/stack | solution.py:251
  903.4 13.0 convolution_convert_fusion.4
  918.4 141.4 %all-reduce.19.cloned.1.call-done = bf16[2,1536,2240]{2,0,1:T(2,128)(2,1)} async-done(((bf16[2,1536,2240]{2,0,1:T(2,128)(2,1)}), bf16[2,1536,2240]{2,0,1:T(2,128)(2,1)}) %all-reduce.19.cloned.1.call-update) | async-done | bytes 13762576
  1064.5 64.3 %reduce-scatter.26.cloned.1.call-done = bf16[2240,192]{0,1:T(8,128)(2,1)} async-done(((bf16[2240,1536]{0,1:T(8,128)(2,1)}), bf16[2240,192]{0,1:T(8,128)(2,1)}) %reduce-scatter.26.cloned.1.call-update) | async-done | bytes 860176 | tf_op jit(solution)/shard_map/reduce_scatter | solution.py:333
  1131.2 37.7 %reduce-scatter.24.cloned.1.call-done = bf16[384,192]{0,1:T(8,128)(2,1)} async-done(((bf16[384,1536]{0,1:T(8,128)(2,1)}), bf16[384,192]{0,1:T(8,128)(2,1)}) %reduce-scatter.24.cloned.1.call-update) | async-done | bytes 147472 | tf_op jit(solution)/shard_map/reduce_scatter | solution.py:324
  1170.6 38.2 %reduce-scatter.20.cloned.1.call-done = bf16[192,384]{1,0:T(8,128)(2,1)} async-done(((bf16[1536,384]{1,0:T(8,128)(2,1)}), bf16[192,384]{1,0:T(8,128)(2,1)}) %reduce-scatter.20.cloned.1.call-update) | async-done | bytes 147472 | tf_op jit(solution)/shard_map/reduce_scatter | solution.py:312
  1210.7 34.2 %all-reduce.17.cloned.1.call-done = bf16[192,512]{1,0:T(8,128)(2,1)} async-done(((bf16[192,512]{1,0:T(8,128)(2,1)}), bf16[192,512]{1,0:T(8,128)(2,1)}) %all-reduce.17.cloned.1.call-update) | async-done | bytes 196624 | tf_op jit(solution)/shard_map/psum | solution.py:350
  1246.5 60.5 %reduce-scatter.16.cloned.1.call-done = bf16[256,1536]{1,0:T(8,128)(2,1)} async-done(((bf16[1024,1536]{1,0:T(8,128)(2,1)}), bf16[256,1536]{1,0:T(8,128)(2,1)}) %reduce-scatter.16.cloned.1.call-update) | async-done | bytes 786448 | tf_op jit(solution)/shard_map/reduce_scatter | solution.py:291
  1311.0 24.8 %all-reduce.11 = (bf16[1536]{0:T(1024)(128)(2,1)S(1)}, bf16[384]{0:T(512)(128)(2,1)S(1)}, bf16[512]{0:T(512)(128)(2,1)S(1)}, bf16[1536]{0:T(1024)(128)(2,1)S(1)}) all-reduce(bf16[1536]{0:T(1024)(128)(2,1)S(1)} %get-tuple-element.110, bf16[384]{0:T(512)(128)(2,1)S(1)} %bitcast.170, ...), channel_id=7, replica_groups=mesh['dp'=8,'tensor'=4] {'dp'}, use_global_device_ids=true, to_apply=%region_18.19.clone | all-reduce | flops 3968 | bytes 15872
  1349.8 19.9 %reduce-scatter.12.cloned.1.call-done = bf16[256,1536]{1,0:T(8,128)(2,1)} async-done(((bf16[1024,1536]{1,0:T(8,128)(2,1)}), bf16[256,1536]{1,0:T(8,128)(2,1)}) %reduce-scatter.12.cloned.1.call-update) | async-done | bytes 786448 | tf_op jit(solution)/shard_map/reduce_scatter | solution.py:220
  (234 shorter events, 221.1 us)
Async XLA Ops:
  7.2 44.1 %all-gather.12.cloned.1.call-start = ((), (), s32[]{:S(2)}) async-start(), calls=%async_computation.10 | async-start | bytes 1769472 | tf_op jit(solution)/shard_map/all_gather | solution.py:148
  7.9 95.5 %all-gather.10.cloned.1.call-start = ((), (), s32[]{:S(2)}) async-start(), calls=%async_computation.9 | async-start | bytes 3932160 | tf_op jit(solution)/shard_map/all_gather | solution.py:176
  43.2 87.4 %all-gather.14.cloned.1.call-start = ((), (), s32[]{:S(2)}) async-start(), calls=%async_computation.11 | async-start | bytes 1327104 | tf_op jit(solution)/shard_map/all_gather | solution.py:146
  44.0 112.5 %all-gather.16.cloned.1.call-start = ((), (), s32[]{:S(2)}) async-start(), calls=%async_computation.12 | async-start | bytes 1327104 | tf_op jit(solution)/shard_map/all_gather | solution.py:150
  44.6 228.1 %reduce-scatter.10.cloned.1.call-start = ((), (), s32[]{:S(2)}) async-start(), calls=%async_computation.13 | async-start | bytes 7864320 | tf_op jit(solution)/shard_map/reduce_scatter | solution.py:209
  140.5 621.2 %copy-start.1 = (f32[3,512,512]{1,2,0:T(8,128)}, f32[3,512,512]{1,2,0:T(8,128)S(1)}, u32[]{:S(2)}) copy-start(f32[3,512,512]{1,2,0:T(8,128)S(1)} %get-tuple-element.159) | copy-start | bytes 9437188
  162.5 176.7 %all-gather.18.cloned.1.call-start = ((), (), s32[]{:S(2)}) async-start(), calls=%async_computation.14 | async-start | bytes 3932160 | tf_op jit(solution)/shard_map/all_gather | solution.py:213
  276.9 144.3 %all-gather.20.cloned.1.call-start = ((), (), s32[]{:S(2)}) async-start(), calls=%async_computation.15 | async-start | bytes 15925248 | tf_op jit(solution)/shard_map/all_gather | solution.py:152
  277.7 206.0 %all-gather.24.cloned.1.call-start = ((), (), s32[]{:S(2)}) async-start(), calls=%async_computation.18 | async-start | bytes 3932160 | tf_op jit(solution)/shard_map/all_gather | solution.py:246
  278.4 257.3 %all-gather.22.cloned.1.call-start = ((), (), s32[]{:S(2)}) async-start(), calls=%async_computation.16 | async-start | bytes 7962624 | tf_op jit(solution)/shard_map/all_gather | solution.py:153
  279.2 410.6 %reduce-scatter.14.cloned.1.call-start = ((), (), s32[]{:S(2)}) async-start(), calls=%async_computation.19 | async-start | bytes 7864320 | tf_op jit(solution)/shard_map/reduce_scatter | solution.py:260
  579.6 177.8 %all-gather.26.cloned.1.call-start = ((), (), s32[]{:S(2)}) async-start(), calls=%async_computation.20 | async-start | bytes 3932160 | tf_op jit(solution)/shard_map/all_gather | solution.py:264
  695.2 116.0 %reduce-scatter.18.cloned.1.call-start = ((), (), s32[]{:S(2)}) async-start(), calls=%async_computation.22 | async-start | bytes 1310720 | tf_op jit(solution)/shard_map/reduce_scatter | solution.py:294
  784.9 114.0 %reduce-scatter.22.cloned.1.call-start = ((), (), s32[]{:S(2)}) async-start(), calls=%async_computation.24 | async-start | bytes 1769472 | tf_op jit(solution)/shard_map/reduce_scatter | solution.py:318
  814.0 245.8 %all-reduce.19.cloned.1.call-start = ((), (), s32[]{:S(2)}) async-start(), calls=%async_computation.28 | async-start | bytes 28311552
  869.1 259.7 %reduce-scatter.26.cloned.1.call-start = ((), (), s32[]{:S(2)}) async-start(), calls=%async_computation.27 | async-start | bytes 7962624 | tf_op jit(solution)/shard_map/reduce_scatter | solution.py:333
  882.8 286.2 %reduce-scatter.24.cloned.1.call-start = ((), (), s32[]{:S(2)}) async-start(), calls=%async_computation.26 | async-start | bytes 1327104 | tf_op jit(solution)/shard_map/reduce_scatter | solution.py:324
  888.8 320.1 %reduce-scatter.20.cloned.1.call-start = ((), (), s32[]{:S(2)}) async-start(), calls=%async_computation.23 | async-start | bytes 1327104 | tf_op jit(solution)/shard_map/reduce_scatter | solution.py:312
  898.9 345.9 %all-reduce.17.cloned.1.call-start = ((), (), s32[]{:S(2)}) async-start(), calls=%async_computation.25 | async-start | bytes 393216 | tf_op jit(solution)/shard_map/psum | solution.py:350
  899.5 407.6 %reduce-scatter.16.cloned.1.call-start = ((), (), s32[]{:S(2)}) async-start(), calls=%async_computation.21 | async-start | bytes 3932160 | tf_op jit(solution)/shard_map/reduce_scatter | solution.py:291
  903.1 466.6 %reduce-scatter.12.cloned.1.call-start = ((), (), s32[]{:S(2)}) async-start(), calls=%async_computation.17 | async-start | bytes 3932160 | tf_op jit(solution)/shard_map/reduce_scatter | solution.py:220
  1064.5 242.6 %copy-start.31 = (f32[1536]{0:T(1024)S(1)}, f32[1536]{0:T(1024)}, u32[]{:S(2)}) copy-start(f32[1536]{0:T(1024)} %copy-done.30) | copy-start | bytes 18436
  1064.5 242.6 %copy-start.34 = (f32[256]{0:T(256)S(1)}, f32[256]{0:T(256)}, u32[]{:S(2)}) copy-start(f32[256]{0:T(256)} %copy-done.33) | copy-start | bytes 3076
  1210.5 159.2 %copy-start.10 = (f32[256,1536]{1,0:T(8,128)S(1)}, f32[256,1536]{1,0:T(8,128)}, u32[]{:S(2)}) copy-start(f32[256,1536]{1,0:T(8,128)} %reduce-scatter.14.cloned.1.call-done) | copy-start | bytes 4718596
  (39 other events, 564.2 us)
Sparse Core Ops, SparseCore 0:
  9.9 26.8 all-gather.11
  43.4 59.9 all-gather.9
  105.3 25.3 all-gather.13
  132.4 24.0 all-gather.15
  162.7 109.9 reduce-scatter.9
  277.0 62.1 all-gather.17
  341.2 80.0 all-gather.19
  422.8 60.8 all-gather.23
  485.6 50.1 all-gather.21
  579.7 110.0 reduce-scatter.13
  695.3 62.1 all-gather.25
  785.0 26.0 reduce-scatter.17
  814.8 39.3 reduce-scatter.21
  869.2 190.4 all-reduce.18
  1063.1 65.6 reduce-scatter.25
  1132.2 36.7 reduce-scatter.23
  1172.1 36.7 reduce-scatter.19
  1211.2 33.6 all-reduce.16
  1247.1 59.8 reduce-scatter.15
  1309.2 60.4 reduce-scatter.11
where the time goes:
time: 1390 us; the launch traced here: 1380 us
  waiting for transfers between devices  1010 us (73%)
  matrix products  176 us (13%)
  blocking collectives  60.7 us (4%)
  other arithmetic  57.1 us (4%)
  local copies, waits for them, and re-layouts  54.9 us (4%)
  between operations  19.3 us (1%)
    unnamed x21, waiting for transfers between devices  146 us
    reduce_scatter x1, waiting for transfers between devices, local(): lax.psum_scatter(second_terms, 'tensor', scatter_dimension=0, tiled=True)  110 us
    reduce_scatter x1, waiting for transfers between devices, local(): lax.psum_scatter(branch_terms, 'tensor', scatter_dimension=0, tiled=True)  110 us
    all_gather x1, waiting for transfers between devices, local(): lax.all_gather(gateup_weight, 'dp', axis=1, tiled=True)  82 us
    reduce_scatter x1, waiting for transfers between devices, local(): lax.psum_scatter(down_grad.astype(jnp.bfloat16), 'dp', scatter_dimension=...  64.3 us
    all_gather x1, waiting for transfers between devices, local(): branch_rows = lax.all_gather(d_branch, 'tensor', axis=0, tiled=True)  62.2 us
    reduce_scatter x1, waiting for transfers between devices, local(): lax.psum_scatter(normed_terms.astype(jnp.bfloat16), 'tensor', scatter_dim...  60.5 us
    all_gather x1, waiting for transfers between devices, local(): second_rows = lax.all_gather(second_own, 'tensor', axis=0, tiled=True)  60 us
  transfers between devices with their start and end apart: 20, of which 18 were waited for; matrix products, arithmetic and copies ran while one was open for 14% of the time, Pallas kernels for 0%

commit v1 on v0

v1 whole, which is shorter than its diff:
```python
import functools
import math

import jax
import jax.numpy as jnp
from jax import lax
from jax.experimental import pallas as pl
from jax.experimental.pallas import tpu as pltpu
from jax.sharding import PartitionSpec as P

QUERY_HEADS = 12
KEYVALUE_HEADS = 2
HEAD_DIMENSION = 128
REPEAT = QUERY_HEADS // KEYVALUE_HEADS

EPSILON = 1e-06
THETA = 1000000.0
NEGATIVE = -1e30

F32 = jnp.float32
BF16 = jnp.bfloat16


def rms_scale(rows):
    return lax.rsqrt(jnp.mean(rows * rows, axis=-1, keepdims=True) + EPSILON)


def norm_back(rows, gain, grad):
    scale = rms_scale(rows)
    normed = rows * scale
    weighted = grad * gain
    inner = jnp.mean(weighted * normed, axis=-1, keepdims=True)
    return (scale * (weighted - normed * inner), jnp.sum(grad * normed, axis=0))


def rope_tables(segments, head_extent):
    index = jnp.arange(segments.shape[0], dtype=jnp.int32)
    starts = jnp.concatenate([jnp.ones((1,), dtype=bool), segments[1:] != segments[:-1]])
    first = lax.cummax(jnp.where(starts, index, jnp.zeros_like(index)), axis=0)
    placed = (index - first).astype(F32)
    freqs = jnp.exp(
        jnp.arange(head_extent // 2, dtype=F32) * (-2.0 * math.log(THETA) / head_extent)
    )
    return placed, freqs


def apply_rotation(value_rows, cosine_table, sine_table):
    half = value_rows.shape[-1] // 2
    former = value_rows[..., :half]
    latter = value_rows[..., half:]
    return jnp.concatenate(
        [former * cosine_table - latter * sine_table, latter * cosine_table + former * sine_table],
        axis=-1,
    )


def unrotate(grads, cosine_table, sine_table):
    return apply_rotation(grads, cosine_table, -sine_table)


def dot(left, right):
    return jnp.dot(left, right, preferred_element_type=F32)


def dot_nt(left, right):
    return lax.dot_general(left, right, (((1,), (1,)), ((), ())), preferred_element_type=F32)


def dot_tn(left, right):
    return lax.dot_general(left, right, (((0,), (0,)), ((), ())), preferred_element_type=F32)


MESH = pl.DeviceIdType.MESH
ANY = pl.ANY


def flip(index, bit):
    return index + (1 << bit) * (1 - 2 * ((index // (1 << bit)) % 2))


class Place:
    def __init__(self, dp, tp):
        self.dp, self.tp = dp, tp
        self.d, self.z = lax.axis_index("dp"), lax.axis_index("tensor")
        self.steps = dp.bit_length() - 2
        odd = self.d % 2
        self.partners = []
        for step in range(self.steps):
            first, other = flip(self.d, 1 + step), flip(self.d, self.steps - step)
            self.partners.append(first + odd * (other - first))
        self.sibling = flip(self.d, 0)
        self.deltas = [partner - self.d for partner in self.partners]

    def block(self, mask):
        index = self.d
        for step in range(self.steps):
            if (mask >> step) & 1:
                index = index + self.deltas[step]
        return index

    def sibling_block(self, mask):
        index = self.sibling
        for step in range(self.steps):
            if (mask >> step) & 1:
                index = index + self.deltas[self.steps - 1 - step]
        return index

    def device(self, index):
        return (index, self.z)

    def beside(self, offset):
        return (self.d, self.z + offset)

    def greet(self, plane, line):
        barrier = pltpu.get_barrier_semaphore()
        count = 0
        if plane:
            for partner in self.partners + [self.sibling]:
                pl.semaphore_signal(
                    barrier, inc=1, device_id=self.device(partner), device_id_type=MESH
                )
            count = self.steps + 1
        if line:
            for offset in (-1, 1):

                @pl.when(self.has(offset))
                def _():
                    pl.semaphore_signal(
                        barrier, inc=1, device_id=self.beside(offset), device_id_type=MESH
                    )

            count = count + jnp.where(self.z > 0, 1, 0) + jnp.where(self.z < self.tp - 1, 1, 0)
        pl.semaphore_wait(barrier, count)

    def has(self, offset):
        return (self.z + offset >= 0) & (self.z + offset < self.tp)


def remote(src, dst, send, recv, device):
    return pltpu.make_async_remote_copy(
        src_ref=src, dst_ref=dst, send_sem=send, recv_sem=recv, device_id=device, device_id_type=MESH
    )


class PlaneGather:
    def __init__(self, place, own, full, send, recv):
        self.place, self.own, self.full, self.send, self.recv = place, own, full, send, recv
        self.half = 1 << place.steps

    def at(self, mask):
        return self.full(self.place.block(mask)) if mask else self.own

    def copy(self, mask, step):
        place = self.place
        if step < place.steps:
            label, device = mask | (1 << step), place.device(place.partners[step])
        else:
            label, device = self.half + mask, place.device(place.sibling)
        return remote(
            self.at(mask), self.full(place.block(mask)), self.send(label), self.recv(label), device
        )

    def arrival(self, label):
        place = self.place
        if label < self.half:
            ref = self.full(place.block(label))
        else:
            ref = self.full(place.sibling_block(label - self.half))
        return remote(ref, ref, self.send(label), self.recv(label), place.device(place.sibling))

    def sends(self, mask):
        return [self.copy(mask, step) for step in range(mask.bit_length(), self.place.steps + 1)]

    def start(self):
        for copy in self.sends(0):
            copy.start()

    def hand_on(self, mask):
        self.arrival(mask).wait_recv()
        for copy in self.sends(mask):
            copy.start()

    def finish(self):
        for mask in range(self.half):
            self.arrival(self.half + mask).wait_recv()
        for mask in range(self.half):
            for copy in self.sends(mask):
                copy.wait_send()


class LineGather:
    def __init__(self, place, own, full, send, recv):
        self.place, self.own, self.full, self.send, self.recv = place, own, full, send, recv

    def copy(self, distance, offset):
        place = self.place
        source = place.z - offset * distance
        side = 0 if offset > 0 else 1
        src = self.full(source) if distance else self.own
        return remote(
            src,
            self.full(source),
            self.send(side, distance),
            self.recv(side, distance),
            place.beside(offset),
        )

    def each(self, distance, act):
        place = self.place
        for offset in (1, -1):

            @pl.when(place.has(-offset * distance) & place.has(offset))
            def _():
                act(self.copy(distance, offset))

    def start(self):
        self.each(0, lambda copy: copy.start())

    def arrived(self, distance):
        place = self.place
        for offset in (1, -1):

            @pl.when(place.has(-offset * distance))
            def _():
                side = 0 if offset > 0 else 1
                ref = self.full(place.z - offset * distance)
                remote(
                    ref,
                    ref,
                    self.send(side, distance - 1),
                    self.recv(side, distance - 1),
                    place.beside(-offset),
                ).wait_recv()

    def hand_on(self, distance):
        self.arrived(distance)
        if distance < self.place.tp - 1:
            self.each(distance, lambda copy: copy.start())

    def finish(self):
        for distance in range(self.place.tp - 1):
            self.each(distance, lambda copy: copy.wait_send())


def gather_kernel(
    dp, tp, zq, zo, kvs, ff, cot, q_out, o_out, kv_out, ff_out, cot_out,
    plane_send, plane_recv, line_send, line_recv, local_sem,
):
    place = Place(dp, tp)
    d, z = place.d, place.z
    locals_ = [
        pltpu.make_async_copy(zq, q_out.at[d, z], local_sem.at[0]),
        pltpu.make_async_copy(zo, o_out.at[d, z], local_sem.at[1]),
        pltpu.make_async_copy(kvs, kv_out.at[d], local_sem.at[2]),
        pltpu.make_async_copy(ff, ff_out.at[d], local_sem.at[3]),
        pltpu.make_async_copy(cot, cot_out.at[z], local_sem.at[4]),
    ]
    for copy in locals_:
        copy.start()
    place.greet(True, True)

    def plane(item, own, full):
        return PlaneGather(
            place, own, full, lambda m: plane_send.at[item, m], lambda m: plane_recv.at[item, m]
        )

    def line(item, own, full):
        return LineGather(
            place,
            own,
            full,
            lambda s, k: line_send.at[item, s, k],
            lambda s, k: line_recv.at[item, s, k],
        )

    line_q = line(0, zq, lambda t: q_out.at[d, t])
    line_o = line(1, zo, lambda t: o_out.at[d, t])
    line_cot = line(2, cot, lambda t: cot_out.at[t])
    plane_kv = plane(0, kvs, lambda b: kv_out.at[b])
    plane_q = plane(1, q_out.at[d], lambda b: q_out.at[b])
    plane_o = plane(2, o_out.at[d], lambda b: o_out.at[b])
    plane_ff = [
        plane(3 + part, ff.at[part], lambda b, part=part: ff_out.at[b, part]) for part in (2, 0, 1)
    ]
    line_q.start()
    plane_kv.start()
    for distance in range(1, tp):
        line_q.hand_on(distance)
    line_o.start()
    locals_[0].wait()
    plane_q.start()
    for mask in range(1, 1 << place.steps):
        plane_kv.hand_on(mask)
    for distance in range(1, tp):
        line_o.hand_on(distance)
    line_cot.start()
    locals_[1].wait()
    queue = [plane_q, plane_o] + plane_ff
    for item, following in zip(queue, queue[1:] + [None]):
        if following is not None:
            following.start()
        for mask in range(1, 1 << place.steps):
            item.hand_on(mask)
    for distance in range(1, tp):
        line_cot.hand_on(distance)
    for item in [plane_kv] + queue:
        item.finish()
    for item in (line_q, line_o, line_cot):
        item.finish()
    for copy in locals_[2:]:
        copy.wait()


def gather_all(dp, tp, zq, zo, kvs, ff, cot):
    def shape(*dims):
        return jax.ShapeDtypeStruct(dims, BF16)

    return pl.pallas_call(
        functools.partial(gather_kernel, dp, tp),
        out_shape=(
            shape(dp, tp, *zq.shape),
            shape(dp, tp, *zo.shape),
            shape(dp, *kvs.shape),
            shape(dp, *ff.shape),
            shape(tp, *cot.shape),
        ),
        in_specs=[pl.BlockSpec(memory_space=ANY)] * 5,
        out_specs=[pl.BlockSpec(memory_space=ANY)] * 5,
        scratch_shapes=[
            pltpu.SemaphoreType.DMA((6, dp)),
            pltpu.SemaphoreType.DMA((6, dp)),
            pltpu.SemaphoreType.DMA((3, 2, tp)),
            pltpu.SemaphoreType.DMA((3, 2, tp)),
            pltpu.SemaphoreType.DMA((5,)),
        ],
        compiler_params=pltpu.CompilerParams(collective_id=0, has_side_effects=True),
        name="gather_weights",
    )(zq, zo, kvs, ff, cot)


def local(
    inputs,
    segment_ids,
    first_gain,
    query_weight,
    query_bias,
    key_value_weight,
    key_value_bias,
    output_weight,
    second_gain,
    gateup_weight,
    down_weight,
    cotangent,
):
    dp = lax.axis_size("dp")
    tp = lax.axis_size("tensor")
    rank = lax.axis_index("tensor")
    width = inputs.shape[1]
    own_rows = inputs.shape[0]
    depth = query_weight.shape[0]
    columns = query_weight.shape[1]
    kv_columns = key_value_weight.shape[1]
    hidden_units = gateup_weight.shape[2]
    heads_width = columns * tp
    head = HEAD_DIMENSION
    scale = 1.0 / math.sqrt(head)

    padded = -(-hidden_units // 256) * 256
    ff_own = jnp.stack([gateup_weight[0], gateup_weight[1], down_weight.T])
    ff_own = jnp.pad(ff_own, ((0, 0), (0, 0), (0, padded - hidden_units)))
    bias_rows = jnp.pad(query_bias[None, :], ((0, 15), (0, columns - query_bias.shape[0])))
    own_kvbias = jnp.pad(key_value_bias, (0, depth - key_value_bias.shape[0]))
    side = jnp.pad(jnp.stack([first_gain, second_gain, own_kvbias], axis=1), ((0, 0), (0, 125)))
    q_all, o_all, kv_all, ff_all, grad_rows = gather_all(
        dp,
        tp,
        jnp.concatenate([query_weight, bias_rows], axis=0),
        output_weight.T,
        jnp.concatenate([key_value_weight, side], axis=1),
        ff_own,
        cotangent,
    )
    grad_rows = grad_rows.reshape(-1, width)
    edge_q = heads_width
    edge_kv = edge_q + kv_columns
    edge_o = edge_kv + heads_width
    query_full = q_all[:, :, :depth].transpose(0, 2, 1, 3).reshape(width, -1)
    qbias_full = q_all[:, :, depth, : query_bias.shape[0]].transpose(1, 0, 2).reshape(-1)
    out_t_weight = o_all.transpose(0, 2, 1, 3).reshape(width, -1)
    kv_all = kv_all.reshape(width, -1)
    qkv_weight = jnp.concatenate([query_full, kv_all[:, :kv_columns]], axis=1)
    side = kv_all[:, kv_columns : kv_columns + 3].T.astype(F32)
    gain_one, gain_two = side[0], side[1]
    kvbias_full = side[2].reshape(dp, depth)[:, : key_value_bias.shape[0]].reshape(-1)
    qbias_full = qbias_full.astype(F32)
    gate_w = ff_all[:, 0].reshape(width, padded)
    up_w = ff_all[:, 1].reshape(width, padded)
    down_t = ff_all[:, 2].reshape(width, padded)

    own_inputs = inputs.astype(F32)
    normed_own = (own_inputs * rms_scale(own_inputs) * gain_one).astype(BF16)
    placed, freqs = rope_tables(segment_ids, head)
    begin = rank * own_rows
    own_placed = lax.dynamic_slice_in_dim(placed, begin, own_rows, 0)
    own_segments = lax.dynamic_slice_in_dim(segment_ids, begin, own_rows, 0)
    angles = own_placed[:, None] * freqs[None, :]
    cosine, sine = jnp.cos(angles)[:, None, :], jnp.sin(angles)[:, None, :]

    qkv = dot(normed_own, qkv_weight) + jnp.concatenate([qbias_full, kvbias_full])
    half_kv = kv_columns // 2
    rot = apply_rotation(
        qkv[:, : edge_q + half_kv].reshape(own_rows, -1, head), cosine, sine
    ).astype(BF16)
    rot_query = rot[:, :QUERY_HEADS]
    own_kv = jnp.concatenate(
        [rot[:, QUERY_HEADS:].reshape(own_rows, half_kv), qkv[:, edge_q + half_kv :].astype(BF16)],
        axis=1,
    )
    all_kv = lax.all_gather(own_kv, "tensor", axis=0, tiled=True)
    items = all_kv.shape[0]
    all_kv = all_kv.reshape(items, 2, KEYVALUE_HEADS, head)
    keys, value_rows = all_kv[:, 0], all_kv[:, 1]
    grouped = rot_query.reshape(own_rows, KEYVALUE_HEADS, REPEAT, head)

    index = jnp.arange(items, dtype=jnp.int32)
    own_index = begin + jnp.arange(own_rows, dtype=jnp.int32)
    allowed = (own_segments[:, None] == segment_ids[None, :]) & (
        index[None, :] <= own_index[:, None]
    )
    scores = jnp.einsum("qgrd,kgd->grqk", grouped, keys, preferred_element_type=F32) * scale
    scores = jnp.where(allowed[None, None], scores, NEGATIVE)
    top = jnp.max(scores, axis=-1, keepdims=True)
    weights = jnp.exp(scores - top)
    total = jnp.sum(weights, axis=-1, keepdims=True)
    probs = weights / total
    probs_low = probs.astype(BF16)
    attended = (
        jnp.einsum("grqk,kgd->qgrd", probs_low, value_rows, preferred_element_type=F32)
        .reshape(own_rows, -1)
        .astype(BF16)
    )
    residual = own_inputs + dot_nt(attended, out_t_weight)
    second_own = (residual * rms_scale(residual) * gain_two).astype(BF16)
    second_rows = lax.all_gather(second_own, "tensor", axis=0, tiled=True)

    gate = dot(second_rows, gate_w)
    upper = dot(second_rows, up_w)
    sigmoid = jax.nn.sigmoid(gate)
    swish = gate * sigmoid
    hidden = (swish * upper).astype(BF16)
    d_hidden = dot(grad_rows, down_t)
    d_gate = (d_hidden * upper * sigmoid * (1.0 + gate * (1.0 - sigmoid))).astype(BF16)
    d_up = (d_hidden * swish).astype(BF16)
    second_terms = dot_nt(d_gate, gate_w) + dot_nt(d_up, up_w)
    d_second = lax.psum_scatter(
        second_terms.astype(BF16), "tensor", scatter_dimension=0, tiled=True
    ).astype(F32)
    down_grad = dot_tn(grad_rows, hidden).astype(BF16)
    down_sh = lax.psum_scatter(down_grad, "dp", scatter_dimension=0, tiled=True)
    gate_grad = dot_tn(second_rows, d_gate).astype(BF16)
    gate_sh = lax.psum_scatter(gate_grad, "dp", scatter_dimension=0, tiled=True)
    up_grad = dot_tn(second_rows, d_up).astype(BF16)
    up_sh = lax.psum_scatter(up_grad, "dp", scatter_dimension=0, tiled=True)
    mlp_terms = dot_nt(hidden, down_t).astype(BF16)
    mlp_own = lax.psum_scatter(mlp_terms, "tensor", scatter_dimension=0, tiled=True)
    output = (residual + mlp_own.astype(F32)).astype(BF16)

    residual_part, gain_two_grad = norm_back(residual, gain_two, d_second)
    d_residual = cotangent.astype(F32) + residual_part
    d_branch = d_residual.astype(BF16)
    d_attended = dot(d_branch, out_t_weight).astype(BF16)
    d_att = d_attended.reshape(own_rows, KEYVALUE_HEADS, REPEAT, head)
    d_probs = jnp.einsum("qgrd,kgd->grqk", d_att, value_rows, preferred_element_type=F32)
    inner = jnp.sum(probs * d_probs, axis=-1, keepdims=True)
    d_scores = (scale * probs * (d_probs - inner)).astype(BF16)
    d_rot_query = jnp.einsum("grqk,kgd->qgrd", d_scores, keys, preferred_element_type=F32)
    d_keys = jnp.einsum("grqk,qgrd->kgd", d_scores, grouped, preferred_element_type=F32)
    d_values = jnp.einsum("grqk,qgrd->kgd", probs_low, d_att, preferred_element_type=F32)
    d_kv = lax.psum_scatter(
        jnp.concatenate([d_keys.reshape(items, -1), d_values.reshape(items, -1)], axis=1).astype(
            BF16
        ),
        "tensor",
        scatter_dimension=0,
        tiled=True,
    ).astype(F32)
    d_rot = jnp.concatenate(
        [
            d_rot_query.reshape(own_rows, QUERY_HEADS, head),
            d_kv[:, :half_kv].reshape(own_rows, KEYVALUE_HEADS, head),
        ],
        axis=1,
    )
    d_rot = unrotate(d_rot, cosine, sine).reshape(own_rows, -1)
    d_qkv = jnp.concatenate([d_rot, d_kv[:, half_kv:]], axis=1).astype(BF16)
    d_normed = dot_nt(d_qkv, qkv_weight)
    bias_grad = jnp.sum(d_qkv.astype(F32), axis=0)
    input_part, gain_one_grad = norm_back(own_inputs, gain_one, d_normed)
    input_grad = (d_residual + input_part).astype(BF16)

    qkv_grad = dot_tn(normed_own, d_qkv)
    out_grad = dot_tn(d_branch, attended)
    qb = bias_grad[:edge_q].reshape(tp, dp, -1).transpose(1, 0, 2).reshape(-1)
    kvb = jnp.pad(bias_grad[edge_q:].reshape(dp, -1), ((0, 0), (0, depth - kv_columns // dp)))
    side_grad = jnp.stack([gain_one_grad, gain_two_grad, qb, kvb.reshape(-1)], axis=1)
    side_grad = jnp.pad(side_grad, ((0, 0), (0, 124)))
    attn_grad = jnp.concatenate([qkv_grad, out_grad, side_grad], axis=1).astype(BF16)
    attn_sh = lax.psum_scatter(attn_grad, "dp", scatter_dimension=0, tiled=True)
    q_part = attn_sh[:, :edge_q].reshape(depth, tp, columns).transpose(1, 0, 2)
    o_part = attn_sh[:, edge_kv:edge_o].reshape(depth, tp, columns).transpose(1, 0, 2)
    qo = lax.psum_scatter(
        jnp.concatenate([q_part, o_part], axis=1).reshape(tp * 2 * depth, columns),
        "tensor",
        scatter_dimension=0,
        tiled=True,
    ).astype(F32)
    rest = lax.psum(
        jnp.concatenate([attn_sh[:, edge_q:edge_kv], attn_sh[:, edge_o:]], axis=1), "tensor"
    ).astype(F32)
    side_sh = rest[:, kv_columns : kv_columns + 4].T
    qb_count = query_bias.shape[0]
    return (
        output,
        input_grad,
        side_sh[0],
        qo[:depth],
        lax.dynamic_slice_in_dim(side_sh[2], rank * qb_count, qb_count, 0),
        rest[:, :kv_columns],
        side_sh[3][: kv_columns // dp],
        qo[depth:].T,
        side_sh[1],
        jnp.stack([gate_sh[:, :hidden_units], up_sh[:, :hidden_units]]).astype(F32),
        down_sh[:, :hidden_units].T.astype(F32),
    )


def solution(mesh):
    in_specs = (
        P(("dp", "tensor"), None),
        P("dp"),
        P("dp"),
        P("dp", "tensor"),
        P(("tensor", "dp")),
        P("dp", None),
        P("dp"),
        P("tensor", "dp"),
        P("dp"),
        P(None, "dp", "tensor"),
        P("tensor", "dp"),
        P(("dp", "tensor"), None),
    )
    out_specs = (
        P(("dp", "tensor"), None),
        P(("dp", "tensor"), None),
        P("dp"),
        P("dp", "tensor"),
        P(("tensor", "dp")),
        P("dp", None),
        P("dp"),
        P("tensor", "dp"),
        P("dp"),
        P(None, "dp", "tensor"),
        P("tensor", "dp"),
    )
    return jax.shard_map(local, mesh=mesh, in_specs=in_specs, out_specs=out_specs, check_vma=False)
```

time: 1390 us -> 981 us (0.71)
  waiting for transfers between devices: 1010 us -> 479 us
  Pallas kernels: 0 us -> 192 us
  blocking collectives: 60.7 us -> 0 us
  other arithmetic: 57.1 us -> 40 us
  local copies, waits for them, and re-layouts: 54.9 us -> 70.4 us
    all_gather x8 -> x1, waiting for transfers between devices: 317 us -> 18.4 us  [local(): all_kv = lax.all_gather(own_kv, 'tensor', axis=0, tiled=True)]
    pallas_call x0 -> x1, Pallas kernels: none -> 192 us  [gather_all(): pl.pallas_call(functools.partial(gather_kernel, dp, tp), out_shape=(shape...]
    unnamed x21 -> x11, waiting for transfers between devices: 146 us -> 0.18 us
    reduce_scatter x9 -> x8, waiting for transfers between devices: 455 us -> 379 us  [the longest x1 88.5 us: local(): attn_sh = lax.psum_scatter(attn_grad, 'dp', scatter_dimension=0, tiled=True)]
    unnamed x2 -> x0, blocking collectives: 49.1 us -> none
    another operation x3 -> x13, local copies, waits for them, and re-layouts: 35.7 us -> 4.55 us  [the longest x2 2.45 us: local(): jnp.stack([gate_sh[:, :hidden_units], up_sh[:, :hidden_units]]).astype(F32)]
    slice x2 -> x18, local copies, waits for them, and re-layouts: 1.08 us -> 32.1 us  [the longest x1 15 us: local(): down_t = ff_all[:, 2].reshape(width, padded)]
    convert_element_type x20 -> x10, other arithmetic: 28 us -> 13.6 us  [the longest x1 2.72 us: local(): input_grad = (d_residual + input_part).astype(BF16)]
  transfers between devices with their start and end apart: 20 -> 11, of which waited for: 18 -> 11; matrix products, arithmetic and copies ran while one was open for 14% -> 13% of each run, Pallas kernels for 0% -> 0%
where the time goes in v1:
time: 981 us; the launch traced here: 968 us
  waiting for transfers between devices  479 us (49%)
  Pallas kernels  192 us (20%)
  matrix products  171 us (17%)
  local copies, waits for them, and re-layouts  70.4 us (7%)
  other arithmetic  40 us (4%)
  between operations  15 us (2%)
    pallas_call x1, Pallas kernels, gather_all(): pl.pallas_call(functools.partial(gather_kernel, dp, tp), out_shape=(shape...  192 us
    reduce_scatter x1, waiting for transfers between devices, local(): attn_sh = lax.psum_scatter(attn_grad, 'dp', scatter_dimension=0, tiled=True)  88.5 us
    reduce_scatter x1, waiting for transfers between devices, local(): down_sh = lax.psum_scatter(down_grad, 'dp', scatter_dimension=0, tiled=True)  65.8 us
    reduce_scatter x1, waiting for transfers between devices, local(): up_sh = lax.psum_scatter(up_grad, 'dp', scatter_dimension=0, tiled=True)  63.3 us
    reduce_scatter x1, waiting for transfers between devices, local(): lax.psum_scatter(mlp_terms, 'tensor', scatter_dimension=0, tiled=True)  60.7 us
    dot_general x5, matrix products, dot(): return jnp.dot(left, right, preferred_element_type=F32)  50.3 us
    reduce_scatter x1, waiting for transfers between devices, local(): lax.psum_scatter(second_terms.astype(BF16), 'tensor', scatter_dimension=0...  47.9 us
    all_gather x1, waiting for transfers between devices, local(): second_rows = lax.all_gather(second_own, 'tensor', axis=0, tiled=True)  46.5 us
  transfers between devices with their start and end apart: 11, of which 11 were waited for; matrix products, arithmetic and copies ran while one was open for 13% of the time, Pallas kernels for 0%

profile of v1, /device:TPU:24, one launch (start us, length us, event | category | flops | bytes accessed | tf_op | source)
XLA Modules:
  0.0 968.3 jit_solution(13483319728529815899)
XLA Ops:
  16.1 192.3 %gather_weights.1 = (bf16[8,4,208,384]{3,2,1,0:T(8,128)(2,1)}, bf16[8,4,192,384]{3,2,1,0:T(8,128)(2,1)}, bf16[8,192,640]{2,1,0:T(8,128)(2,1)}, bf16[8,3,192,2304]{3,2,1,0:T(8,128)(2,1)}, bf16[4,256,1536]{2,1,0:T(8,128)(2,1)}) custom-call(bf16[208,384]{1,0:T(8,128)(2,1)} %fusion.66.zq, bf16[192,384]{1,0:T(8,128)(2,1)} %bitcast.201, ...), custom_call_target="tpu_custom_call" | custom-call | tf_op jit(solution)/shard_map/gather_weights/pallas_call | solution.py:318
  244.9 18.4 %all-gather.3.cloned.1.call-done = bf16[1024,512]{1,0:T(8,128)(2,1)} async-done(((bf16[256,512]{1,0:T(8,128)(2,1)}), bf16[1024,512]{1,0:T(8,128)(2,1)}) %all-gather.3.cloned.1.call-update) | async-done | bytes 1048592 | tf_op jit(solution)/shard_map/all_gather | solution.py:419
  267.7 7.0 fusion.78
  286.0 15.0 %fusion.74 = (bf16[8,1,192,2304]{3,2,1,0:T(8,128)(2,1)}, bf16[8,1,192,2304]{3,2,1,0:T(8,128)(2,1)}, bf16[8,1,192,2304]{3,2,1,0:T(8,128)(2,1)}) fusion(bf16[8,3,192,2304]{3,2,1,0:T(8,128)(2,1)} %get-tuple-element.19), kind=kLoop, calls=%fused_computation.146 | loop fusion | bytes 42467328 | tf_op jit(solution)/shard_map/slice | solution.py:398
  301.0 46.5 %all-gather.5.cloned.1.call-done = bf16[1024,1536]{1,0:T(8,128)(2,1)} async-done(((bf16[256,1536]{1,0:T(8,128)(2,1)}), bf16[1024,1536]{1,0:T(8,128)(2,1)}) %all-gather.5.cloned.1.call-update) | async-done | bytes 3145744 | tf_op jit(solution)/shard_map/all_gather | solution.py:444
  347.5 13.4 %fusion.80 = f32[1024,2304]{1,0:T(8,128)} fusion(bf16[1024,1536]{1,0:T(8,128)(2,1)} %all-gather.5.cloned.1.call-done, bf16[1536,2304]{1,0:T(8,128)(2,1)} %bitcast.175), kind=kOutput, calls=%fused_computation.152 | convolution fusion | flops 7247757312 | bytes 19660800 | tf_op jit(solution)/shard_map/dot_general | solution.py:62
  360.9 9.8 %fusion.79 = f32[1024,2304]{1,0:T(8,128)} fusion(bf16[1024,1536]{1,0:T(8,128)(2,1)S(1)} %copy-done.26, bf16[1536,2304]{1,0:T(8,128)(2,1)S(1)} %bitcast.178), kind=kOutput, calls=%fused_computation.151 | convolution fusion | flops 7247757312 | bytes 19660800 | tf_op jit(solution)/shard_map/dot_general | solution.py:62
  370.8 18.7 %multiply_convert_fusion = (bf16[1024,2304]{1,0:T(8,128)(2,1)}, bf16[1024,2304]{1,0:T(8,128)(2,1)}, bf16[1024,2304]{1,0:T(8,128)(2,1)}) fusion(f32[1024,2304]{1,0:T(8,128)} %fusion.79, f32[1024,2304]{1,0:T(8,128)} %fusion.80, bf16[1024,1536]{1,0:T(8,128)(2,1)S(1)} %bitcast.207, bf16[1536,2304]{1,0:T(8,128)(2,1)} %bitcast.173), kind=kOutput, calls=%fused_computation.15 | convolution fusion | flops 7283146752 | bytes 43253760 | tf_op jit(solution)/shard_map/dot_general | solution.py:62
  389.4 11.3 %fusion.81 = f32[1024,1536]{1,0:T(8,128)S(1)} fusion(bf16[1024,2304]{1,0:T(8,128)(2,1)} %get-tuple-element.34, bf16[1536,2304]{1,0:T(8,128)(2,1)} %bitcast.177), kind=kOutput, calls=%fused_computation.153 | convolution fusion | flops 7247757312 | bytes 18087936 | tf_op jit(solution)/shard_map/dot_general | solution.py:66
  400.7 11.1 %add_convert_fusion = bf16[1024,1536]{1,0:T(8,128)(2,1)} fusion(f32[1024,1536]{1,0:T(8,128)S(1)} %fusion.81, bf16[1024,2304]{1,0:T(8,128)(2,1)S(1)} %copy-done.27, bf16[1536,2304]{1,0:T(8,128)(2,1)} %bitcast.176), kind=kOutput, calls=%fused_computation.23 | convolution fusion | flops 7250903040 | bytes 21233664 | tf_op jit(solution)/shard_map/dot_general | solution.py:66
  411.9 12.4 %convolution_convert_fusion.5 = bf16[1024,1536]{1,0:T(8,128)(2,1)} fusion(bf16[1024,2304]{1,0:T(8,128)(2,1)} %get-tuple-element.35, bf16[1536,2304]{1,0:T(8,128)(2,1)} %bitcast.174), kind=kOutput, calls=%fused_computation.34 | convolution fusion | flops 7249330176 | bytes 14942208 | tf_op jit(solution)/shard_map/dot_general | solution.py:66
  424.4 47.9 %reduce-scatter.11.cloned.1.call-done = bf16[256,1536]{1,0:T(8,128)(2,1)} async-done(((bf16[1024,1536]{1,0:T(8,128)(2,1)}), bf16[256,1536]{1,0:T(8,128)(2,1)}) %reduce-scatter.11.cloned.1.call-update) | async-done | bytes 786448 | tf_op jit(solution)/shard_map/reduce_scatter | solution.py:455
  474.0 60.7 %reduce-scatter.9.cloned.1.call-done = bf16[256,1536]{1,0:T(8,128)(2,1)} async-done(((bf16[1024,1536]{1,0:T(8,128)(2,1)}), bf16[256,1536]{1,0:T(8,128)(2,1)}) %reduce-scatter.9.cloned.1.call-update) | async-done | bytes 786448 | tf_op jit(solution)/shard_map/reduce_scatter | solution.py:465
  543.7 6.9 fusion.47
  550.6 6.1 fusion.2
  566.1 12.6 %convolution_convert_fusion.2 = bf16[1536,2304]{1,0:T(8,128)(2,1)} fusion(bf16[1024,1536]{1,0:T(8,128)(2,1)} %all-gather.5.cloned.1.call-done, bf16[1024,2304]{1,0:T(8,128)(2,1)} %get-tuple-element.34), kind=kOutput, calls=%fused_computation.13 | convolution fusion | flops 7251296256 | bytes 14942208 | tf_op jit(solution)/shard_map/dot_general | solution.py:70
  610.6 13.1 %convolution_convert_fusion.1 = bf16[1536,2304]{1,0:T(8,128)(2,1)} fusion(bf16[1024,1536]{1,0:T(8,128)(2,1)} %all-gather.5.cloned.1.call-done, bf16[1024,2304]{1,0:T(8,128)(2,1)} %get-tuple-element.33), kind=kOutput, calls=%fused_computation.12 | convolution fusion | flops 7251296256 | bytes 14942208 | tf_op jit(solution)/shard_map/dot_general | solution.py:70
  623.7 12.4 %convolution_convert_fusion = bf16[1536,2304]{1,0:T(8,128)(2,1)} fusion(bf16[1024,1536]{1,0:T(8,128)(2,1)} %bitcast.206, bf16[1024,2304]{1,0:T(8,128)(2,1)} %get-tuple-element.35), kind=kOutput, calls=%fused_computation.11 | convolution fusion | flops 7251296256 | bytes 14942208 | tf_op jit(solution)/shard_map/dot_general | solution.py:70
  640.3 22.3 %reduce-scatter.19.cloned.1.call-done = bf16[192,2304]{1,0:T(8,128)(2,1)} async-done(((bf16[1536,2304]{1,0:T(8,128)(2,1)}), bf16[192,2304]{1,0:T(8,128)(2,1)}) %reduce-scatter.19.cloned.1.call-update) | async-done | bytes 884752 | tf_op jit(solution)/shard_map/reduce_scatter | solution.py:461
  663.8 88.5 %reduce-scatter.15.cloned.1.call-done = bf16[192,3712]{1,0:T(8,128)(2,1)} async-done(((bf16[1536,3712]{1,0:T(8,128)(2,1)}), bf16[192,3712]{1,0:T(8,128)(2,1)}) %reduce-scatter.15.cloned.1.call-update) | async-done | bytes 1425424 | tf_op jit(solution)/shard_map/reduce_scatter | solution.py:508
  758.4 63.3 %reduce-scatter.21.cloned.1.call-done = bf16[192,2304]{1,0:T(8,128)(2,1)} async-done(((bf16[1536,2304]{1,0:T(8,128)(2,1)}), bf16[192,2304]{1,0:T(8,128)(2,1)}) %reduce-scatter.21.cloned.1.call-update) | async-done | bytes 884752 | tf_op jit(solution)/shard_map/reduce_scatter | solution.py:463
  825.0 65.8 %reduce-scatter.23.cloned.1.call-done = bf16[192,2304]{1,0:T(8,128)(2,1)} async-done(((bf16[1536,2304]{1,0:T(8,128)(2,1)}), bf16[192,2304]{1,0:T(8,128)(2,1)}) %reduce-scatter.23.cloned.1.call-update) | async-done | bytes 884752 | tf_op jit(solution)/shard_map/reduce_scatter | solution.py:459
  893.3 34.6 %all-reduce.8.cloned.1.call-done = bf16[192,640]{1,0:T(8,128)(2,1)} async-done(((bf16[192,640]{1,0:T(8,128)(2,1)}), bf16[192,640]{1,0:T(8,128)(2,1)}) %all-reduce.8.cloned.1.call-update) | async-done | bytes 245776 | tf_op jit(solution)/shard_map/psum | solution.py:517
  932.7 25.3 %reduce-scatter.17.cloned.1.call-done = bf16[384,384]{1,0:T(8,128)(2,1)} async-done(((bf16[1536,384]{1,0:T(8,128)(2,1)}), bf16[384,384]{1,0:T(8,128)(2,1)}) %reduce-scatter.17.cloned.1.call-update) | async-done | bytes 294928 | tf_op jit(solution)/shard_map/reduce_scatter | solution.py:511
  (203 shorter events, 138.0 us)
Async XLA Ops:
  7.2 256.1 %all-gather.3.cloned.1.call-start = ((), (), s32[]{:S(2)}) async-start(), calls=%async_computation.8 | async-start | bytes 1310720 | tf_op jit(solution)/shard_map/all_gather | solution.py:419
  232.5 9.0 copy-start.15
  235.2 112.3 %all-gather.5.cloned.1.call-start = ((), (), s32[]{:S(2)}) async-start(), calls=%async_computation.9 | async-start | bytes 3932160 | tf_op jit(solution)/shard_map/all_gather | solution.py:444
  244.6 30.0 %copy-start.6 = (bf16[256,12,128]{0,2,1:T(8,128)(2,1)}, bf16[256,12,128]{0,2,1:T(8,128)(2,1)S(1)}, u32[]{:S(2)}) copy-start(bf16[256,12,128]{0,2,1:T(8,128)(2,1)S(1)} %pad_maximum_fusion.10) | copy-start | bytes 2359300
  266.2 8.5 copy-start.8
  285.5 186.8 %reduce-scatter.11.cloned.1.call-start = ((), (), s32[]{:S(2)}) async-start(), calls=%async_computation.11 | async-start | bytes 3932160 | tf_op jit(solution)/shard_map/reduce_scatter | solution.py:455
  347.5 13.4 %copy-start.5 = (bf16[8,1,192,2304]{3,2,1,0:T(8,128)(2,1)S(1)}, bf16[8,1,192,2304]{3,2,1,0:T(8,128)(2,1)}, u32[]{:S(2)}) copy-start(bf16[8,1,192,2304]{3,2,1,0:T(8,128)(2,1)} %get-tuple-element.32) | copy-start | bytes 21233668
  347.5 13.4 %copy-start.26 = (bf16[1024,1536]{1,0:T(8,128)(2,1)S(1)}, bf16[1024,1536]{1,0:T(8,128)(2,1)}, u32[]{:S(2)}) copy-start(bf16[1024,1536]{1,0:T(8,128)(2,1)} %all-gather.5.cloned.1.call-done) | copy-start | bytes 9437188
  360.9 9.8 %copy-start.25 = (bf16[4,256,1536]{2,1,0:T(8,128)(2,1)S(1)}, bf16[4,256,1536]{2,1,0:T(8,128)(2,1)}, u32[]{:S(2)}) copy-start(bf16[4,256,1536]{2,1,0:T(8,128)(2,1)} %get-tuple-element.20) | copy-start | bytes 9437188
  389.4 11.3 %copy-start.27 = (bf16[1024,2304]{1,0:T(8,128)(2,1)S(1)}, bf16[1024,2304]{1,0:T(8,128)(2,1)}, u32[]{:S(2)}) copy-start(bf16[1024,2304]{1,0:T(8,128)(2,1)} %get-tuple-element.33) | copy-start | bytes 14155780
  411.9 122.9 %reduce-scatter.9.cloned.1.call-start = ((), (), s32[]{:S(2)}) async-start(), calls=%async_computation.10 | async-start | bytes 3932160 | tf_op jit(solution)/shard_map/reduce_scatter | solution.py:465
  424.3 110.5 %copy-start.7 = (bf16[256,1536]{1,0:T(8,128)(2,1)S(1)}, bf16[256,1536]{1,0:T(8,128)(2,1)}, u32[]{:S(2)}) copy-start(bf16[256,1536]{1,0:T(8,128)(2,1)} %cot.1) | copy-start | bytes 2359300
  424.3 167.9 %reduce-scatter.13.cloned.1.call-start = ((), (), s32[]{:S(2)}) async-start(), calls=%async_computation.12 | async-start | bytes 1310720 | tf_op jit(solution)/shard_map/reduce_scatter | solution.py:479
  543.7 13.0 %slice-start.4 = ((s8[12582912]{0:T(1024)(128)(4,1)}), s8[4194304]{0:T(1024)(128)(4,1)S(1)}, s32[]{:S(2)}) async-start(s8[12582912]{0:T(1024)(128)(4,1)} %bitcast.167), calls=%async_computation.23 | async-start | bytes 8388608
  543.7 13.0 %slice-start.5 = ((s8[12582912]{0:T(1024)(128)(4,1)}), s8[4194304]{0:T(1024)(128)(4,1)S(1)}, s32[]{:S(2)}) async-start(s8[12582912]{0:T(1024)(128)(4,1)} %bitcast.167), calls=%async_computation.24 | async-start | bytes 8388608
  566.0 96.5 %reduce-scatter.19.cloned.1.call-start = ((), (), s32[]{:S(2)}) async-start(), calls=%async_computation.16 | async-start | bytes 7962624 | tf_op jit(solution)/shard_map/reduce_scatter | solution.py:461
  578.7 173.6 %reduce-scatter.15.cloned.1.call-start = ((), (), s32[]{:S(2)}) async-start(), calls=%async_computation.13 | async-start | bytes 12828672 | tf_op jit(solution)/shard_map/reduce_scatter | solution.py:508
  585.0 8.4 copy-start.16
  585.1 8.4 copy-start.19
  587.3 8.2 copy-start.24
  610.5 211.2 %reduce-scatter.21.cloned.1.call-start = ((), (), s32[]{:S(2)}) async-start(), calls=%async_computation.17 | async-start | bytes 7962624 | tf_op jit(solution)/shard_map/reduce_scatter | solution.py:463
  623.7 267.1 %reduce-scatter.23.cloned.1.call-start = ((), (), s32[]{:S(2)}) async-start(), calls=%async_computation.18 | async-start | bytes 7962624 | tf_op jit(solution)/shard_map/reduce_scatter | solution.py:459
  636.1 291.7 %all-reduce.8.cloned.1.call-start = ((), (), s32[]{:S(2)}) async-start(), calls=%async_computation.14 | async-start | bytes 491520 | tf_op jit(solution)/shard_map/psum | solution.py:517
  754.8 203.2 %reduce-scatter.17.cloned.1.call-start = ((), (), s32[]{:S(2)}) async-start(), calls=%async_computation.15 | async-start | bytes 1474560 | tf_op jit(solution)/shard_map/reduce_scatter | solution.py:511
  (22 other events, 99.4 us)
Sparse Core Ops, SparseCore 0:
  235.3 27.9 all-gather.2
  285.7 61.8 all-gather.4
  412.0 60.2 reduce-scatter.10
  474.5 60.2 reduce-scatter.8
  566.1 26.0 reduce-scatter.12
  596.1 66.4 reduce-scatter.18
  666.2 85.9 reduce-scatter.14
  756.2 65.4 reduce-scatter.20
  825.2 65.4 reduce-scatter.22
  893.6 34.1 all-reduce.7
  930.1 27.7 reduce-scatter.16

commit v2 on v1

--- a/solution.py
+++ b/solution.py
@@ -180,17 +180,24 @@
         for copy in self.sends(mask):
             copy.start()
 
-    def finish(self):
+    def spread(self):
+        for mask in range(1, self.half):
+            self.hand_on(mask)
+
+    def complete(self):
         for mask in range(self.half):
             self.arrival(self.half + mask).wait_recv()
+
+    def finish(self):
         for mask in range(self.half):
             for copy in self.sends(mask):
                 copy.wait_send()
 
 
 class LineGather:
-    def __init__(self, place, own, full, send, recv):
+    def __init__(self, place, own, full, send, recv, offsets=(1, -1)):
         self.place, self.own, self.full, self.send, self.recv = place, own, full, send, recv
+        self.offsets = offsets
 
     def copy(self, distance, offset):
         place = self.place
@@ -207,7 +214,7 @@
 
     def each(self, distance, act):
         place = self.place
-        for offset in (1, -1):
+        for offset in self.offsets:
 
             @pl.when(place.has(-offset * distance) & place.has(offset))
             def _():
@@ -218,7 +225,7 @@
 
     def arrived(self, distance):
         place = self.place
-        for offset in (1, -1):
+        for offset in self.offsets:
 
             @pl.when(place.has(-offset * distance))
             def _():
@@ -242,100 +249,847 @@
             self.each(distance, lambda copy: copy.wait_send())
 
 
-def gather_kernel(
-    dp, tp, zq, zo, kvs, ff, cot, q_out, o_out, kv_out, ff_out, cot_out,
-    plane_send, plane_recv, line_send, line_recv, local_sem,
+def turned(rows, cosine, sine):
+    return rows * cosine + pltpu.roll(rows, rows.shape[1] // 2, 1) * sine
+
+
+def forward_kernel(
+    dp, tp, kvb_count, qb_count,
+    x, seg_row, seg_col, zq, zo, zb, kvs, ff, cot,
+    ff_out, cot_out, n2_out, wq_out, wo_out, wkv_out, p_out,
+    res, att, n1, q, kv, cosine, sine, vectors,
+    wq, wo, wkv, wb, spread, mask, probs, n2, n2_own,
+    plane_send, plane_recv, line_send, line_recv, local_sem, probs_sem,
 ):
     place = Place(dp, tp)
     d, z = place.d, place.z
-    locals_ = [
-        pltpu.make_async_copy(zq, q_out.at[d, z], local_sem.at[0]),
-        pltpu.make_async_copy(zo, o_out.at[d, z], local_sem.at[1]),
-        pltpu.make_async_copy(kvs, kv_out.at[d], local_sem.at[2]),
-        pltpu.make_async_copy(ff, ff_out.at[d], local_sem.at[3]),
-        pltpu.make_async_copy(cot, cot_out.at[z], local_sem.at[4]),
-    ]
-    for copy in locals_:
-        copy.start()
-    place.greet(True, True)
+    own_rows, width = x.shape
+    depth, columns = zq.shape
+    items = seg_row.shape[1]
+    head = HEAD_DIMENSION
+    kv_columns = kv.shape[1]
+    my_rows = pl.ds(pl.multiple_of(d * depth, 16), depth)
+
+    def rows_of(b):
+        return pl.ds(pl.multiple_of(b * depth, 16), depth)
 
     def plane(item, own, full):
         return PlaneGather(
             place, own, full, lambda m: plane_send.at[item, m], lambda m: plane_recv.at[item, m]
         )
 
-    def line(item, own, full):
+    def line(item, own, full, offsets=(1, -1)):
         return LineGather(
             place,
             own,
             full,
             lambda s, k: line_send.at[item, s, k],
             lambda s, k: line_recv.at[item, s, k],
+            offsets,
         )
 
-    line_q = line(0, zq, lambda t: q_out.at[d, t])
-    line_o = line(1, zo, lambda t: o_out.at[d, t])
-    line_cot = line(2, cot, lambda t: cot_out.at[t])
-    plane_kv = plane(0, kvs, lambda b: kv_out.at[b])
-    plane_q = plane(1, q_out.at[d], lambda b: q_out.at[b])
-    plane_o = plane(2, o_out.at[d], lambda b: o_out.at[b])
+    starts = [
+        pltpu.make_async_copy(zq, wq.at[z, my_rows], local_sem.at[0]),
+        pltpu.make_async_copy(zo, wo.at[z, my_rows], local_sem.at[1]),
+        pltpu.make_async_copy(zb, wb.at[d, z], local_sem.at[2]),
+        pltpu.make_async_copy(kvs, wkv.at[my_rows], local_sem.at[3]),
+        pltpu.make_async_copy(ff, ff_out.at[d], local_sem.at[4]),
+        pltpu.make_async_copy(cot, cot_out.at[z], local_sem.at[5]),
+    ]
+    for copy in starts:
+        copy.start()
+    place.greet(True, True)
+    line_q = line(0, zq, lambda t: wq.at[t, my_rows])
+    line_o = line(1, zo, lambda t: wo.at[t, my_rows])
+    line_b = line(2, zb, lambda t: wb.at[d, t])
+    line_cot = line(3, cot, lambda t: cot_out.at[t])
+    line_kv = line(
+        4,
+        kv.at[pl.ds(pl.multiple_of(z * own_rows, 16), own_rows)],
+        lambda t: kv.at[pl.ds(pl.multiple_of(t * own_rows, 16), own_rows)],
+        (1,),
+    )
+    line_n2 = line(5, n2, lambda t: n2_out.at[t])
+    plane_kv = plane(0, kvs, lambda b: wkv.at[rows_of(b)])
+    plane_q = plane(1, wq.at[:, my_rows], lambda b: wq.at[:, rows_of(b)])
+    plane_o = plane(2, wo.at[:, my_rows], lambda b: wo.at[:, rows_of(b)])
+    plane_b = plane(3, wb.at[d], lambda b: wb.at[b])
     plane_ff = [
-        plane(3 + part, ff.at[part], lambda b, part=part: ff_out.at[b, part]) for part in (2, 0, 1)
+        plane(4 + part, ff.at[part], lambda b, part=part: ff_out.at[b, part]) for part in (2, 0, 1)
     ]
+    line_b.start()
     line_q.start()
     plane_kv.start()
+    plane_ff[0].start()
+
+    begin = z * own_rows
+    row_at = begin + lax.broadcasted_iota(jnp.int32, (own_rows, items), 0)
+    col_at = lax.broadcasted_iota(jnp.int32, (own_rows, items), 1)
+    mine, theirs = seg_col[...], seg_row[...]
+    allowed = (mine == theirs) & (col_at <= row_at)
+    mask[...] = jnp.where(allowed, 0.0, NEGATIVE)
+    below = jnp.sum(jnp.where(theirs < mine, 1.0, 0.0), axis=1, keepdims=True)
+    lane = lax.broadcasted_iota(jnp.int32, (own_rows, head), 1)
+    half = lane % (head // 2)
+    index = begin + lax.broadcasted_iota(jnp.int32, (own_rows, head), 0)
+    freqs = jnp.exp(half.astype(F32) * (-2.0 * math.log(THETA) / head))
+    angles = (index.astype(F32) - below) * freqs
+    cosine[...] = jnp.cos(angles)
+    sine[...] = jnp.sin(angles) * jnp.where(lane < head // 2, -1.0, 1.0)
+
     for distance in range(1, tp):
+        line_b.hand_on(distance)
+    line_q.hand_on(1)
+    line_o.start()
+    for distance in range(2, tp):
         line_q.hand_on(distance)
-    line_o.start()
-    locals_[0].wait()
+    starts[2].wait()
+    starts[0].wait()
+    plane_b.start()
     plane_q.start()
-    for mask in range(1, 1 << place.steps):
-        plane_kv.hand_on(mask)
+    plane_kv.spread()
     for distance in range(1, tp):
         line_o.hand_on(distance)
+    starts[1].wait()
+    plane_o.start()
     line_cot.start()
-    locals_[1].wait()
-    queue = [plane_q, plane_o] + plane_ff
-    for item, following in zip(queue, queue[1:] + [None]):
-        if following is not None:
-            following.start()
-        for mask in range(1, 1 << place.steps):
-            item.hand_on(mask)
-    for distance in range(1, tp):
+    starts[3].wait()
+    plane_kv.complete()
+
+    pick_row = lax.broadcasted_iota(jnp.int32, (16, 128), 0)
+    pick_col = lax.broadcasted_iota(jnp.int32, (16, 128), 1)
+    pick = jnp.where(pick_row == pick_col, 1.0, 0.0).astype(BF16)
+    rows16 = dot_nt(pick, wkv[:, kv_columns:])
+    vectors[...] = rows16
+    block_row = lax.broadcasted_iota(jnp.int32, (depth, kv_columns), 0)
+    block_col = lax.broadcasted_iota(jnp.int32, (depth, kv_columns), 1)
+    for b in range(dp):
+        hit = (block_row < kvb_count) & (block_col == block_row + b * kvb_count)
+        spread[b * depth : (b + 1) * depth, :] = jnp.where(hit, 1.0, 0.0).astype(BF16)
+    kv_bias = dot(rows16.astype(BF16), spread[...])[2:3, :]
+
+    xs = x[...].astype(F32)
+    n1[...] = (xs * rms_scale(xs) * rows16[0:1, :]).astype(BF16)
+    kv_rows = dot(n1[...], wkv[:, :kv_columns]) + kv_bias
+    at = pl.ds(pl.multiple_of(begin, 16), own_rows)
+    for h in range(KEYVALUE_HEADS):
+        cut = slice(h * head, (h + 1) * head)
+        kv[at, cut] = turned(kv_rows[:, cut], cosine[...], sine[...]).astype(BF16)
+    kv[at, KEYVALUE_HEADS * head :] = kv_rows[:, KEYVALUE_HEADS * head :].astype(BF16)
+    line_kv.start()
+
+    plane_b.spread()
+    plane_q.spread()
+    plane_b.complete()
+    small_row = lax.broadcasted_iota(jnp.int32, (128, columns), 0)
+    small_col = lax.broadcasted_iota(jnp.int32, (128, columns), 1)
+    q_bias = jnp.zeros((tp * 16, columns), F32)
+    for b in range(dp):
+        hit = (small_row < qb_count) & (small_col == small_row + b * qb_count)
+        one = jnp.where(hit, 1.0, 0.0).astype(BF16)
+        q_bias = q_bias + dot(wb[b].reshape(tp * 16, 128), one)
+    plane_ff[0].spread()
+    plane_ff[1].start()
+    line_kv.hand_on(1)
+    line_cot.hand_on(1)
+    plane_q.complete()
+    for t in range(tp):
+        rows = dot(n1[...], wq[t]) + q_bias[t * 16 : t * 16 + 1, :]
+        for h in range(columns // head):
+            cut = slice(h * head, (h + 1) * head)
+            out = slice(t * columns + h * head, t * columns + (h + 1) * head)
+            q[:, out] = turned(rows[:, cut], cosine[...], sine[...]).astype(BF16)
+    line_kv.hand_on(2)
+    plane_o.spread()
+    for distance in range(3, tp):
+        line_kv.hand_on(distance)
+    line_cot.hand_on(2)
+    outs = [
+        pltpu.make_async_copy(wq, wq_out, local_sem.at[0]),
+        pltpu.make_async_copy(wkv, wkv_out, local_sem.at[3]),
+    ]
+    for copy in outs:
+        copy.start()
+
+    scale = 1.0 / math.sqrt(head)
+    group = QUERY_HEADS // tp
+
+    def probs_copy(part, count):
+        at = pl.ds(part * group, group)
+        return pltpu.make_async_copy(
+            probs.at[at, :, pl.ds(0, count)], p_out.at[at, :, pl.ds(0, count)], probs_sem.at[part]
+        )
+
+    for part in range(tp):
+        for blocks in range(1, tp + 1):
+            count = blocks * own_rows
+
+            @pl.when(z == blocks - 1)
+            def _():
+                def one_head(i, carry):
+                    h = part * group + i
+                    at = pl.ds(pl.multiple_of(h * head, head), head)
+                    shared = h // REPEAT
+                    key_at = pl.ds(pl.multiple_of(shared * head, head), head)
+                    value_at = pl.ds(pl.multiple_of((KEYVALUE_HEADS + shared) * head, head), head)
+                    scores = dot_nt(q[:, at], kv[0:count, key_at]) * scale + mask[:, 0:count]
+                    top = jnp.max(scores, axis=1, keepdims=True)
+                    weights = jnp.exp(scores - top)
+                    total = jnp.sum(weights, axis=1, keepdims=True)
+                    low = (weights / total).astype(BF16)
+                    probs[h, :, 0:count] = low
+                    att[:, at] = dot(low, kv[0:count, value_at]).astype(BF16)
+                    return carry
+
+                lax.fori_loop(0, group, one_head, 0)
+                probs_copy(part, count).start()
+
+        if part == 0:
+            plane_ff[1].spread()
+            plane_ff[2].start()
+    plane_o.complete()
+    outs.append(pltpu.make_async_copy(wo, wo_out, local_sem.at[1]))
+    outs[-1].start()
+    for j in range(width // 512):
+        cut = slice(j * 512, (j + 1) * 512)
+        acc = x[:, cut].astype(F32)
+        for t in range(tp):
+            acc = acc + dot_nt(att[:, t * columns : (t + 1) * columns], wo[t, cut, :])
+        res[:, cut] = acc
+    residual = res[...]
+    n2[...] = (residual * rms_scale(residual) * vectors[1:2, :]).astype(BF16)
+    line_n2.start()
+    n2_copy = pltpu.make_async_copy(n2, n2_out.at[z], local_sem.at[2])
+    n2_copy.start()
+    for distance in range(3, tp):
         line_cot.hand_on(distance)
-    for item in [plane_kv] + queue:
+    line_n2.hand_on(1)
+    plane_ff[2].spread()
+    for distance in range(2, tp):
+        line_n2.hand_on(distance)
+    for item in plane_ff:
+        item.complete()
+    for item in [plane_kv, plane_q, plane_o, plane_b] + plane_ff:
         item.finish()
-    for item in (line_q, line_o, line_cot):
+    for item in (line_q, line_o, line_b, line_cot, line_kv, line_n2):
         item.finish()
-    for copy in locals_[2:]:
+    for copy in starts[4:] + outs + [n2_copy]:
         copy.wait()
-
-
-def gather_all(dp, tp, zq, zo, kvs, ff, cot):
-    def shape(*dims):
-        return jax.ShapeDtypeStruct(dims, BF16)
-
+    for part in range(tp):
+        for blocks in range(1, tp + 1):
+
+            @pl.when(z == blocks - 1)
+            def _():
+                probs_copy(part, blocks * own_rows).wait()
+
+
+def forward_part(dp, tp, kvb_count, qb_count, x, seg_row, seg_col, zq, zo, zb, kvs, ff, cot):
+    def shape(*dims, kind=BF16):
+        return jax.ShapeDtypeStruct(dims, kind)
+
+    own_rows, width = x.shape
+    depth, columns = zq.shape
+    items = seg_row.shape[1]
+    head = HEAD_DIMENSION
+    kv_columns = 2 * KEYVALUE_HEADS * head
+    vmem = pl.BlockSpec(memory_space=pltpu.VMEM)
+    anywhere = pl.BlockSpec(memory_space=ANY)
     return pl.pallas_call(
-        functools.partial(gather_kernel, dp, tp),
+        functools.partial(forward_kernel, dp, tp, kvb_count, qb_count),
         out_shape=(
-            shape(dp, tp, *zq.shape),
-            shape(dp, tp, *zo.shape),
-            shape(dp, *kvs.shape),
             shape(dp, *ff.shape),
             shape(tp, *cot.shape),
+            shape(tp, own_rows, width),
+            shape(tp, width, columns),
+            shape(tp, width, columns),
+            shape(width, kvs.shape[1]),
+            shape(QUERY_HEADS, own_rows, items),
+            shape(own_rows, width, kind=F32),
+            shape(own_rows, tp * columns),
+            shape(own_rows, width),
+            shape(own_rows, tp * columns),
+            shape(items, kv_columns),
+            shape(own_rows, head, kind=F32),
+            shape(own_rows, head, kind=F32),
+            shape(16, width, kind=F32),
         ),
-        in_specs=[pl.BlockSpec(memory_space=ANY)] * 5,
-        out_specs=[pl.BlockSpec(memory_space=ANY)] * 5,
+        in_specs=[vmem] * 7 + [anywhere] * 2,
+        out_specs=(anywhere,) * 7 + (vmem,) * 8,
         scratch_shapes=[
-            pltpu.SemaphoreType.DMA((6, dp)),
-            pltpu.SemaphoreType.DMA((6, dp)),
-            pltpu.SemaphoreType.DMA((3, 2, tp)),
-            pltpu.SemaphoreType.DMA((3, 2, tp)),
-            pltpu.SemaphoreType.DMA((5,)),
+            pltpu.VMEM((tp, width, columns), BF16),
+            pltpu.VMEM((tp, width, columns), BF16),
+            pltpu.VMEM((width, kvs.shape[1]), BF16),
+            pltpu.VMEM((dp, tp, 16, 128), BF16),
+            pltpu.VMEM((width, kv_columns), BF16),
+            pltpu.VMEM((own_rows, items), F32),
+            pltpu.VMEM((QUERY_HEADS, own_rows, items), BF16),
+            pltpu.VMEM((own_rows, width), BF16),
+            pltpu.VMEM((16, 128), BF16),
+            pltpu.SemaphoreType.DMA((7, dp)),
+            pltpu.SemaphoreType.DMA((7, dp)),
+            pltpu.SemaphoreType.DMA((6, 2, tp)),
+            pltpu.SemaphoreType.DMA((6, 2, tp)),
+            pltpu.SemaphoreType.DMA((6,)),
+            pltpu.SemaphoreType.DMA((tp,)),
         ],
-        compiler_params=pltpu.CompilerParams(collective_id=0, has_side_effects=True),
-        name="gather_weights",
-    )(zq, zo, kvs, ff, cot)
+        compiler_params=pltpu.CompilerParams(
+            collective_id=0, has_side_effects=True, vmem_limit_bytes=56 << 20
+        ),
+        name="forward_part",
+    )(x, seg_row, seg_col, zq, zo, zb, kvs, ff, cot)
+
+
+class PlaneReduce:
+    def __init__(self, place, part, held, send, recv):
+        self.place, self.part, self.held, self.send, self.recv = place, part, held, send, recv
+        self.half = 1 << place.steps
+        self.last = place.steps
+
+    def count(self, level):
+        return self.half >> level
+
+    def slot(self, level, i):
+        return sum(self.count(k) for k in range(level)) + i
+
+    def copy(self, level, i):
+        place = self.place
+        slot = self.slot(level, i)
+        if level:
+            src, device = self.held(self.slot(level - 1, 2 * i + 1)), place.partners[level - 1]
+        else:
+            src, device = self.part(place.sibling_block(i)), place.sibling
+        return remote(
+            src, self.held(slot), self.send(slot), self.recv(slot), place.device(device)
+        )
+
+    def start(self, level):
+        for i in range(self.count(level)):
+            self.copy(level, i).start()
+
+    def wait_send(self, level):
+        for i in range(self.count(level)):
+            self.copy(level, i).wait_send()
+
+    def absorb(self, level, out=None):
+        order = sorted(range(self.count(level)), key=lambda i: 1 - i % 2)
+        for i in order:
+            slot = self.slot(level, i)
+            self.copy(level, i).wait_recv()
+            if level:
+                other = self.held(self.slot(level - 1, 2 * i))
+            else:
+                other = self.part(self.place.block(i))
+            add_into(self.held(slot), other, self.held(slot) if out is None else out)
+            if i % 2:
+                self.copy(level + 1, i // 2).start()
+
+
+def add_into(one, other, out):
+    rows = one.shape[0]
+    step = 48 if rows % 48 == 0 else rows
+
+    def body(k, carry):
+        at = pl.ds(pl.multiple_of(k * step, 16), step)
+        out[at, :] = (one[at, :].astype(F32) + other[at, :].astype(F32)).astype(out.dtype)
+        return carry
+
+    lax.fori_loop(0, rows // step, body, 0)
+
+
+FF_PARTS = 3
+
+
+class LineReduce:
+    def __init__(self, place, term, sent, got, send, recv):
+        self.place, self.term, self.sent, self.got = place, term, sent, got
+        self.send, self.recv = send, recv
+
+    def owner(self, turn):
+        place = self.place
+        if turn == place.tp - 1:
+            return place.z
+        falling = place.tp - 1 - turn
+        falling = jnp.where(falling > place.z, falling, falling - 1)
+        rising = jnp.where(turn < place.z, turn, turn + 1)
+        return jnp.where(place.z < place.tp // 2, falling, rising)
+
+    def way(self, turn):
+        place = self.place
+        owner = self.owner(turn)
+        right = jnp.where(owner > place.z, 1, 0)
+        side, offset = 1 - right, 2 * right - 1
+        return side, offset, (owner - place.z) * offset
+
+    def copy(self, turn):
+        side, offset, distance = self.way(turn)
+        return remote(
+            self.sent(turn),
+            self.got(side, distance - 1),
+            self.send(turn),
+            self.recv(side, distance - 1),
+            self.place.beside(offset),
+        )
+
+    def arrival(self, side, distance):
+        ref = self.got(side, distance)
+        return remote(
+            ref, ref, self.send(0), self.recv(side, distance), self.place.beside(0)
+        )
+
+    def step(self, turn):
+        side, offset, distance = self.way(turn)
+        fed = self.place.has(-offset)
+
+        @pl.when(fed)
+        def _():
+            self.arrival(side, distance).wait_recv()
+            add_into(self.term(turn), self.got(side, distance), self.sent(turn))
+
+        if self.term is not self.sent:
+
+            @pl.when(jnp.logical_not(fed))
+            def _():
+                copy_into(self.term(turn), self.sent(turn))
+
+        self.copy(turn).start()
+
+    def total(self, out):
+        last = self.place.tp - 1
+        copy_into(self.term(last), out)
+        for side, offset in ((0, -1), (1, 1)):
+
+            @pl.when(self.place.has(offset))
+            def _():
+                self.arrival(side, 0).wait_recv()
+                add_into(out, self.got(side, 0), out)
+
+    def finish(self):
+        for turn in range(self.place.tp - 1):
+            self.copy(turn).wait_send()
+
+
+def copy_into(one, out):
+    rows = one.shape[0]
+    step = 32 if rows % 32 == 0 else rows
+
+    def body(k, carry):
+        at = pl.ds(pl.multiple_of(k * step, 16), step)
+        out[at, :] = one[at, :].astype(out.dtype)
+        return carry
+
+    lax.fori_loop(0, rows // step, body, 0)
+
+
+def ff_kernel(
+    dp, tp, ff, cot, n2, act, lhs, mlp, d2,
+    wg, wu, wd, x, ct, made, term, sent, got, branch, turned_rows,
+    w_sem, in_sem, act_sem, lhs_sem, mlp_sem, send_sem, recv_sem,
+):
+    place = Place(dp, tp)
+    own_rows, width = d2.shape
+    depth = ff.shape[2]
+    padded = ff.shape[3]
+    tile = 256
+    weights = (wg, wu, wd)
+    loads = [
+        [
+            pltpu.make_async_copy(
+                ff.at[b, p], weights[p].at[pl.ds(b * depth, depth)], w_sem.at[p, b]
+            )
+            for b in range(dp)
+        ]
+        for p in range(FF_PARTS)
+    ]
+    sums = LineReduce(
+        place,
+        lambda turn: term.at[turn % 2],
+        lambda turn: sent.at[turn],
+        lambda side, k: got.at[side, k],
+        lambda turn: send_sem.at[turn],
+        lambda side, k: recv_sem.at[side, k],
+    )
+
+    def fetch(turn):
+        owner = sums.owner(turn)
+        return [
+            pltpu.make_async_copy(n2.at[owner], x.at[turn % 2], in_sem.at[turn % 2, 0]),
+            pltpu.make_async_copy(cot.at[owner], ct.at[turn % 2], in_sem.at[turn % 2, 1]),
+        ]
+
+    def stores(turn, kinds=(0, 1, 2)):
+        return [copies() for kind, copies in enumerate(store_kinds(turn)) if kind in kinds]
+
+    def store_kinds(turn):
+        owner = sums.owner(turn)
+        at = pl.ds(pl.multiple_of(owner * own_rows, 128), own_rows)
+        slot = turn % 2
+        return (
+            lambda: [
+                pltpu.make_async_copy(made.at[slot, p], act.at[p, at], act_sem.at[slot, p])
+                for p in range(FF_PARTS)
+            ],
+            lambda: [
+                pltpu.make_async_copy(
+                    turned_rows.at[slot, k], lhs.at[k, :, at], lhs_sem.at[slot, k]
+                )
+                for k in range(2)
+            ],
+            lambda: [pltpu.make_async_copy(branch.at[slot], mlp.at[owner], mlp_sem.at[slot])],
+        )
+
+    for copy in fetch(0):
+        copy.start()
+    for part in loads:
+        for copy in part:
+            copy.start()
+    place.greet(False, True)
+    for turn in range(tp):
+        slot = turn % 2
+        for copy in fetch(turn):
+            copy.wait()
+        if turn + 1 < tp:
+            for copy in fetch(turn + 1):
+                copy.start()
+        if turn >= 2:
+            for copies in stores(turn - 2):
+                for copy in copies:
+                    copy.wait()
+        turned_rows[slot, 0] = x[slot].T
+        turned_rows[slot, 1] = ct[slot].T
+        for copy in stores(turn, (1,))[0]:
+            copy.start()
+        if turn == 0:
+            for part in loads:
+                for copy in part:
+                    copy.wait()
+
+        def units(n, carry, slot=slot):
+            for k in range(3):
+                at = pl.ds(pl.multiple_of((n * 3 + k) * tile, tile), tile)
+                gate = dot(x[slot], wg[:, at])
+                upper = dot(x[slot], wu[:, at])
+                d_hidden = dot(ct[slot], wd[:, at])
+                sigmoid = 1.0 / (1.0 + jnp.exp(-gate))
+                swish = gate * sigmoid
+                made[slot, 2, :, at] = (swish * upper).astype(BF16)
+                made[slot, 1, :, at] = (d_hidden * swish).astype(BF16)
+                made[slot, 0, :, at] = (
+                    d_hidden * upper * sigmoid * (1.0 + gate * (1.0 - sigmoid))
+                ).astype(BF16)
+            return carry
+
+        lax.fori_loop(0, padded // (3 * tile), units, 0)
+
+        def columns(n, carry, slot=slot):
+            at = pl.ds(pl.multiple_of(n * tile, tile), tile)
+            term[slot, :, at] = dot_nt(made[slot, 0], wg[at, :]) + dot_nt(
+                made[slot, 1], wu[at, :]
+            )
+            branch[slot, :, at] = dot_nt(made[slot, 2], wd[at, :]).astype(BF16)
+            return carry
+
+        if turn > 0:
+            sums.step(turn - 1)
+        lax.fori_loop(0, width // tile, columns, 0)
+        for copies in stores(turn, (0, 2)):
+            for copy in copies:
+                copy.start()
+    sums.total(d2)
+    sums.finish()
+    for turn in range(tp - 2, tp):
+        for copies in stores(turn):
+            for copy in copies:
+                copy.wait()
+
+
+def ff_part(dp, tp, ff, cot, n2):
+    def shape(*dims, kind=BF16):
+        return jax.ShapeDtypeStruct(dims, kind)
+
+    own_rows, width = cot.shape[1:]
+    padded = ff.shape[3]
+    vmem = pl.BlockSpec(memory_space=pltpu.VMEM)
+    anywhere = pl.BlockSpec(memory_space=ANY)
+    return pl.pallas_call(
+        functools.partial(ff_kernel, dp, tp),
+        out_shape=(
+            shape(FF_PARTS, tp * own_rows, padded),
+            shape(2, width, tp * own_rows),
+            shape(tp, own_rows, width),
+            shape(own_rows, width, kind=F32),
+        ),
+        in_specs=[anywhere] * 3,
+        out_specs=(anywhere,) * 3 + (vmem,),
+        scratch_shapes=[
+            pltpu.VMEM((width, padded), BF16),
+            pltpu.VMEM((width, padded), BF16),
+            pltpu.VMEM((width, padded), BF16),
+            pltpu.VMEM((2, own_rows, width), BF16),
+            pltpu.VMEM((2, own_rows, width), BF16),
+            pltpu.VMEM((2, FF_PARTS, own_rows, padded), BF16),
+            pltpu.VMEM((2, own_rows, width), F32),
+            pltpu.VMEM((tp - 1, own_rows, width), BF16),
+            pltpu.VMEM((2, tp - 1, own_rows, width), BF16),
+            pltpu.VMEM((2, own_rows, width), BF16),
+            pltpu.VMEM((2, 2, width, own_rows), BF16),
+            pltpu.SemaphoreType.DMA((FF_PARTS, dp)),
+            pltpu.SemaphoreType.DMA((2, 2)),
+            pltpu.SemaphoreType.DMA((2, FF_PARTS)),
+            pltpu.SemaphoreType.DMA((2, 2)),
+            pltpu.SemaphoreType.DMA((2,)),
+            pltpu.SemaphoreType.DMA((tp - 1,)),
+            pltpu.SemaphoreType.DMA((2, tp - 1)),
+        ],
+        compiler_params=pltpu.CompilerParams(
+            collective_id=3, has_side_effects=True, vmem_limit_bytes=60 << 20
+        ),
+        name="ff_part",
+    )(ff, cot, n2)
+
+
+def ff_grad_kernel(
+    dp, tp, chunk, lhs, act, mlp, out, mlp_out,
+    part, taken, held, terms, got, act_sem, send_sem, recv_sem, mlp_sem, line_send, line_recv,
+):
+    place = Place(dp, tp)
+    depth = out.shape[1]
+    group = max(1, 384 // depth)
+    tile = 256
+    per_part = act.shape[2] // chunk
+    units = [(p, k) for p in range(FF_PARTS) for k in range(per_part)]
+
+    def fetch(u):
+        p, k = units[u]
+        return pltpu.make_async_copy(
+            act.at[p, :, pl.ds(k * chunk, chunk)], taken.at[u % 2], act_sem.at[u % 2]
+        )
+
+    fetch(0).start()
+    terms_copy = pltpu.make_async_copy(mlp, terms, mlp_sem.at[0])
+    terms_copy.start()
+    place.greet(True, True)
+
+    def own_terms(turn):
+        return terms.at[line.owner(turn)]
+
+    line = LineReduce(
+        place,
+        own_terms,
+        own_terms,
+        lambda side, k: got.at[side, k],
+        lambda turn: line_send.at[turn],
+        lambda side, k: line_recv.at[side, k],
+    )
+    sums = [
+        PlaneReduce(
+            place,
+            lambda b, u=u: part.at[u % 2, b],
+            lambda s, u=u: held.at[u, s],
+            lambda s, u=u: send_sem.at[u, s],
+            lambda s, u=u: recv_sem.at[u, s],
+        )
+        for u in range(len(units))
+    ]
+    last = place.steps
+    for turn in range(len(units) + last + 1):
+        if turn < len(units):
+            u = turn
+            p, k = units[u]
+            if u + 1 < len(units):
+                fetch(u + 1).start()
+            fetch(u).wait()
+            if u >= 2:
+                sums[u - 2].wait_send(0)
+
+            def body(n, carry, u=u, p=p):
+                i, j = n // (chunk // tile), n % (chunk // tile)
+                rows = pl.ds(pl.multiple_of(i * (group * depth), 16), group * depth)
+                cols = pl.ds(pl.multiple_of(j * tile, tile), tile)
+                found = dot(lhs[p // 2, rows, :], taken[u % 2, :, cols]).astype(BF16)
+                for g in range(group):
+                    part[u % 2, i * group + g, :, cols] = found[g * depth : (g + 1) * depth]
+                return carry
+
+            lax.fori_loop(0, dp // group * (chunk // tile), body, 0)
+            sums[u].start(0)
+        if turn == 0:
+            terms_copy.wait()
+        if turn % 2 == 0 and turn // 2 < tp - 1:
+            line.step(turn // 2)
+        for level in range(last + 1):
+            u = turn - 1 - level
+            if 0 <= u < len(units):
+                p, k = units[u]
+                sums[u].absorb(
+                    level, out.at[p, :, pl.ds(k * chunk, chunk)] if level == last else None
+                )
+    line.total(mlp_out)
+    line.finish()
+    for u in range(len(units)):
+        for level in range(0 if u >= len(units) - 2 else 1, last + 1):
+            sums[u].wait_send(level)
+
+
+def ff_grads(dp, tp, lhs, act, mlp):
+    depth = lhs.shape[1] // dp
+    items, columns = act.shape[1:]
+    chunk = 768
+    count = FF_PARTS * columns // chunk
+    vmem = pl.BlockSpec(memory_space=pltpu.VMEM)
+    return pl.pallas_call(
+        functools.partial(ff_grad_kernel, dp, tp, chunk),
+        out_shape=(
+            jax.ShapeDtypeStruct((FF_PARTS, depth, columns), F32),
+            jax.ShapeDtypeStruct(mlp.shape[1:], F32),
+        ),
+        in_specs=[vmem, pl.BlockSpec(memory_space=ANY), pl.BlockSpec(memory_space=ANY)],
+        out_specs=(vmem, vmem),
+        scratch_shapes=[
+            pltpu.VMEM((2, dp, depth, chunk), BF16),
+            pltpu.VMEM((2, items, chunk), BF16),
+            pltpu.VMEM((count, dp - 1, depth, chunk), BF16),
+            pltpu.VMEM(mlp.shape, BF16),
+            pltpu.VMEM((2, tp - 1) + mlp.shape[1:], BF16),
+            pltpu.SemaphoreType.DMA((2,)),
+            pltpu.SemaphoreType.DMA((count, dp - 1)),
+            pltpu.SemaphoreType.DMA((count, dp - 1)),
+            pltpu.SemaphoreType.DMA((1,)),
+            pltpu.SemaphoreType.DMA((tp - 1,)),
+            pltpu.SemaphoreType.DMA((2, tp - 1)),
+        ],
+        compiler_params=pltpu.CompilerParams(
+            collective_id=1, has_side_effects=True, vmem_limit_bytes=56 << 20
+        ),
+        name="ff_grads",
+    )(lhs, act, mlp)
+
+
+def attn_grad_kernel(
+    dp, tp, widths, grads, kv_out, q_out, o_out,
+    held, own, line_kv, line_qo, send_sem, recv_sem, line_send, line_recv,
+):
+    place = Place(dp, tp)
+    z = place.z
+    columns = q_out.shape[1]
+    barrier = pltpu.get_barrier_semaphore()
+    for partner in place.partners + [place.sibling]:
+        pl.semaphore_signal(barrier, inc=1, device_id=place.device(partner), device_id_type=MESH)
+    for t in range(tp):
+
+        @pl.when(t != z)
+        def _():
+            pl.semaphore_signal(barrier, inc=1, device_id=(place.d, t), device_id_type=MESH)
+
+    pl.semaphore_wait(barrier, place.steps + tp)
+    starts = [sum(widths[:u]) for u in range(len(widths))]
+    count = len(widths)
+    sums = [
+        PlaneReduce(
+            place,
+            lambda b, u=u: grads.at[b, :, pl.ds(starts[u], widths[u])],
+            lambda s, u=u: held.at[u, s, :, pl.ds(0, widths[u])],
+            lambda s, u=u: send_sem.at[u, s],
+            lambda s, u=u: recv_sem.at[u, s],
+        )
+        for u in range(count)
+    ]
+
+    def line_copies(u):
+        found = []
+        for t in range(tp):
+            if u == 0:
+                src, dst = own.at[0, :, pl.ds(0, widths[0])], line_kv.at[z]
+                found.append((t, remote(
+                    src, dst, line_send.at[u, t], line_recv.at[u, z], (place.d, t)
+                )))
+            else:
+                half, kind = (u - 1) % 2, (u - 1) // 2
+                if t // 2 == half:
+                    src = own.at[u, :, pl.ds((t % 2) * columns, columns)]
+                    dst = line_qo.at[kind, z]
+                    found.append((t, remote(
+                        src, dst, line_send.at[u, t], line_recv.at[1 + kind, z], (place.d, t)
+                    )))
+        return found
+
+    last = place.steps
+    for u in range(count):
+        sums[u].start(0)
+    for turn in range(count + last):
+        for level in range(last + 1):
+            u = turn - level
+            if 0 <= u < count:
+                target = own.at[u, :, pl.ds(0, widths[u])] if level == last else None
+                sums[u].absorb(level, target)
+                if level == last:
+                    for t, copy in line_copies(u):
+
+                        @pl.when(t != z)
+                        def _():
+                            copy.start()
+
+    def arrived(ref, kind):
+        for t in range(tp):
+
+            @pl.when(t != z)
+            def _():
+                remote(
+                    ref.at[t], ref.at[t], line_send.at[0, t], line_recv.at[kind, t], (place.d, t)
+                ).wait_recv()
+
+    def total(ref, mine, out):
+        acc = mine.astype(F32)
+        for t in range(tp):
+            acc = acc + jnp.where(t != z, ref[t].astype(F32), 0.0)
+        out[...] = acc
+
+    arrived(line_kv, 0)
+    total(line_kv, own[0, :, : widths[0]], kv_out)
+    for kind, out in ((0, q_out), (1, o_out)):
+        arrived(line_qo.at[kind], 1 + kind)
+        at = pl.ds(pl.multiple_of((z % 2) * columns, 128), columns)
+        mine = own[1 + 2 * kind + z // 2, :, at]
+        total(line_qo.at[kind], mine, out)
+    for u in range(count):
+        for level in range(last + 1):
+            sums[u].wait_send(level)
+        for t, copy in line_copies(u):
+
+            @pl.when(t != z)
+            def _():
+                copy.wait_send()
+
+
+def attn_grads(dp, tp, grads, side_width):
+    depth, columns = grads.shape[1:]
+    qo_width = (columns - side_width) // 4
+    widths = (side_width,) + (qo_width,) * 4
+    own_width = 2 * qo_width // tp
+    vmem = pl.BlockSpec(memory_space=pltpu.VMEM)
+    return pl.pallas_call(
+        functools.partial(attn_grad_kernel, dp, tp, widths),
+        out_shape=(
+            jax.ShapeDtypeStruct((depth, side_width), F32),
+            jax.ShapeDtypeStruct((depth, own_width), F32),
+            jax.ShapeDtypeStruct((depth, own_width), F32),
+        ),
+        in_specs=[vmem],
+        out_specs=(vmem,) * 3,
+        scratch_shapes=[
+            pltpu.VMEM((5, dp - 1, depth, qo_width), BF16),
+            pltpu.VMEM((5, depth, qo_width), BF16),
+            pltpu.VMEM((tp, depth, side_width), BF16),
+            pltpu.VMEM((2, tp, depth, own_width), BF16),
+            pltpu.SemaphoreType.DMA((5, dp - 1)),
+            pltpu.SemaphoreType.DMA((5, dp - 1)),
+            pltpu.SemaphoreType.DMA((5, tp)),
+            pltpu.SemaphoreType.DMA((3, tp)),
+        ],
+        compiler_params=pltpu.CompilerParams(
+            collective_id=2, has_side_effects=True, vmem_limit_bytes=56 << 20
+        ),
+        name="attn_grads",
+    )(grads)
 
 
 def local(
@@ -368,102 +1122,49 @@
     padded = -(-hidden_units // 256) * 256
     ff_own = jnp.stack([gateup_weight[0], gateup_weight[1], down_weight.T])
     ff_own = jnp.pad(ff_own, ((0, 0), (0, 0), (0, padded - hidden_units)))
-    bias_rows = jnp.pad(query_bias[None, :], ((0, 15), (0, columns - query_bias.shape[0])))
-    own_kvbias = jnp.pad(key_value_bias, (0, depth - key_value_bias.shape[0]))
+    qb_count, kvb_count = query_bias.shape[0], key_value_bias.shape[0]
+    own_kvbias = jnp.pad(key_value_bias, (0, depth - kvb_count))
     side = jnp.pad(jnp.stack([first_gain, second_gain, own_kvbias], axis=1), ((0, 0), (0, 125)))
-    q_all, o_all, kv_all, ff_all, grad_rows = gather_all(
+    own_segments = lax.dynamic_slice_in_dim(segment_ids, rank * own_rows, own_rows, 0)
+    (
+        ff_all, grad_rows, second_rows, wq, wo, wkv, probs_low,
+        residual, attended, normed_own, rot_query, all_kv, cosine, sine, vectors,
+    ) = forward_part(
         dp,
         tp,
-        jnp.concatenate([query_weight, bias_rows], axis=0),
+        kvb_count,
+        qb_count,
+        inputs,
+        segment_ids[None, :],
+        own_segments[:, None],
+        query_weight,
         output_weight.T,
+        jnp.pad(query_bias[None, :], ((0, 15), (0, 128 - qb_count))),
         jnp.concatenate([key_value_weight, side], axis=1),
         ff_own,
         cotangent,
     )
-    grad_rows = grad_rows.reshape(-1, width)
     edge_q = heads_width
-    edge_kv = edge_q + kv_columns
-    edge_o = edge_kv + heads_width
-    query_full = q_all[:, :, :depth].transpose(0, 2, 1, 3).reshape(width, -1)
-    qbias_full = q_all[:, :, depth, : query_bias.shape[0]].transpose(1, 0, 2).reshape(-1)
-    out_t_weight = o_all.transpose(0, 2, 1, 3).reshape(width, -1)
-    kv_all = kv_all.reshape(width, -1)
-    qkv_weight = jnp.concatenate([query_full, kv_all[:, :kv_columns]], axis=1)
-    side = kv_all[:, kv_columns : kv_columns + 3].T.astype(F32)
-    gain_one, gain_two = side[0], side[1]
-    kvbias_full = side[2].reshape(dp, depth)[:, : key_value_bias.shape[0]].reshape(-1)
-    qbias_full = qbias_full.astype(F32)
-    gate_w = ff_all[:, 0].reshape(width, padded)
-    up_w = ff_all[:, 1].reshape(width, padded)
-    down_t = ff_all[:, 2].reshape(width, padded)
-
+    half_kv = kv_columns // 2
+    items = all_kv.shape[0]
+    qkv_weight = jnp.concatenate(
+        [wq.transpose(1, 0, 2).reshape(width, -1), wkv[:, :kv_columns]], axis=1
+    )
+    out_t_weight = wo.transpose(1, 0, 2).reshape(width, -1)
+    gain_one, gain_two = vectors[0], vectors[1]
     own_inputs = inputs.astype(F32)
-    normed_own = (own_inputs * rms_scale(own_inputs) * gain_one).astype(BF16)
-    placed, freqs = rope_tables(segment_ids, head)
-    begin = rank * own_rows
-    own_placed = lax.dynamic_slice_in_dim(placed, begin, own_rows, 0)
-    own_segments = lax.dynamic_slice_in_dim(segment_ids, begin, own_rows, 0)
-    angles = own_placed[:, None] * freqs[None, :]
-    cosine, sine = jnp.cos(angles)[:, None, :], jnp.sin(angles)[:, None, :]
-
-    qkv = dot(normed_own, qkv_weight) + jnp.concatenate([qbias_full, kvbias_full])
-    half_kv = kv_columns // 2
-    rot = apply_rotation(
-        qkv[:, : edge_q + half_kv].reshape(own_rows, -1, head), cosine, sine
-    ).astype(BF16)
-    rot_query = rot[:, :QUERY_HEADS]
-    own_kv = jnp.concatenate(
-        [rot[:, QUERY_HEADS:].reshape(own_rows, half_kv), qkv[:, edge_q + half_kv :].astype(BF16)],
-        axis=1,
-    )
-    all_kv = lax.all_gather(own_kv, "tensor", axis=0, tiled=True)
-    items = all_kv.shape[0]
-    all_kv = all_kv.reshape(items, 2, KEYVALUE_HEADS, head)
+    cosine, sine = cosine[:, None, : head // 2], sine[:, None, head // 2 :]
+    valid = jnp.arange(items)[:, None] < (rank + 1) * own_rows
+    all_kv = jnp.where(valid, all_kv, 0).reshape(items, 2, KEYVALUE_HEADS, head)
     keys, value_rows = all_kv[:, 0], all_kv[:, 1]
     grouped = rot_query.reshape(own_rows, KEYVALUE_HEADS, REPEAT, head)
-
-    index = jnp.arange(items, dtype=jnp.int32)
-    own_index = begin + jnp.arange(own_rows, dtype=jnp.int32)
-    allowed = (own_segments[:, None] == segment_ids[None, :]) & (
-        index[None, :] <= own_index[:, None]
-    )
-    scores = jnp.einsum("qgrd,kgd->grqk", grouped, keys, preferred_element_type=F32) * scale
-    scores = jnp.where(allowed[None, None], scores, NEGATIVE)
-    top = jnp.max(scores, axis=-1, keepdims=True)
-    weights = jnp.exp(scores - top)
-    total = jnp.sum(weights, axis=-1, keepdims=True)
-    probs = weights / total
-    probs_low = probs.astype(BF16)
-    attended = (
-        jnp.einsum("grqk,kgd->qgrd", probs_low, value_rows, preferred_element_type=F32)
-        .reshape(own_rows, -1)
-        .astype(BF16)
-    )
-    residual = own_inputs + dot_nt(attended, out_t_weight)
-    second_own = (residual * rms_scale(residual) * gain_two).astype(BF16)
-    second_rows = lax.all_gather(second_own, "tensor", axis=0, tiled=True)
-
-    gate = dot(second_rows, gate_w)
-    upper = dot(second_rows, up_w)
-    sigmoid = jax.nn.sigmoid(gate)
-    swish = gate * sigmoid
-    hidden = (swish * upper).astype(BF16)
-    d_hidden = dot(grad_rows, down_t)
-    d_gate = (d_hidden * upper * sigmoid * (1.0 + gate * (1.0 - sigmoid))).astype(BF16)
-    d_up = (d_hidden * swish).astype(BF16)
-    second_terms = dot_nt(d_gate, gate_w) + dot_nt(d_up, up_w)
-    d_second = lax.psum_scatter(
-        second_terms.astype(BF16), "tensor", scatter_dimension=0, tiled=True
-    ).astype(F32)
-    down_grad = dot_tn(grad_rows, hidden).astype(BF16)
-    down_sh = lax.psum_scatter(down_grad, "dp", scatter_dimension=0, tiled=True)
-    gate_grad = dot_tn(second_rows, d_gate).astype(BF16)
-    gate_sh = lax.psum_scatter(gate_grad, "dp", scatter_dimension=0, tiled=True)
-    up_grad = dot_tn(second_rows, d_up).astype(BF16)
-    up_sh = lax.psum_scatter(up_grad, "dp", scatter_dimension=0, tiled=True)
-    mlp_terms = dot_nt(hidden, down_t).astype(BF16)
-    mlp_own = lax.psum_scatter(mlp_terms, "tensor", scatter_dimension=0, tiled=True)
-    output = (residual + mlp_own.astype(F32)).astype(BF16)
+    probs_low = jnp.where(valid.T[None], probs_low, 0)
+    probs_low = probs_low.reshape(KEYVALUE_HEADS, REPEAT, own_rows, items)
+    probs = probs_low.astype(F32)
+
+    act, lhs, mlp_terms, d_second = ff_part(dp, tp, ff_all, grad_rows, second_rows)
+    ff_sh, mlp_own = ff_grads(dp, tp, lhs, act, mlp_terms)
+    output = (residual + mlp_own).astype(BF16)
 
     residual_part, gain_two_grad = norm_back(residual, gain_two, d_second)
     d_residual = cotangent.astype(F32) + residual_part
@@ -504,33 +1205,25 @@
     kvb = jnp.pad(bias_grad[edge_q:].reshape(dp, -1), ((0, 0), (0, depth - kv_columns // dp)))
     side_grad = jnp.stack([gain_one_grad, gain_two_grad, qb, kvb.reshape(-1)], axis=1)
     side_grad = jnp.pad(side_grad, ((0, 0), (0, 124)))
-    attn_grad = jnp.concatenate([qkv_grad, out_grad, side_grad], axis=1).astype(BF16)
-    attn_sh = lax.psum_scatter(attn_grad, "dp", scatter_dimension=0, tiled=True)
-    q_part = attn_sh[:, :edge_q].reshape(depth, tp, columns).transpose(1, 0, 2)
-    o_part = attn_sh[:, edge_kv:edge_o].reshape(depth, tp, columns).transpose(1, 0, 2)
-    qo = lax.psum_scatter(
-        jnp.concatenate([q_part, o_part], axis=1).reshape(tp * 2 * depth, columns),
-        "tensor",
-        scatter_dimension=0,
-        tiled=True,
-    ).astype(F32)
-    rest = lax.psum(
-        jnp.concatenate([attn_sh[:, edge_q:edge_kv], attn_sh[:, edge_o:]], axis=1), "tensor"
-    ).astype(F32)
+    attn_grad = jnp.concatenate(
+        [qkv_grad[:, edge_q:], side_grad, qkv_grad[:, :edge_q], out_grad], axis=1
+    ).astype(BF16)
+    rest, q_sh, o_sh = attn_grads(
+        dp, tp, attn_grad.reshape(dp, depth, -1), kv_columns + side_grad.shape[1]
+    )
     side_sh = rest[:, kv_columns : kv_columns + 4].T
-    qb_count = query_bias.shape[0]
     return (
         output,
         input_grad,
         side_sh[0],
-        qo[:depth],
+        q_sh,
         lax.dynamic_slice_in_dim(side_sh[2], rank * qb_count, qb_count, 0),
         rest[:, :kv_columns],
         side_sh[3][: kv_columns // dp],
-        qo[depth:].T,
+        o_sh.T,
         side_sh[1],
-        jnp.stack([gate_sh[:, :hidden_units], up_sh[:, :hidden_units]]).astype(F32),
-        down_sh[:, :hidden_units].T.astype(F32),
+        ff_sh[:2, :, :hidden_units],
+        ff_sh[2, :, :hidden_units].T,
     )
 
 

time: 981 us -> 639 us (0.65)
  waiting for transfers between devices: 479 us -> 22.6 us
  Pallas kernels: 192 us -> 479 us
  matrix products: 171 us -> 22.7 us
  local copies, waits for them, and re-layouts: 70.4 us -> 58.8 us
    reduce_scatter x7 -> x0, waiting for transfers between devices: 374 us -> none  [the longest x1 88.5 us: local(): attn_sh = lax.psum_scatter(attn_grad, 'dp', scatter_dimension=0, tiled=True)]
    pallas_call x1 -> x4, Pallas kernels: 192 us -> 479 us  [the longest x1 195 us: forward_part(): pl.pallas_call(functools.partial(forward_kernel, dp, tp, kvb_count, qb_co...]
    all_gather x2 -> x0, waiting for transfers between devices: 65 us -> none  [the longest x1 46.5 us: local(): second_rows = lax.all_gather(second_own, 'tensor', axis=0, tiled=True)]
    dot_general x5 -> x1, matrix products: 50.3 us -> 1.41 us  [dot(): return jnp.dot(left, right, preferred_element_type=F32)]
    dot_general x5 -> x2, matrix products: 45.3 us -> 5.46 us  [dot_tn(): lax.dot_general(left, right, (((0,), (0,)), ((), ())), preferred_element_...]
    dot_general x5 -> x1, matrix products: 44.5 us -> 6.99 us  [dot_nt(): lax.dot_general(left, right, (((1,), (1,)), ((), ())), preferred_element_...]
    psum x1 -> x0, waiting for transfers between devices: 34.6 us -> none  [local(): lax.psum(jnp.concatenate([attn_sh[:, edge_q:edge_kv], attn_sh[:, edge_o:]...]
    reduce_scatter x1, waiting for transfers between devices: 5 us -> 22.6 us  [local(): lax.psum_scatter(jnp.concatenate([d_keys.reshape(items, -1), d_values.res...]
  transfers between devices with their start and end apart: 11 -> 1, of which waited for: 11 -> 1; matrix products, arithmetic and copies ran while one was open for 13% -> 4% of each run, Pallas kernels for 0% -> 0%
where the time goes in v2:
time: 639 us; the launch traced here: 629 us
  Pallas kernels  479 us (75%)
  local copies, waits for them, and re-layouts  58.8 us (9%)
  other arithmetic  31.4 us (5%)
  matrix products  22.7 us (4%)
  waiting for transfers between devices  22.6 us (4%)
  between operations  15 us (2%)
    pallas_call x1, Pallas kernels, forward_part(): pl.pallas_call(functools.partial(forward_kernel, dp, tp, kvb_count, qb_co...  195 us
    pallas_call x1, Pallas kernels, ff_grads(): pl.pallas_call(functools.partial(ff_grad_kernel, dp, tp, chunk), out_shap...  115 us
    pallas_call x1, Pallas kernels, ff_part(): pl.pallas_call(functools.partial(ff_kernel, dp, tp), out_shape=(shape(FF_...  92.4 us
    pallas_call x1, Pallas kernels, attn_grads(): pl.pallas_call(functools.partial(attn_grad_kernel, dp, tp, widths), out_s...  76.2 us
    reduce_scatter x1, waiting for transfers between devices, local(): lax.psum_scatter(jnp.concatenate([d_keys.reshape(items, -1), d_values.res...  22.6 us
  transfers between devices with their start and end apart: 1, of which 1 were waited for; matrix products, arithmetic and copies ran while one was open for 4% of the time, Pallas kernels for 0%

profile of v2, /device:TPU:24, one launch (start us, length us, event | category | flops | bytes accessed | tf_op | source)
XLA Modules:
  0.0 629.3 jit_solution(5362769193419001257)
XLA Ops:
  12.2 3.5 fusion.9.ff
  16.4 194.9 %forward_part.1 = (bf16[8,3,192,2304]{3,2,1,0:T(8,128)(2,1)}, bf16[4,256,1536]{2,1,0:T(8,128)(2,1)}, bf16[4,256,1536]{2,1,0:T(8,128)(2,1)}, bf16[4,1536,384]{2,1...) custom-call(bf16[256,1536]{1,0:T(8,128)(2,1)} %x.13, ...), custom_call_target="tpu_custom_call" | custom-call | tf_op jit(solution)/shard_map/forward_part/pallas_call | solution.py:497
  213.9 92.4 %ff_part.1 = (bf16[3,1024,2304]{2,1,0:T(8,128)(2,1)}, bf16[2,1536,1024]{2,1,0:T(8,128)(2,1)}, bf16[4,256,1536]{2,1,0:T(8,128)(2,1)}, f32[256,1536]{1,0:T(8,128)}) custom-call(bf16[8,3,192,2304]{3,2,1,0:T(8,128)(2,1)} %get-tuple-element.36.ff, bf16[4,256,1536]{2,1,0:T(8,128)(2,1)} %get-tuple-element.37.cot, bf16[4,256,1536]{2,1,0:T(8,128)(2,1)} %get-tuple-element.38.n2), custom_call_target="tpu_custom_call" | custom-call | tf_op jit(solution)/shard_map/ff_part/pallas_call | solution.py:813
  306.3 1.9 multiply_reduce_fusion
  308.2 6.6 %copy.74 = bf16[1536,4,384]{0,2,1:T(8,128)(2,1)} copy(bf16[1536,4,384]{2,0,1:T(8,128)(2,1)} %bitcast.96) | data formatting | bytes 9437184 | tf_op jit(solution)/shard_map/transpose | solution.py:1153
  314.9 115.2 %ff_grads.1 = (f32[3,192,2304]{2,1,0:T(8,128)}, f32[256,1536]{1,0:T(8,128)}) custom-call(bf16[2,1536,1024]{2,1,0:T(8,128)(2,1)} %get-tuple-element.39.lhs, bf16[3,1024,2304]{2,1,0:T(8,128)(2,1)} %get-tuple-element.40.act, bf16[4,256,1536]{2,1,0:T(8,128)(2,1)} %get-tuple-element.41.mlp), custom_call_target="tpu_custom_call" | custom-call | tf_op jit(solution)/shard_map/ff_grads/pallas_call | solution.py:939
  430.1 2.9 multiply_add_fusion
  435.9 5.9 broadcast_select_fusion
  441.8 8.8 %copy.72 = bf16[2,6,256,1024]{2,3,1,0:T(8,128)(2,1)} copy(bf16[2,6,256,1024]{3,2,1,0:T(8,128)(2,1)} %bitcast.78) | data formatting | bytes 12582912 | tf_op jit(solution)/shard_map/reshape | solution.py:1162
  452.6 2.4 copy.78
  455.0 3.9 fusion.21
  460.8 2.2 fusion.1
  463.1 2.1 fusion.20
  469.7 6.8 %copy.82 = bf16[1536,4,384]{0,2,1:T(8,128)(2,1)} copy(bf16[1536,4,384]{2,0,1:T(8,128)(2,1)} %bitcast.94) | data formatting | bytes 9437184 | tf_op jit(solution)/shard_map/transpose | solution.py:1151
  476.7 1.8 copy.83
  478.5 4.2 slice.113
  483.0 3.6 convolution_convert_fusion.1
  487.6 2.8 slice_bitcast_fusion
  490.5 22.6 %reduce-scatter.2.cloned.1.call-done = bf16[256,512]{0,1:T(8,128)(2,1)} async-done(((bf16[1024,512]{0,1:T(8,128)(2,1)}), bf16[256,512]{0,1:T(8,128)(2,1)}) %reduce-scatter.2.cloned.1.call-update) | async-done | bytes 262160 | tf_op jit(solution)/shard_map/reduce_scatter | solution.py:1180
  515.4 1.9 convolution_convert_fusion
  517.3 3.0 slice.124
  521.8 7.0 %fusion.18 = (bf16[1536]{0:T(1024)(128)(2,1)S(1)}, f32[256]{0:T(256)}, f32[256,1536]{1,0:T(8,128)}) fusion(bf16[256,1536]{1,0:T(8,128)(2,1)} %x.13, f32[256]{0:T(256)S(1)} %add_rsqrt_fusion, f32[1536]{0:T(1024)S(1)} %get-tuple-element.65, bf16[1536,512]{0,1:T(8,128)(2,1)} %copy.83, bf16[1536,1536]{0,1:T(8,128)(2,1)} %bitcast.95, ...), kind=kOutput, calls=%fused_computation.32 | convolution fusion | flops 1628043520 | bytes 9710592 | tf_op jit(solution)/shard_map/dot_general | solution.py:66
  529.2 9.1 %pad_maximum_fusion.grads = bf16[8,192,3712]{2,1,0:T(8,128)(2,1)} fusion(bf16[8,192,1536]{2,1,0:T(8,128)(2,1)} %bitcast.85, bf16[8,192,1536]{2,1,0:T(8,128)(2,1)} %bitcast.88, bf16[8,192,128]{2,1,0:T(8,128)(2,1)S(1)} %bitcast.100, bf16[8,192,512]{2,1,0:T(8,128)(2,1)S(1)} %bitcast.84), kind=kLoop, calls=%fused_computation.6 | loop fusion | flops 45613056 | bytes 22806528 | tf_op jit(solution)/shard_map/concatenate | solution.py:1208
  538.3 76.2 %attn_grads.1 = (f32[192,640]{1,0:T(8,128)}, f32[192,384]{1,0:T(8,128)}, f32[192,384]{1,0:T(8,128)}) custom-call(bf16[8,192,3712]{2,1,0:T(8,128)(2,1)} %pad_maximum_fusion.grads), custom_call_target="tpu_custom_call" | custom-call | tf_op jit(solution)/shard_map/attn_grads/pallas_call | solution.py:1069
  (128 shorter events, 32.6 us)
Async XLA Ops:
  7.2 505.9 %reduce-scatter.2.cloned.1.call-start = ((), (), s32[]{:S(2)}) async-start(), calls=%async_computation.1 | async-start | bytes 1310720 | tf_op jit(solution)/shard_map/reduce_scatter | solution.py:1180
  213.9 307.9 %copy-start.26 = (f32[1536]{0:T(1024)}, f32[1536]{0:T(1024)S(1)}, u32[]{:S(2)}) copy-start(f32[1536]{0:T(1024)S(1)} %get-tuple-element.65) | copy-start | bytes 18436
  213.9 92.4 %copy-start.4 = (f32[256,1536]{1,0:T(8,128)S(1)}, f32[256,1536]{1,0:T(8,128)}, u32[]{:S(2)}) copy-start(f32[256,1536]{1,0:T(8,128)} %get-tuple-element.35) | copy-start | bytes 4718596
  314.9 115.2 %copy-start.8 = (f32[256,1536]{1,0:T(8,128)S(1)}, f32[256,1536]{1,0:T(8,128)}, u32[]{:S(2)}) copy-start(f32[256,1536]{1,0:T(8,128)} %get-tuple-element.43) | copy-start | bytes 4718596
  314.9 115.3 %copy-start.10 = (bf16[256,1536]{1,0:T(8,128)(2,1)S(1)}, bf16[256,1536]{1,0:T(8,128)(2,1)}, u32[]{:S(2)}) copy-start(bf16[256,1536]{1,0:T(8,128)(2,1)} %cot.1) | copy-start | bytes 2359300
  430.1 4.1 copy-start.9
  441.8 8.8 %copy-start.17 = (bf16[1024,512]{1,0:T(8,128)(2,1)S(1)}, bf16[1024,512]{1,0:T(8,128)(2,1)}, u32[]{:S(2)}) copy-start(bf16[1024,512]{1,0:T(8,128)(2,1)} %get-tuple-element.45) | copy-start | bytes 3145732
  452.6 6.4 %slice-start = ((s8[6291456]{0:T(1024)(128)(4,1)}), s8[2097152]{0:T(1024)(128)(4,1)S(1)}, s32[]{:S(2)}) async-start(s8[6291456]{0:T(1024)(128)(4,1)} %bitcast.80), calls=%async_computation.2 | async-start | bytes 4194304
  455.0 4.0 slice-start.1
  469.7 6.8 %copy-start.16 = (bf16[1536,640]{1,0:T(8,128)(2,1)S(1)}, bf16[1536,640]{1,0:T(8,128)(2,1)}, u32[]{:S(2)}) copy-start(bf16[1536,640]{1,0:T(8,128)(2,1)} %get-tuple-element.52) | copy-start | bytes 5898244
  478.5 4.2 copy-start.6
  478.5 4.4 copy-start.3
  478.5 4.4 copy-start.18
  482.7 3.9 slice-start.2
  483.0 3.6 slice-start.3
  487.6 26.5 %copy-start.21 = (f32[256,64]{0,1:T(8,128)S(1)}, f32[256,64]{0,1:T(8,128)}, u32[]{:S(2)}) copy-start(f32[256,64]{0,1:T(8,128)} %copy.81) | copy-start | bytes 196612
  487.6 26.5 %copy-start.22 = (f32[256,64]{0,1:T(8,128)S(1)}, f32[256,64]{0,1:T(8,128)}, u32[]{:S(2)}) copy-start(f32[256,64]{0,1:T(8,128)} %copy.80) | copy-start | bytes 196612
  517.3 4.1 copy-start.1
  521.8 7.4 %slice-start.4 = ((bf16[1536,2048]{1,0:T(8,128)(2,1)}), bf16[1536,512]{1,0:T(8,128)(2,1)S(1)}, s32[]{:S(2)}) async-start(bf16[1536,2048]{1,0:T(8,128)(2,1)} %copy-done.1), calls=%async_computation.6 | async-start | bytes 3145728 | tf_op jit(solution)/shard_map/slice | solution.py:1209
  538.2 80.4 %copy-start.28 = (f32[256]{0:T(256)S(1)}, f32[256]{0:T(256)}, u32[]{:S(2)}) copy-start(f32[256]{0:T(256)} %get-tuple-element.62) | copy-start | bytes 3076
  538.2 81.0 %copy-start.7 = (bf16[256,1536]{1,0:T(8,128)(2,1)S(1)}, bf16[256,1536]{1,0:T(8,128)(2,1)}, u32[]{:S(2)}) copy-start(bf16[256,1536]{1,0:T(8,128)(2,1)} %x.13) | copy-start | bytes 2359300
  538.2 81.0 %copy-start.14 = (f32[256,1536]{1,0:T(8,128)S(1)}, f32[256,1536]{1,0:T(8,128)}, u32[]{:S(2)}) copy-start(f32[256,1536]{1,0:T(8,128)} %get-tuple-element.78) | copy-start | bytes 4718596
  538.2 81.0 %copy-start.27 = (f32[1536]{0:T(1024)S(1)}, f32[1536]{0:T(1024)}, u32[]{:S(2)}) copy-start(f32[1536]{0:T(1024)} %copy-done.26) | copy-start | bytes 18436
  616.2 4.4 copy-start.20
  (11 other events, 23.3 us)
Sparse Core Ops, SparseCore 0:
  466.9 46.0 reduce-scatter.1

commit v3 on v2

--- a/solution.py
+++ b/solution.py
@@ -258,7 +258,7 @@
     x, seg_row, seg_col, zq, zo, zb, kvs, ff, cot,
     ff_out, cot_out, n2_out, wq_out, wo_out, wkv_out, p_out,
     res, att, n1, q, kv, cosine, sine, vectors,
-    wq, wo, wkv, wb, spread, mask, probs, n2, n2_own,
+    wq, wo, wkv, wb, spread, mask, probs, n2,
     plane_send, plane_recv, line_send, line_recv, local_sem, probs_sem,
 ):
     place = Place(dp, tp)
@@ -359,17 +359,17 @@
     pick_row = lax.broadcasted_iota(jnp.int32, (16, 128), 0)
     pick_col = lax.broadcasted_iota(jnp.int32, (16, 128), 1)
     pick = jnp.where(pick_row == pick_col, 1.0, 0.0).astype(BF16)
-    rows16 = dot_nt(pick, wkv[:, kv_columns:])
-    vectors[...] = rows16
+    vector_rows = dot_nt(pick, wkv[:, kv_columns:])
+    vectors[...] = vector_rows
     block_row = lax.broadcasted_iota(jnp.int32, (depth, kv_columns), 0)
     block_col = lax.broadcasted_iota(jnp.int32, (depth, kv_columns), 1)
     for b in range(dp):
         hit = (block_row < kvb_count) & (block_col == block_row + b * kvb_count)
         spread[b * depth : (b + 1) * depth, :] = jnp.where(hit, 1.0, 0.0).astype(BF16)
-    kv_bias = dot(rows16.astype(BF16), spread[...])[2:3, :]
+    kv_bias = dot(vector_rows.astype(BF16), spread[...])[2:3, :]
 
     xs = x[...].astype(F32)
-    n1[...] = (xs * rms_scale(xs) * rows16[0:1, :]).astype(BF16)
+    n1[...] = (xs * rms_scale(xs) * vector_rows[0:1, :]).astype(BF16)
     kv_rows = dot(n1[...], wkv[:, :kv_columns]) + kv_bias
     at = pl.ds(pl.multiple_of(begin, 16), own_rows)
     for h in range(KEYVALUE_HEADS):
@@ -524,7 +524,6 @@
             pltpu.VMEM((own_rows, items), F32),
             pltpu.VMEM((QUERY_HEADS, own_rows, items), BF16),
             pltpu.VMEM((own_rows, width), BF16),
-            pltpu.VMEM((16, 128), BF16),
             pltpu.SemaphoreType.DMA((7, dp)),
             pltpu.SemaphoreType.DMA((7, dp)),
             pltpu.SemaphoreType.DMA((6, 2, tp)),
@@ -847,16 +846,69 @@
     )(ff, cot, n2)
 
 
-def ff_grad_kernel(
-    dp, tp, chunk, lhs, act, mlp, out, mlp_out,
-    part, taken, held, terms, got, act_sem, send_sem, recv_sem, mlp_sem, line_send, line_recv,
+class DownReduce:
+    def __init__(self, place, term, got, send, recv):
+        self.place, self.term, self.got, self.send, self.recv = place, term, got, send, recv
+
+    def copy(self, distance):
+        return remote(
+            self.term(self.place.z - distance),
+            self.got(distance - 1),
+            self.send(distance),
+            self.recv(distance - 1),
+            self.place.beside(-1),
+        )
+
+    def take(self, distance, out):
+        place = self.place
+
+        @pl.when(place.z < place.tp - 1)
+        def _():
+            ref = self.got(distance)
+            remote(
+                ref, ref, self.send(distance), self.recv(distance), place.beside(0)
+            ).wait_recv()
+            add_into(out, ref, out)
+
+    def step(self, distance):
+        place = self.place
+
+        @pl.when(place.z >= distance)
+        def _():
+            if distance < place.tp - 1:
+                self.take(distance, self.term(place.z - distance))
+            self.copy(distance).start()
+
+    def finish(self):
+        for distance in range(1, self.place.tp):
+
+            @pl.when(self.place.z >= distance)
+            def _():
+                self.copy(distance).wait_send()
+
+
+def backward_kernel(
+    dp, tp, chunk,
+    res, vectors, att, q, kv, cosine, sine, d2, cot, x, lhs, act, mlp, probs, wo, wq, wkv,
+    out, mlp_sent, mlp_got, d_branch, d_qkv, output, input_grad, vector_grads,
+    part, taken, held, left, block, stage, weight, kv_weight, prob, d_att, d_kv, d_kv_low, kv_got,
+    acc, wide, own_bf, d_res,
+    act_sem, send_sem, recv_sem, left_sem, stage_sem, line_send, line_recv, out_sem, weight_sem,
+    prob_sem, kv_send, kv_recv, in_sem,
 ):
     place = Place(dp, tp)
-    depth = out.shape[1]
+    z = place.z
+    own_rows, width = res.shape
+    depth = width // dp
     group = max(1, 384 // depth)
     tile = 256
+    head = HEAD_DIMENSION
+    scale = 1.0 / math.sqrt(head)
+    columns = wq.shape[2]
+    heads_width = tp * columns
+    half_kv = KEYVALUE_HEADS * head
     per_part = act.shape[2] // chunk
-    units = [(p, k) for p in range(FF_PARTS) for k in range(per_part)]
+    units = [(p, k) for p in (2, 0, 1) for k in range(per_part)]
 
     def fetch(u):
         p, k = units[u]
@@ -864,22 +916,213 @@
             act.at[p, :, pl.ds(k * chunk, chunk)], taken.at[u % 2], act_sem.at[u % 2]
         )
 
+    def fetch_left(k):
+        return pltpu.make_async_copy(lhs.at[k], left, left_sem.at[0])
+
+    def fetch_weight(n):
+        source = wo if n < tp else wq
+        return pltpu.make_async_copy(source.at[n % tp], weight.at[n % 2], weight_sem.at[n % 2])
+
+    def fetch_probs(h, slot):
+        return pltpu.make_async_copy(probs.at[h], prob.at[slot], prob_sem.at[slot])
+
+    d2_copy = pltpu.make_async_copy(d2, wide, in_sem.at[0])
+    cot_copy = pltpu.make_async_copy(cot, own_bf, in_sem.at[1])
+    x_copy = pltpu.make_async_copy(x, own_bf, in_sem.at[2])
+    kv_weight_copy = pltpu.make_async_copy(
+        wkv.at[:, pl.ds(0, 2 * half_kv)], kv_weight, in_sem.at[3]
+    )
+    fetch_left(1).start()
     fetch(0).start()
-    terms_copy = pltpu.make_async_copy(mlp, terms, mlp_sem.at[0])
-    terms_copy.start()
+    for copy in (d2_copy, cot_copy, fetch_weight(0), fetch_weight(1), kv_weight_copy):
+        copy.start()
+    for h in range(2):
+        fetch_probs(h, h).start()
     place.greet(True, True)
-
-    def own_terms(turn):
-        return terms.at[line.owner(turn)]
 
     line = LineReduce(
         place,
-        own_terms,
-        own_terms,
-        lambda side, k: got.at[side, k],
+        None,
+        lambda turn: mlp_sent.at[turn],
+        lambda side, k: mlp_got.at[side, k],
         lambda turn: line_send.at[turn],
         lambda side, k: line_recv.at[side, k],
     )
+
+    def load_term(turn):
+        return pltpu.make_async_copy(mlp.at[line.owner(turn)], stage.at[0], stage_sem.at[0])
+
+    def load_got(side, distance):
+        return pltpu.make_async_copy(mlp_got.at[side, distance], stage.at[1], stage_sem.at[1])
+
+    def line_step(turn):
+        side, offset, distance = line.way(turn)
+        load_term(turn).wait()
+
+        @pl.when(place.has(-offset))
+        def _():
+            line.arrival(side, distance).wait_recv()
+            load_got(side, distance).start()
+            load_got(side, distance).wait()
+            add_into(stage.at[0], stage.at[1], stage.at[0])
+
+        store = pltpu.make_async_copy(stage.at[0], mlp_sent.at[turn], stage_sem.at[0])
+        store.start()
+        store.wait()
+        line.copy(turn).start()
+        load_term(turn + 1).start()
+
+    def line_total():
+        load_term(tp - 1).wait()
+        add_into(res, stage.at[0], d_res)
+        for side, offset in ((0, -1), (1, 1)):
+
+            @pl.when(place.has(offset))
+            def _():
+                line.arrival(side, 0).wait_recv()
+                load_got(side, 0).start()
+                load_got(side, 0).wait()
+                add_into(d_res, stage.at[1], d_res)
+
+        copy_into(d_res, output)
+
+    load_term(0).start()
+    down = DownReduce(
+        place,
+        lambda r: d_kv_low.at[pl.ds(pl.multiple_of(r * own_rows, 16), own_rows)],
+        lambda k: kv_got.at[k],
+        lambda k: kv_send.at[k],
+        lambda k: kv_recv.at[k],
+    )
+
+    def second_norm():
+        d2_copy.wait()
+        cot_copy.wait()
+        values, grad = res[...], wide[...]
+        s = rms_scale(values)
+        normed = values * s
+        weighted = grad * vectors[1:2, :]
+        inner = jnp.mean(weighted * normed, axis=1, keepdims=True)
+        found = own_bf[...].astype(F32) + s * (weighted - normed * inner)
+        d_res[...] = found
+        d_branch[...] = found.astype(BF16)
+        vector_grads[...] = jnp.zeros_like(vector_grads)
+        vector_grads[1:2, :] = jnp.sum(grad * normed, axis=0, keepdims=True)
+        x_copy.start()
+        d_kv[...] = jnp.zeros_like(d_kv)
+
+    def attended_grad(ts):
+        for t in ts:
+            fetch_weight(t).wait()
+            d_att[:, t * columns : (t + 1) * columns] = dot(d_branch[...], weight[t % 2]).astype(
+                BF16
+            )
+            fetch_weight(t + 2).start()
+
+    def some_heads(begin, end):
+        def one_head(h, carry):
+            slot = h % 2
+            at = pl.ds(pl.multiple_of(h * head, head), head)
+            shared = h // REPEAT
+            key_at = pl.ds(pl.multiple_of(shared * head, head), head)
+            value_at = pl.ds(pl.multiple_of(half_kv + shared * head, head), head)
+            fetch_probs(h, slot).wait()
+            d_out = d_att[:, at]
+            inner = jnp.sum(
+                d_out.astype(F32) * att[:, at].astype(F32), axis=1, keepdims=True
+            )
+            acc[...] = jnp.zeros_like(acc)
+
+            def one_block(j, carry):
+                rows = pl.ds(pl.multiple_of(j * own_rows, 256), own_rows)
+                low = prob[slot, :, rows]
+                d_probs = dot_nt(d_out, kv[rows, value_at])
+                d_scores = (low.astype(F32) * (scale * (d_probs - inner))).astype(BF16)
+                acc[...] += dot(d_scores, kv[rows, key_at])
+                d_kv[rows, key_at] += dot_tn(d_scores, q[:, at])
+                d_kv[rows, value_at] += dot_tn(low, d_out)
+                return carry
+
+            lax.fori_loop(0, z + 1, one_block, 0)
+            d_qkv[:, at] = turned(acc[...], cosine[...], -sine[...]).astype(BF16)
+
+            @pl.when(h + 2 < QUERY_HEADS)
+            def _():
+                fetch_probs(h + 2, slot).start()
+
+            return carry
+
+        lax.fori_loop(begin, end, one_head, 0)
+
+    def send_kv():
+        def body(j, carry):
+            rows = pl.ds(pl.multiple_of(j * own_rows, 256), own_rows)
+            d_kv_low[rows, :] = d_kv[rows, :].astype(BF16)
+            return carry
+
+        lax.fori_loop(0, z + 1, body, 0)
+        down.step(tp - 1)
+        for distance in range(tp - 2, 0, -1):
+            down.step(distance)
+
+    def normed_grad(ts):
+        for t in ts:
+            fetch_weight(tp + t).wait()
+            for j in range(width // 512):
+                cut = slice(j * 512, (j + 1) * 512)
+                found = dot_nt(
+                    d_qkv[:, t * columns : (t + 1) * columns], weight[(tp + t) % 2, cut, :]
+                )
+                wide[:, cut] = found + wide[:, cut] if t else found
+            if t + 2 < tp:
+                fetch_weight(tp + t + 2).start()
+
+    def first_norm():
+        mine = pl.ds(pl.multiple_of(z * own_rows, 16), own_rows)
+        down.take(0, d_kv.at[mine])
+        for h in range(KEYVALUE_HEADS):
+            cut = slice(h * head, (h + 1) * head)
+            d_qkv[:, heads_width + h * head : heads_width + (h + 1) * head] = turned(
+                d_kv[mine, cut], cosine[...], -sine[...]
+            ).astype(BF16)
+        d_qkv[:, heads_width + half_kv :] = d_kv[mine, half_kv:].astype(BF16)
+        kv_weight_copy.wait()
+        for j in range(width // 512):
+            cut = slice(j * 512, (j + 1) * 512)
+            wide[:, cut] += dot_nt(d_qkv[:, heads_width:], kv_weight[cut, :])
+        x_copy.wait()
+        values, grad = own_bf[...].astype(F32), wide[...]
+        s = rms_scale(values)
+        normed = values * s
+        weighted = grad * vectors[0:1, :]
+        inner = jnp.mean(weighted * normed, axis=1, keepdims=True)
+        input_grad[...] = (d_res[...] + s * (weighted - normed * inner)).astype(BF16)
+        vector_grads[0:1, :] = jnp.sum(grad * normed, axis=0, keepdims=True)
+        sums_of = jnp.sum(d_qkv[...].astype(F32), axis=0, keepdims=True)
+        vector_grads[2:3, :] = sums_of[:, :heads_width]
+        vector_grads[3:4, : 2 * half_kv] = sums_of[:, heads_width:]
+
+    per = QUERY_HEADS // tp
+    pieces = [
+        [second_norm, lambda: attended_grad(range(tp))],
+        [lambda: some_heads(0, 2), lambda: line_step(0)],
+        [lambda: some_heads(2, 4)],
+        [lambda: some_heads(4, 6)],
+        [lambda: some_heads(6, 8), lambda: line_step(1)],
+        [lambda: some_heads(8, 10)],
+        [lambda: some_heads(10, 12), send_kv],
+        [lambda: normed_grad(range(tp)), lambda: line_step(2)],
+        [],
+        [first_norm],
+        [line_total],
+    ]
+
+    def stored(u):
+        p, k = units[u]
+        return pltpu.make_async_copy(
+            block.at[u % 2], out.at[p, :, pl.ds(k * chunk, chunk)], out_sem.at[u % 2]
+        )
+
     sums = [
         PlaneReduce(
             place,
@@ -891,86 +1134,132 @@
         for u in range(len(units))
     ]
     last = place.steps
-    for turn in range(len(units) + last + 1):
+    fetch_left(1).wait()
+    for turn in range(max(len(units) + last + 1, len(pieces))):
         if turn < len(units):
             u = turn
             p, k = units[u]
             if u + 1 < len(units):
                 fetch(u + 1).start()
+            if u == per_part:
+                fetch_left(0).wait()
             fetch(u).wait()
             if u >= 2:
                 sums[u - 2].wait_send(0)
 
-            def body(n, carry, u=u, p=p):
+            def body(n, carry, u=u):
                 i, j = n // (chunk // tile), n % (chunk // tile)
                 rows = pl.ds(pl.multiple_of(i * (group * depth), 16), group * depth)
                 cols = pl.ds(pl.multiple_of(j * tile, tile), tile)
-                found = dot(lhs[p // 2, rows, :], taken[u % 2, :, cols]).astype(BF16)
+                found = dot(left[rows, :], taken[u % 2, :, cols]).astype(BF16)
                 for g in range(group):
                     part[u % 2, i * group + g, :, cols] = found[g * depth : (g + 1) * depth]
                 return carry
 
             lax.fori_loop(0, dp // group * (chunk // tile), body, 0)
             sums[u].start(0)
-        if turn == 0:
-            terms_copy.wait()
-        if turn % 2 == 0 and turn // 2 < tp - 1:
-            line.step(turn // 2)
+            if u == per_part - 1:
+                fetch_left(0).start()
         for level in range(last + 1):
             u = turn - 1 - level
             if 0 <= u < len(units):
-                p, k = units[u]
-                sums[u].absorb(
-                    level, out.at[p, :, pl.ds(k * chunk, chunk)] if level == last else None
-                )
-    line.total(mlp_out)
+                if level == last:
+                    if u >= 2:
+                        stored(u - 2).wait()
+                    sums[u].absorb(level, block.at[u % 2])
+                    stored(u).start()
+                else:
+                    sums[u].absorb(level)
+        if turn < len(pieces):
+            for piece in pieces[turn]:
+                piece()
     line.finish()
+    down.finish()
     for u in range(len(units)):
+        if u >= len(units) - 2:
+            stored(u).wait()
         for level in range(0 if u >= len(units) - 2 else 1, last + 1):
             sums[u].wait_send(level)
 
 
-def ff_grads(dp, tp, lhs, act, mlp):
-    depth = lhs.shape[1] // dp
-    items, columns = act.shape[1:]
+def backward_part(
+    dp, tp, res, vectors, att, q, kv, cosine, sine, d2, cot, x, lhs, act, mlp, probs, wo, wq, wkv
+):
+    def shape(*dims, kind=BF16):
+        return jax.ShapeDtypeStruct(dims, kind)
+
+    own_rows, width = res.shape
+    depth = width // dp
+    items, padded = act.shape[1:]
+    columns = wq.shape[2]
+    kv_columns = kv.shape[1]
     chunk = 768
-    count = FF_PARTS * columns // chunk
+    count = FF_PARTS * padded // chunk
     vmem = pl.BlockSpec(memory_space=pltpu.VMEM)
+    anywhere = pl.BlockSpec(memory_space=ANY)
     return pl.pallas_call(
-        functools.partial(ff_grad_kernel, dp, tp, chunk),
+        functools.partial(backward_kernel, dp, tp, chunk),
         out_shape=(
-            jax.ShapeDtypeStruct((FF_PARTS, depth, columns), F32),
-            jax.ShapeDtypeStruct(mlp.shape[1:], F32),
+            shape(FF_PARTS, depth, padded, kind=F32),
+            shape(tp - 1, own_rows, width),
+            shape(2, tp - 1, own_rows, width),
+            shape(own_rows, width),
+            shape(own_rows, tp * columns + kv_columns),
+            shape(own_rows, width),
+            shape(own_rows, width),
+            shape(8, width, kind=F32),
         ),
-        in_specs=[vmem, pl.BlockSpec(memory_space=ANY), pl.BlockSpec(memory_space=ANY)],
-        out_specs=(vmem, vmem),
+        in_specs=[vmem] * 7 + [anywhere] * 10,
+        out_specs=(anywhere,) * 3 + (vmem,) * 5,
         scratch_shapes=[
             pltpu.VMEM((2, dp, depth, chunk), BF16),
             pltpu.VMEM((2, items, chunk), BF16),
             pltpu.VMEM((count, dp - 1, depth, chunk), BF16),
-            pltpu.VMEM(mlp.shape, BF16),
-            pltpu.VMEM((2, tp - 1) + mlp.shape[1:], BF16),
+            pltpu.VMEM((width, items), BF16),
+            pltpu.VMEM((2, depth, chunk), F32),
+            pltpu.VMEM((2, own_rows, width), BF16),
+            pltpu.VMEM((2, width, columns), BF16),
+            pltpu.VMEM((width, kv_columns), BF16),
+            pltpu.VMEM((2, own_rows, items), BF16),
+            pltpu.VMEM((own_rows, tp * columns), BF16),
+            pltpu.VMEM((items, kv_columns), F32),
+            pltpu.VMEM((items, kv_columns), BF16),
+            pltpu.VMEM((tp - 1, own_rows, kv_columns), BF16),
+            pltpu.VMEM((own_rows, HEAD_DIMENSION), F32),
+            pltpu.VMEM((own_rows, width), F32),
+            pltpu.VMEM((own_rows, width), BF16),
+            pltpu.VMEM((own_rows, width), F32),
             pltpu.SemaphoreType.DMA((2,)),
             pltpu.SemaphoreType.DMA((count, dp - 1)),
             pltpu.SemaphoreType.DMA((count, dp - 1)),
             pltpu.SemaphoreType.DMA((1,)),
+            pltpu.SemaphoreType.DMA((2,)),
             pltpu.SemaphoreType.DMA((tp - 1,)),
             pltpu.SemaphoreType.DMA((2, tp - 1)),
+            pltpu.SemaphoreType.DMA((2,)),
+            pltpu.SemaphoreType.DMA((2,)),
+            pltpu.SemaphoreType.DMA((2,)),
+            pltpu.SemaphoreType.DMA((tp,)),
+            pltpu.SemaphoreType.DMA((tp - 1,)),
+            pltpu.SemaphoreType.DMA((4,)),
         ],
         compiler_params=pltpu.CompilerParams(
-            collective_id=1, has_side_effects=True, vmem_limit_bytes=56 << 20
+            collective_id=1, has_side_effects=True, vmem_limit_bytes=63 << 20
         ),
-        name="ff_grads",
-    )(lhs, act, mlp)
+        name="backward_part",
+    )(res, vectors, att, q, kv, cosine, sine, d2, cot, x, lhs, act, mlp, probs, wo, wq, wkv)
 
 
 def attn_grad_kernel(
-    dp, tp, widths, grads, kv_out, q_out, o_out,
-    held, own, line_kv, line_qo, send_sem, recv_sem, line_send, line_recv,
+    dp, tp, widths, n1, d_qkv, d_branch, att, vectors, kv_out, q_out, o_out, vectors_out,
+    turned_rows, part, held, own, line_kv, line_qo, vector_sum, vector_got, line_vector,
+    send_sem, recv_sem, line_send, line_recv, vector_send, vector_recv,
 ):
     place = Place(dp, tp)
     z = place.z
-    columns = q_out.shape[1]
+    depth, columns = q_out.shape
+    width = dp * depth
+    heads_width = tp * columns
     barrier = pltpu.get_barrier_semaphore()
     for partner in place.partners + [place.sibling]:
         pl.semaphore_signal(barrier, inc=1, device_id=place.device(partner), device_id_type=MESH)
@@ -981,12 +1270,14 @@
             pl.semaphore_signal(barrier, inc=1, device_id=(place.d, t), device_id_type=MESH)
 
     pl.semaphore_wait(barrier, place.steps + tp)
-    starts = [sum(widths[:u]) for u in range(len(widths))]
+    kinds = (0, 0, 2, 1, 1)
+    halves = (0, 1, 0, 0, 1)
     count = len(widths)
+    group = max(1, 384 // depth)
     sums = [
         PlaneReduce(
             place,
-            lambda b, u=u: grads.at[b, :, pl.ds(starts[u], widths[u])],
+            lambda b, u=u: part.at[u, b, :, pl.ds(0, widths[u])],
             lambda s, u=u: held.at[u, s, :, pl.ds(0, widths[u])],
             lambda s, u=u: send_sem.at[u, s],
             lambda s, u=u: recv_sem.at[u, s],
@@ -994,28 +1285,45 @@
         for u in range(count)
     ]
 
+    def make(u):
+        kind, half = kinds[u], halves[u]
+        left = 1 if kind == 1 else 0
+        right = att if kind == 1 else d_qkv
+        base = heads_width if kind == 2 else half * widths[u]
+
+        def body(i, carry):
+            rows = pl.ds(pl.multiple_of(i * (group * depth), 16), group * depth)
+            for j in range(widths[u] // 256):
+                found = dot(
+                    turned_rows[left, rows, :], right[:, base + j * 256 : base + (j + 1) * 256]
+                ).astype(BF16)
+                for g in range(group):
+                    part[u, i * group + g, :, j * 256 : (j + 1) * 256] = found[
+                        g * depth : (g + 1) * depth
+                    ]
+            return carry
+
+        lax.fori_loop(0, dp // group, body, 0)
+        sums[u].start(0)
+
     def line_copies(u):
         found = []
+        kind, half = kinds[u], halves[u]
         for t in range(tp):
-            if u == 0:
-                src, dst = own.at[0, :, pl.ds(0, widths[0])], line_kv.at[z]
-                found.append((t, remote(
-                    src, dst, line_send.at[u, t], line_recv.at[u, z], (place.d, t)
-                )))
+            if kind == 2:
+                src, dst = own.at[u, :, pl.ds(0, widths[u])], line_kv.at[z]
+            elif t // 2 == half:
+                src, dst = own.at[u, :, pl.ds((t % 2) * columns, columns)], line_qo.at[kind, z]
             else:
-                half, kind = (u - 1) % 2, (u - 1) // 2
-                if t // 2 == half:
-                    src = own.at[u, :, pl.ds((t % 2) * columns, columns)]
-                    dst = line_qo.at[kind, z]
-                    found.append((t, remote(
-                        src, dst, line_send.at[u, t], line_recv.at[1 + kind, z], (place.d, t)
-                    )))
+                continue
+            found.append((t, remote(
+                src, dst, line_send.at[u, t], line_recv.at[kind, z], (place.d, t)
+            )))
         return found
 
     last = place.steps
-    for u in range(count):
-        sums[u].start(0)
-    for turn in range(count + last):
+
+    def work(turn):
         for level in range(last + 1):
             u = turn - level
             if 0 <= u < count:
@@ -1028,6 +1336,51 @@
                         def _():
                             copy.start()
 
+    ways = [place.sibling] + place.partners
+
+    def vector_copy(level):
+        return remote(
+            vectors if level == 0 else vector_sum.at[level - 1],
+            vector_got.at[level],
+            vector_send.at[level],
+            vector_recv.at[level],
+            place.device(ways[level]),
+        )
+
+    def vector_step(level):
+        vector_copy(level).wait_recv()
+        mine = vectors[...] if level == 0 else vector_sum[level - 1]
+        vector_sum[level] = mine + vector_got[level]
+        if level < last:
+            vector_copy(level + 1).start()
+        else:
+            for t in range(tp):
+
+                @pl.when(t != z)
+                def _():
+                    vector_line(t).start()
+
+    def vector_line(t):
+        return remote(
+            vector_sum.at[last],
+            line_vector.at[z],
+            line_send.at[count, t],
+            line_recv.at[3, z],
+            (place.d, t),
+        )
+
+    vector_copy(0).start()
+    turned_rows[0] = n1[...].T
+    make(0)
+    make(1)
+    turned_rows[1] = d_branch[...].T
+    for u in range(2, count):
+        make(u)
+    for turn in range(count + last):
+        work(turn)
+        if turn <= last:
+            vector_step(turn)
+
     def arrived(ref, kind):
         for t in range(tp):
 
@@ -1043,13 +1396,15 @@
             acc = acc + jnp.where(t != z, ref[t].astype(F32), 0.0)
         out[...] = acc
 
-    arrived(line_kv, 0)
-    total(line_kv, own[0, :, : widths[0]], kv_out)
-    for kind, out in ((0, q_out), (1, o_out)):
-        arrived(line_qo.at[kind], 1 + kind)
-        at = pl.ds(pl.multiple_of((z % 2) * columns, 128), columns)
-        mine = own[1 + 2 * kind + z // 2, :, at]
-        total(line_qo.at[kind], mine, out)
+    at = pl.ds(pl.multiple_of((z % 2) * columns, 128), columns)
+    arrived(line_vector, 3)
+    total(line_vector, vector_sum[last], vectors_out)
+    arrived(line_qo.at[0], 0)
+    total(line_qo.at[0], own[z // 2, :, at], q_out)
+    arrived(line_kv, 2)
+    total(line_kv, own[2, :, : widths[2]], kv_out)
+    arrived(line_qo.at[1], 1)
+    total(line_qo.at[1], own[3 + z // 2, :, at], o_out)
     for u in range(count):
         for level in range(last + 1):
             sums[u].wait_send(level)
@@ -1059,37 +1414,57 @@
             def _():
                 copy.wait_send()
 
-
-def attn_grads(dp, tp, grads, side_width):
-    depth, columns = grads.shape[1:]
-    qo_width = (columns - side_width) // 4
-    widths = (side_width,) + (qo_width,) * 4
-    own_width = 2 * qo_width // tp
+    for level in range(last + 1):
+        vector_copy(level).wait_send()
+    for t in range(tp):
+
+        @pl.when(t != z)
+        def _():
+            vector_line(t).wait_send()
+
+
+def attn_grads(dp, tp, n1, d_qkv, d_branch, att, vectors):
+    own_rows, width = n1.shape
+    depth = width // dp
+    heads_width = att.shape[1]
+    kv_columns = d_qkv.shape[1] - heads_width
+    half = heads_width // 2
+    widths = (half, half, kv_columns, half, half)
+    columns = heads_width // tp
+    levels = dp.bit_length() - 1
     vmem = pl.BlockSpec(memory_space=pltpu.VMEM)
     return pl.pallas_call(
         functools.partial(attn_grad_kernel, dp, tp, widths),
         out_shape=(
-            jax.ShapeDtypeStruct((depth, side_width), F32),
-            jax.ShapeDtypeStruct((depth, own_width), F32),
-            jax.ShapeDtypeStruct((depth, own_width), F32),
+            jax.ShapeDtypeStruct((depth, kv_columns), F32),
+            jax.ShapeDtypeStruct((depth, columns), F32),
+            jax.ShapeDtypeStruct((depth, columns), F32),
+            jax.ShapeDtypeStruct(vectors.shape, F32),
         ),
-        in_specs=[vmem],
-        out_specs=(vmem,) * 3,
+        in_specs=[vmem] * 5,
+        out_specs=(vmem,) * 4,
         scratch_shapes=[
-            pltpu.VMEM((5, dp - 1, depth, qo_width), BF16),
-            pltpu.VMEM((5, depth, qo_width), BF16),
-            pltpu.VMEM((tp, depth, side_width), BF16),
-            pltpu.VMEM((2, tp, depth, own_width), BF16),
+            pltpu.VMEM((2, width, own_rows), BF16),
+            pltpu.VMEM((5, dp, depth, half), BF16),
+            pltpu.VMEM((5, dp - 1, depth, half), BF16),
+            pltpu.VMEM((5, depth, half), BF16),
+            pltpu.VMEM((tp, depth, kv_columns), BF16),
+            pltpu.VMEM((2, tp, depth, columns), BF16),
+            pltpu.VMEM((levels,) + vectors.shape, F32),
+            pltpu.VMEM((levels,) + vectors.shape, F32),
+            pltpu.VMEM((tp,) + vectors.shape, F32),
             pltpu.SemaphoreType.DMA((5, dp - 1)),
             pltpu.SemaphoreType.DMA((5, dp - 1)),
-            pltpu.SemaphoreType.DMA((5, tp)),
-            pltpu.SemaphoreType.DMA((3, tp)),
+            pltpu.SemaphoreType.DMA((6, tp)),
+            pltpu.SemaphoreType.DMA((4, tp)),
+            pltpu.SemaphoreType.DMA((levels,)),
+            pltpu.SemaphoreType.DMA((levels,)),
         ],
         compiler_params=pltpu.CompilerParams(
             collective_id=2, has_side_effects=True, vmem_limit_bytes=56 << 20
         ),
         name="attn_grads",
-    )(grads)
+    )(n1, d_qkv, d_branch, att, vectors)
 
 
 def local(
@@ -1144,84 +1519,29 @@
         ff_own,
         cotangent,
     )
-    edge_q = heads_width
-    half_kv = kv_columns // 2
-    items = all_kv.shape[0]
-    qkv_weight = jnp.concatenate(
-        [wq.transpose(1, 0, 2).reshape(width, -1), wkv[:, :kv_columns]], axis=1
+    act, lhs, mlp_terms, d_second = ff_part(dp, tp, ff_all, grad_rows, second_rows)
+    ff_sh, _, _, d_branch, d_qkv, output, input_grad, vector_grads = backward_part(
+        dp, tp, residual, vectors, attended, rot_query, all_kv, cosine, sine,
+        d_second, cotangent, inputs, lhs, act, mlp_terms, probs_low, wo, wq, wkv,
     )
-    out_t_weight = wo.transpose(1, 0, 2).reshape(width, -1)
-    gain_one, gain_two = vectors[0], vectors[1]
-    own_inputs = inputs.astype(F32)
-    cosine, sine = cosine[:, None, : head // 2], sine[:, None, head // 2 :]
-    valid = jnp.arange(items)[:, None] < (rank + 1) * own_rows
-    all_kv = jnp.where(valid, all_kv, 0).reshape(items, 2, KEYVALUE_HEADS, head)
-    keys, value_rows = all_kv[:, 0], all_kv[:, 1]
-    grouped = rot_query.reshape(own_rows, KEYVALUE_HEADS, REPEAT, head)
-    probs_low = jnp.where(valid.T[None], probs_low, 0)
-    probs_low = probs_low.reshape(KEYVALUE_HEADS, REPEAT, own_rows, items)
-    probs = probs_low.astype(F32)
-
-    act, lhs, mlp_terms, d_second = ff_part(dp, tp, ff_all, grad_rows, second_rows)
-    ff_sh, mlp_own = ff_grads(dp, tp, lhs, act, mlp_terms)
-    output = (residual + mlp_own).astype(BF16)
-
-    residual_part, gain_two_grad = norm_back(residual, gain_two, d_second)
-    d_residual = cotangent.astype(F32) + residual_part
-    d_branch = d_residual.astype(BF16)
-    d_attended = dot(d_branch, out_t_weight).astype(BF16)
-    d_att = d_attended.reshape(own_rows, KEYVALUE_HEADS, REPEAT, head)
-    d_probs = jnp.einsum("qgrd,kgd->grqk", d_att, value_rows, preferred_element_type=F32)
-    inner = jnp.sum(probs * d_probs, axis=-1, keepdims=True)
-    d_scores = (scale * probs * (d_probs - inner)).astype(BF16)
-    d_rot_query = jnp.einsum("grqk,kgd->qgrd", d_scores, keys, preferred_element_type=F32)
-    d_keys = jnp.einsum("grqk,qgrd->kgd", d_scores, grouped, preferred_element_type=F32)
-    d_values = jnp.einsum("grqk,qgrd->kgd", probs_low, d_att, preferred_element_type=F32)
-    d_kv = lax.psum_scatter(
-        jnp.concatenate([d_keys.reshape(items, -1), d_values.reshape(items, -1)], axis=1).astype(
-            BF16
-        ),
-        "tensor",
-        scatter_dimension=0,
-        tiled=True,
-    ).astype(F32)
-    d_rot = jnp.concatenate(
-        [
-            d_rot_query.reshape(own_rows, QUERY_HEADS, head),
-            d_kv[:, :half_kv].reshape(own_rows, KEYVALUE_HEADS, head),
-        ],
-        axis=1,
+    kv_sh, q_sh, o_sh, small = attn_grads(
+        dp, tp, normed_own, d_qkv, d_branch, attended, vector_grads
     )
-    d_rot = unrotate(d_rot, cosine, sine).reshape(own_rows, -1)
-    d_qkv = jnp.concatenate([d_rot, d_kv[:, half_kv:]], axis=1).astype(BF16)
-    d_normed = dot_nt(d_qkv, qkv_weight)
-    bias_grad = jnp.sum(d_qkv.astype(F32), axis=0)
-    input_part, gain_one_grad = norm_back(own_inputs, gain_one, d_normed)
-    input_grad = (d_residual + input_part).astype(BF16)
-
-    qkv_grad = dot_tn(normed_own, d_qkv)
-    out_grad = dot_tn(d_branch, attended)
-    qb = bias_grad[:edge_q].reshape(tp, dp, -1).transpose(1, 0, 2).reshape(-1)
-    kvb = jnp.pad(bias_grad[edge_q:].reshape(dp, -1), ((0, 0), (0, depth - kv_columns // dp)))
-    side_grad = jnp.stack([gain_one_grad, gain_two_grad, qb, kvb.reshape(-1)], axis=1)
-    side_grad = jnp.pad(side_grad, ((0, 0), (0, 124)))
-    attn_grad = jnp.concatenate(
-        [qkv_grad[:, edge_q:], side_grad, qkv_grad[:, :edge_q], out_grad], axis=1
-    ).astype(BF16)
-    rest, q_sh, o_sh = attn_grads(
-        dp, tp, attn_grad.reshape(dp, depth, -1), kv_columns + side_grad.shape[1]
-    )
-    side_sh = rest[:, kv_columns : kv_columns + 4].T
+    d = lax.axis_index("dp")
+
+    def mine(row, count, index):
+        return lax.dynamic_slice_in_dim(row, index * count, count, 0)
+
     return (
         output,
         input_grad,
-        side_sh[0],
+        mine(small[0], depth, d),
         q_sh,
-        lax.dynamic_slice_in_dim(side_sh[2], rank * qb_count, qb_count, 0),
-        rest[:, :kv_columns],
-        side_sh[3][: kv_columns // dp],
+        mine(small[2], qb_count, rank * dp + d),
+        kv_sh,
+        mine(small[3], kvb_count, d),
         o_sh.T,
-        side_sh[1],
+        mine(small[1], depth, d),
         ff_sh[:2, :, :hidden_units],
         ff_sh[2, :, :hidden_units].T,
     )

time: 639 us -> 550 us (0.86)
  the two profiles are of different devices: /device:TPU:24 before, /device:TPU:30 now
where the time goes in v3:
time: 550 us; the launch traced here: 541 us
  Pallas kernels  519 us (94%)
  local copies, waits for them, and re-layouts  16 us (3%)
    pallas_call x1, Pallas kernels, forward_part(): pl.pallas_call(functools.partial(forward_kernel, dp, tp, kvb_count, qb_co...  196 us
    pallas_call x1, Pallas kernels, backward_part(): pl.pallas_call(functools.partial(backward_kernel, dp, tp, chunk), out_sha...  127 us
    pallas_call x1, Pallas kernels, attn_grads(): pl.pallas_call(functools.partial(attn_grad_kernel, dp, tp, widths), out_s...  103 us
    pallas_call x1, Pallas kernels, ff_part(): pl.pallas_call(functools.partial(ff_kernel, dp, tp), out_shape=(shape(FF_...  93.4 us

profile of v3, /device:TPU:30, one launch (start us, length us, event | category | flops | bytes accessed | tf_op | source)
XLA Modules:
  0.0 540.7 jit_solution(10952274338287333189)
XLA Ops:
  0.7 0.8 dynamic_slice.23
  1.5 0.8 copy.28.seg_col
  2.3 3.5 fusion.2.ff
  5.8 0.0 copy-done.7
  5.8 0.0 copy-done.9
  5.9 0.1 copy.27
  6.0 0.0 copy-done.5
  6.0 0.7 fusion.4.kvs
  6.7 0.6 pad.16.zb
  7.3 195.7 %forward_part.1 = (bf16[8,3,192,2304]{3,2,1,0:T(8,128)(2,1)}, bf16[4,256,1536]{2,1,0:T(8,128)(2,1)}, bf16[4,256,1536]{2,1,0:T(8,128)(2,1)}, bf16[4,1536,384]{2,1...) custom-call(bf16[256,1536]{1,0:T(8,128)(2,1)} %x.11, ...), custom_call_target="tpu_custom_call" | custom-call | tf_op jit(solution)/shard_map/forward_part/pallas_call | solution.py:497
  203.1 93.4 %ff_part.1 = (bf16[3,1024,2304]{2,1,0:T(8,128)(2,1)}, bf16[2,1536,1024]{2,1,0:T(8,128)(2,1)}, bf16[4,256,1536]{2,1,0:T(8,128)(2,1)}, f32[256,1536]{1,0:T(8,128)}) custom-call(bf16[8,3,192,2304]{3,2,1,0:T(8,128)(2,1)} %get-tuple-element.47.ff, bf16[4,256,1536]{2,1,0:T(8,128)(2,1)} %get-tuple-element.48.cot, bf16[4,256,1536]{2,1,0:T(8,128)(2,1)} %get-tuple-element.49.n2), custom_call_target="tpu_custom_call" | custom-call | tf_op jit(solution)/shard_map/ff_part/pallas_call | solution.py:812
  296.5 127.1 %backward_part.1 = (f32[3,192,2304]{2,1,0:T(8,128)}, bf16[3,256,1536]{2,1,0:T(8,128)(2,1)}, bf16[2,3,256,1536]{3,2,1,0:T(8,128)(2,1)}, bf16[256,1536]{1,0:T(8,12...) custom-call(f32[256,1536]{1,0:T(8,128)} %get-tuple-element.40.res, ...), custom_call_target="tpu_custom_call" | custom-call | tf_op jit(solution)/shard_map/backward_part/pallas_call | solution.py:1200
  423.7 4.0 slice.25
  427.7 103.0 %attn_grads.1 = (f32[192,512]{1,0:T(8,128)}, f32[192,384]{1,0:T(8,128)}, f32[192,384]{1,0:T(8,128)}, f32[8,1536]{1,0:T(8,128)}) custom-call(bf16[256,1536]{1,0:T(8,128)(2,1)} %get-tuple-element.60.n1, bf16[256,2048]{1,0:T(8,128)(2,1)} %get-tuple-element.61.d_qkv, bf16[256,1536]{1,0:T(8,128)(2,1)} %get-tuple-element.62.d_branch, ...), custom_call_target="tpu_custom_call" | custom-call | tf_op jit(solution)/shard_map/attn_grads/pallas_call | solution.py:1436
  530.7 1.0 fusion.7
  531.7 0.6 fusion.5
  532.3 0.6 fusion.6
  532.8 0.6 constant_dynamic-slice_fusion
  533.5 2.9 slice_bitcast_fusion
  536.4 0.9 copy.34
  537.2 0.9 copy.35
  538.1 0.7 copy.36
  538.8 0.7 copy.37
  539.6 0.7 copy.38
  (22 shorter events, 0.1 us)
Async XLA Ops:
  0.6 5.1 copy-start.7
  0.7 5.2 copy-start.8
  0.7 5.2 copy-start.9
  0.7 5.3 copy-start.5
  0.7 6.1 %copy-start.6 = (bf16[48]{0:T(256)(128)(2,1)S(1)}, bf16[48]{0:T(256)(128)(2,1)}, u32[]{:S(2)}) copy-start(bf16[48]{0:T(256)(128)(2,1)} %param.16) | copy-start | bytes 292
  427.7 108.7 %copy-start.1 = (bf16[256,1536]{1,0:T(8,128)(2,1)S(1)}, bf16[256,1536]{1,0:T(8,128)(2,1)}, u32[]{:S(2)}) copy-start(bf16[256,1536]{1,0:T(8,128)(2,1)} %get-tuple-element.86) | copy-start | bytes 2359300
  530.7 6.5 %copy-start = (bf16[256,1536]{1,0:T(8,128)(2,1)S(1)}, bf16[256,1536]{1,0:T(8,128)(2,1)}, u32[]{:S(2)}) copy-start(bf16[256,1536]{1,0:T(8,128)(2,1)} %get-tuple-element.87) | copy-start | bytes 2359300
  533.5 4.6 copy-start.4
  533.5 5.4 copy-start.2
  536.4 3.2 copy-start.3

commit v4 on v3

--- a/solution.py
+++ b/solution.py
@@ -320,7 +320,6 @@
     line_b.start()
     line_q.start()
     plane_kv.start()
-    plane_ff[0].start()
 
     begin = z * own_rows
     row_at = begin + lax.broadcasted_iota(jnp.int32, (own_rows, items), 0)
@@ -340,19 +339,14 @@
     for distance in range(1, tp):
         line_b.hand_on(distance)
     line_q.hand_on(1)
-    line_o.start()
-    for distance in range(2, tp):
+    line_q.hand_on(2)
+    plane_kv.spread()
+    for distance in range(3, tp):
         line_q.hand_on(distance)
+    starts[0].wait()
+    plane_q.start()
     starts[2].wait()
-    starts[0].wait()
     plane_b.start()
-    plane_q.start()
-    plane_kv.spread()
-    for distance in range(1, tp):
-        line_o.hand_on(distance)
-    starts[1].wait()
-    plane_o.start()
-    line_cot.start()
     starts[3].wait()
     plane_kv.complete()
 
@@ -377,9 +371,21 @@
         kv[at, cut] = turned(kv_rows[:, cut], cosine[...], sine[...]).astype(BF16)
     kv[at, KEYVALUE_HEADS * head :] = kv_rows[:, KEYVALUE_HEADS * head :].astype(BF16)
     line_kv.start()
-
+    line_o.start()
+    line_kv.hand_on(1)
     plane_b.spread()
-    plane_q.spread()
+    for mask_of in range(1, 1 << place.steps):
+        if mask_of == plane_q.half - 1:
+            plane_ff[0].start()
+            line_kv.hand_on(2)
+        plane_q.hand_on(mask_of)
+    for distance in range(1, tp):
+        line_o.hand_on(distance)
+    starts[1].wait()
+    plane_o.start()
+    for distance in range(3, tp):
+        line_kv.hand_on(distance)
+    line_cot.start()
     plane_b.complete()
     small_row = lax.broadcasted_iota(jnp.int32, (128, columns), 0)
     small_col = lax.broadcasted_iota(jnp.int32, (128, columns), 1)
@@ -388,10 +394,6 @@
         hit = (small_row < qb_count) & (small_col == small_row + b * qb_count)
         one = jnp.where(hit, 1.0, 0.0).astype(BF16)
         q_bias = q_bias + dot(wb[b].reshape(tp * 16, 128), one)
-    plane_ff[0].spread()
-    plane_ff[1].start()
-    line_kv.hand_on(1)
-    line_cot.hand_on(1)
     plane_q.complete()
     for t in range(tp):
         rows = dot(n1[...], wq[t]) + q_bias[t * 16 : t * 16 + 1, :]
@@ -399,11 +401,6 @@
             cut = slice(h * head, (h + 1) * head)
             out = slice(t * columns + h * head, t * columns + (h + 1) * head)
             q[:, out] = turned(rows[:, cut], cosine[...], sine[...]).astype(BF16)
-    line_kv.hand_on(2)
-    plane_o.spread()
-    for distance in range(3, tp):
-        line_kv.hand_on(distance)
-    line_cot.hand_on(2)
     outs = [
         pltpu.make_async_copy(wq, wq_out, local_sem.at[0]),
         pltpu.make_async_copy(wkv, wkv_out, local_sem.at[3]),
@@ -444,9 +441,10 @@
                 lax.fori_loop(0, group, one_head, 0)
                 probs_copy(part, count).start()
 
-        if part == 0:
-            plane_ff[1].spread()
-            plane_ff[2].start()
+    plane_ff[1].start()
+    line_cot.hand_on(1)
+    plane_o.spread()
+    line_cot.hand_on(2)
     plane_o.complete()
     outs.append(pltpu.make_async_copy(wo, wo_out, local_sem.at[1]))
     outs[-1].start()
@@ -461,11 +459,15 @@
     line_n2.start()
     n2_copy = pltpu.make_async_copy(n2, n2_out.at[z], local_sem.at[2])
     n2_copy.start()
+    plane_ff[0].spread()
+    plane_ff[2].start()
     for distance in range(3, tp):
         line_cot.hand_on(distance)
     line_n2.hand_on(1)
+    plane_ff[1].spread()
+    line_n2.hand_on(2)
     plane_ff[2].spread()
-    for distance in range(2, tp):
+    for distance in range(3, tp):
         line_n2.hand_on(distance)
     for item in plane_ff:
         item.complete()
@@ -513,7 +515,7 @@
             shape(own_rows, head, kind=F32),
             shape(16, width, kind=F32),
         ),
-        in_specs=[vmem] * 7 + [anywhere] * 2,
+        in_specs=[vmem] * 9,
         out_specs=(anywhere,) * 7 + (vmem,) * 8,
         scratch_shapes=[
             pltpu.VMEM((tp, width, columns), BF16),
@@ -955,24 +957,37 @@
     def load_got(side, distance):
         return pltpu.make_async_copy(mlp_got.at[side, distance], stage.at[1], stage_sem.at[1])
 
+    def line_direct(turn):
+        side, offset, distance = line.way(turn)
+
+        @pl.when(jnp.logical_not(place.has(-offset)))
+        def _():
+            remote(
+                mlp.at[line.owner(turn)],
+                mlp_got.at[side, distance - 1],
+                line_send.at[turn],
+                line_recv.at[side, distance - 1],
+                place.beside(offset),
+            ).start()
+
     def line_step(turn):
         side, offset, distance = line.way(turn)
-        load_term(turn).wait()
 
         @pl.when(place.has(-offset))
         def _():
+            load_term(turn).start()
             line.arrival(side, distance).wait_recv()
             load_got(side, distance).start()
+            load_term(turn).wait()
             load_got(side, distance).wait()
             add_into(stage.at[0], stage.at[1], stage.at[0])
-
-        store = pltpu.make_async_copy(stage.at[0], mlp_sent.at[turn], stage_sem.at[0])
-        store.start()
-        store.wait()
-        line.copy(turn).start()
-        load_term(turn + 1).start()
+            store = pltpu.make_async_copy(stage.at[0], mlp_sent.at[turn], stage_sem.at[0])
+            store.start()
+            store.wait()
+            line.copy(turn).start()
 
     def line_total():
+        load_term(tp - 1).start()
         load_term(tp - 1).wait()
         add_into(res, stage.at[0], d_res)
         for side, offset in ((0, -1), (1, 1)):
@@ -986,7 +1001,8 @@
 
         copy_into(d_res, output)
 
-    load_term(0).start()
+    for turn in range(tp - 1):
+        line_direct(turn)
     down = DownReduce(
         place,
         lambda r: d_kv_low.at[pl.ds(pl.multiple_of(r * own_rows, 16), own_rows)],
@@ -1105,13 +1121,13 @@
     per = QUERY_HEADS // tp
     pieces = [
         [second_norm, lambda: attended_grad(range(tp))],
-        [lambda: some_heads(0, 2), lambda: line_step(0)],
-        [lambda: some_heads(2, 4)],
+        [lambda: some_heads(0, 2)],
+        [lambda: some_heads(2, 4), lambda: line_step(0)],
         [lambda: some_heads(4, 6)],
         [lambda: some_heads(6, 8), lambda: line_step(1)],
-        [lambda: some_heads(8, 10)],
+        [lambda: some_heads(8, 10), lambda: line_step(2)],
         [lambda: some_heads(10, 12), send_kv],
-        [lambda: normed_grad(range(tp)), lambda: line_step(2)],
+        [lambda: normed_grad(range(tp))],
         [],
         [first_norm],
         [line_total],

time: 550 us -> 518 us (0.942)
  the two profiles are of different devices: /device:TPU:30 before, /device:TPU:24 now
where the time goes in v4:
time: 518 us; the launch traced here: 509 us
  Pallas kernels  487 us (94%)
  local copies, waits for them, and re-layouts  16 us (3%)
    pallas_call x1, Pallas kernels, forward_part(): pl.pallas_call(functools.partial(forward_kernel, dp, tp, kvb_count, qb_co...  171 us
    pallas_call x1, Pallas kernels, backward_part(): pl.pallas_call(functools.partial(backward_kernel, dp, tp, chunk), out_sha...  120 us
    pallas_call x1, Pallas kernels, ff_part(): pl.pallas_call(functools.partial(ff_kernel, dp, tp), out_shape=(shape(FF_...  98.1 us
    pallas_call x1, Pallas kernels, attn_grads(): pl.pallas_call(functools.partial(attn_grad_kernel, dp, tp, widths), out_s...  98.1 us

profile of v4, /device:TPU:24, one launch (start us, length us, event | category | flops | bytes accessed | tf_op | source)
XLA Modules:
  0.0 508.8 jit_solution(10045065632617882959)
XLA Ops:
  0.6 0.0 copy-start.7
  0.7 0.8 dynamic_slice.23
  1.5 0.8 copy.28.seg_col
  2.3 3.5 fusion.2.ff
  5.9 0.1 copy.27
  6.0 0.7 fusion.4.kvs
  6.7 0.6 pad.16.zb
  7.3 171.0 %forward_part.1 = (bf16[8,3,192,2304]{3,2,1,0:T(8,128)(2,1)}, bf16[4,256,1536]{2,1,0:T(8,128)(2,1)}, bf16[4,256,1536]{2,1,0:T(8,128)(2,1)}, bf16[4,1536,384]{2,1...) custom-call(bf16[256,1536]{1,0:T(8,128)(2,1)} %x.11, ...), custom_call_target="tpu_custom_call" | custom-call | tf_op jit(solution)/shard_map/forward_part/pallas_call | solution.py:499
  178.3 98.1 %ff_part.1 = (bf16[3,1024,2304]{2,1,0:T(8,128)(2,1)}, bf16[2,1536,1024]{2,1,0:T(8,128)(2,1)}, bf16[4,256,1536]{2,1,0:T(8,128)(2,1)}, f32[256,1536]{1,0:T(8,128)}) custom-call(bf16[8,3,192,2304]{3,2,1,0:T(8,128)(2,1)} %get-tuple-element.47.ff, bf16[4,256,1536]{2,1,0:T(8,128)(2,1)} %get-tuple-element.48.cot, bf16[4,256,1536]{2,1,0:T(8,128)(2,1)} %get-tuple-element.49.n2), custom_call_target="tpu_custom_call" | custom-call | tf_op jit(solution)/shard_map/ff_part/pallas_call | solution.py:814
  276.5 120.1 %backward_part.1 = (f32[3,192,2304]{2,1,0:T(8,128)}, bf16[3,256,1536]{2,1,0:T(8,128)(2,1)}, bf16[2,3,256,1536]{3,2,1,0:T(8,128)(2,1)}, bf16[256,1536]{1,0:T(8,12...) custom-call(f32[256,1536]{1,0:T(8,128)} %get-tuple-element.40.res, ...), custom_call_target="tpu_custom_call" | custom-call | tf_op jit(solution)/shard_map/backward_part/pallas_call | solution.py:1216
  396.6 4.0 slice.25
  400.6 98.1 %attn_grads.1 = (f32[192,512]{1,0:T(8,128)}, f32[192,384]{1,0:T(8,128)}, f32[192,384]{1,0:T(8,128)}, f32[8,1536]{1,0:T(8,128)}) custom-call(bf16[256,1536]{1,0:T(8,128)(2,1)} %get-tuple-element.60.n1, bf16[256,2048]{1,0:T(8,128)(2,1)} %get-tuple-element.61.d_qkv, bf16[256,1536]{1,0:T(8,128)(2,1)} %get-tuple-element.62.d_branch, ...), custom_call_target="tpu_custom_call" | custom-call | tf_op jit(solution)/shard_map/attn_grads/pallas_call | solution.py:1452
  498.7 1.0 fusion.7
  499.7 0.6 fusion.5
  500.3 0.6 fusion.6
  500.9 0.6 constant_dynamic-slice_fusion
  501.5 2.9 slice_bitcast_fusion
  504.4 0.9 copy.34
  505.3 0.0 copy-done
  505.3 0.9 copy.35
  506.1 0.7 copy.36
  506.9 0.7 copy.37
  507.6 0.0 copy-done.3
  507.6 0.7 copy.38
  (22 shorter events, 0.1 us)
Async XLA Ops:
  0.6 5.1 %copy-start.7 = (bf16[64]{0:T(256)(128)(2,1)S(1)}, bf16[64]{0:T(256)(128)(2,1)}, u32[]{:S(2)}) copy-start(bf16[64]{0:T(256)(128)(2,1)} %param.18) | copy-start | bytes 388
  0.7 5.2 %copy-start.8 = (bf16[192]{0:T(256)(128)(2,1)S(1)}, bf16[192]{0:T(256)(128)(2,1)}, u32[]{:S(2)}) copy-start(bf16[192]{0:T(256)(128)(2,1)} %param.14) | copy-start | bytes 1156
  0.7 5.2 %copy-start.9 = (bf16[192]{0:T(256)(128)(2,1)S(1)}, bf16[192]{0:T(256)(128)(2,1)}, u32[]{:S(2)}) copy-start(bf16[192]{0:T(256)(128)(2,1)} %param.20) | copy-start | bytes 1156
  0.7 5.3 %copy-start.5 = (bf16[192,512]{1,0:T(8,128)(2,1)S(1)}, bf16[192,512]{1,0:T(8,128)(2,1)}, u32[]{:S(2)}) copy-start(bf16[192,512]{1,0:T(8,128)(2,1)} %param.17) | copy-start | bytes 589828
  0.7 6.1 %copy-start.6 = (bf16[48]{0:T(256)(128)(2,1)S(1)}, bf16[48]{0:T(256)(128)(2,1)}, u32[]{:S(2)}) copy-start(bf16[48]{0:T(256)(128)(2,1)} %param.16) | copy-start | bytes 292
  400.6 103.8 %copy-start.1 = (bf16[256,1536]{1,0:T(8,128)(2,1)S(1)}, bf16[256,1536]{1,0:T(8,128)(2,1)}, u32[]{:S(2)}) copy-start(bf16[256,1536]{1,0:T(8,128)(2,1)} %get-tuple-element.86) | copy-start | bytes 2359300
  498.7 6.5 %copy-start = (bf16[256,1536]{1,0:T(8,128)(2,1)S(1)}, bf16[256,1536]{1,0:T(8,128)(2,1)}, u32[]{:S(2)}) copy-start(bf16[256,1536]{1,0:T(8,128)(2,1)} %get-tuple-element.87) | copy-start | bytes 2359300
  501.5 4.6 copy-start.4
  501.5 5.4 %copy-start.2 = (f32[192,512]{1,0:T(8,128)S(1)}, f32[192,512]{1,0:T(8,128)}, u32[]{:S(2)}) copy-start(f32[192,512]{1,0:T(8,128)} %get-tuple-element.91) | copy-start | bytes 1179652
  504.4 3.2 copy-start.3

commit v5 on v4

--- a/solution.py
+++ b/solution.py
@@ -637,22 +637,22 @@
             ref, ref, self.send(0), self.recv(side, distance), self.place.beside(0)
         )
 
-    def step(self, turn):
+    def direct(self, turn):
         side, offset, distance = self.way(turn)
-        fed = self.place.has(-offset)
-
-        @pl.when(fed)
+
+        @pl.when(jnp.logical_not(self.place.has(-offset)))
+        def _():
+            copy_into(self.term(turn), self.sent(turn))
+            self.copy(turn).start()
+
+    def added(self, turn):
+        side, offset, distance = self.way(turn)
+
+        @pl.when(self.place.has(-offset))
         def _():
             self.arrival(side, distance).wait_recv()
             add_into(self.term(turn), self.got(side, distance), self.sent(turn))
-
-        if self.term is not self.sent:
-
-            @pl.when(jnp.logical_not(fed))
-            def _():
-                copy_into(self.term(turn), self.sent(turn))
-
-        self.copy(turn).start()
+            self.copy(turn).start()
 
     def total(self, out):
         last = self.place.tp - 1
@@ -691,15 +691,19 @@
     depth = ff.shape[2]
     padded = ff.shape[3]
     tile = 256
+    third = padded // 3
     weights = (wg, wu, wd)
     loads = [
         [
             pltpu.make_async_copy(
-                ff.at[b, p], weights[p].at[pl.ds(b * depth, depth)], w_sem.at[p, b]
+                ff.at[b, p, :, pl.ds(c * third, third)],
+                weights[p].at[pl.ds(b * depth, depth), pl.ds(c * third, third)],
+                w_sem.at[p, b, c],
             )
+            for p in range(FF_PARTS)
             for b in range(dp)
         ]
-        for p in range(FF_PARTS)
+        for c in range(3)
     ]
     sums = LineReduce(
         place,
@@ -759,10 +763,6 @@
         turned_rows[slot, 1] = ct[slot].T
         for copy in stores(turn, (1,))[0]:
             copy.start()
-        if turn == 0:
-            for part in loads:
-                for copy in part:
-                    copy.wait()
 
         def units(n, carry, slot=slot):
             for k in range(3):
@@ -779,7 +779,15 @@
                 ).astype(BF16)
             return carry
 
-        lax.fori_loop(0, padded // (3 * tile), units, 0)
+        if turn == 0:
+            for c in range(3):
+                for copy in loads[c]:
+                    copy.wait()
+                lax.fori_loop(
+                    c * (third // (3 * tile)), (c + 1) * (third // (3 * tile)), units, 0
+                )
+        else:
+            lax.fori_loop(0, padded // (3 * tile), units, 0)
 
         def columns(n, carry, slot=slot):
             at = pl.ds(pl.multiple_of(n * tile, tile), tile)
@@ -789,12 +797,16 @@
             branch[slot, :, at] = dot_nt(made[slot, 2], wd[at, :]).astype(BF16)
             return carry
 
-        if turn > 0:
-            sums.step(turn - 1)
         lax.fori_loop(0, width // tile, columns, 0)
+        if turn < tp - 1:
+            sums.direct(turn)
         for copies in stores(turn, (0, 2)):
             for copy in copies:
                 copy.start()
+        if 0 < turn < tp - 1:
+            sums.added(turn - 1)
+        if turn == tp - 2:
+            sums.added(turn)
     sums.total(d2)
     sums.finish()
     for turn in range(tp - 2, tp):
@@ -833,7 +845,7 @@
             pltpu.VMEM((2, tp - 1, own_rows, width), BF16),
             pltpu.VMEM((2, own_rows, width), BF16),
             pltpu.VMEM((2, 2, width, own_rows), BF16),
-            pltpu.SemaphoreType.DMA((FF_PARTS, dp)),
+            pltpu.SemaphoreType.DMA((FF_PARTS, dp, 3)),
             pltpu.SemaphoreType.DMA((2, 2)),
             pltpu.SemaphoreType.DMA((2, FF_PARTS)),
             pltpu.SemaphoreType.DMA((2, 2)),

time: 518 us -> 497 us (0.959)
  Pallas kernels: 487 us -> 466 us
    pallas_call x1, Pallas kernels: 98.1 us -> 78.7 us  [ff_part(): pl.pallas_call(functools.partial(ff_kernel, dp, tp), out_shape=(shape(FF_...]
where the time goes in v5:
time: 497 us; the launch traced here: 488 us
  Pallas kernels  466 us (94%)
  local copies, waits for them, and re-layouts  16 us (3%)
    pallas_call x1, Pallas kernels, forward_part(): pl.pallas_call(functools.partial(forward_kernel, dp, tp, kvb_count, qb_co...  171 us
    pallas_call x1, Pallas kernels, backward_part(): pl.pallas_call(functools.partial(backward_kernel, dp, tp, chunk), out_sha...  122 us
    pallas_call x1, Pallas kernels, attn_grads(): pl.pallas_call(functools.partial(attn_grad_kernel, dp, tp, widths), out_s...  94.6 us
    pallas_call x1, Pallas kernels, ff_part(): pl.pallas_call(functools.partial(ff_kernel, dp, tp), out_shape=(shape(FF_...  78.7 us

profile of v5, /device:TPU:24, one launch (start us, length us, event | category | flops | bytes accessed | tf_op | source)
XLA Modules:
  0.0 487.9 jit_solution(17052940191910491750)
XLA Ops:
  0.6 0.0 copy-start.7
  0.7 0.0 copy-start.8
  0.7 0.0 copy-start.9
  0.7 0.8 dynamic_slice.23
  1.5 0.8 copy.28.seg_col
  2.3 3.5 fusion.2.ff
  5.9 0.1 copy.27
  6.0 0.7 fusion.4.kvs
  6.7 0.6 pad.16.zb
  7.3 171.0 %forward_part.1 = (bf16[8,3,192,2304]{3,2,1,0:T(8,128)(2,1)}, bf16[4,256,1536]{2,1,0:T(8,128)(2,1)}, bf16[4,256,1536]{2,1,0:T(8,128)(2,1)}, bf16[4,1536,384]{2,1...) custom-call(bf16[256,1536]{1,0:T(8,128)(2,1)} %x.11, ...), custom_call_target="tpu_custom_call" | custom-call | tf_op jit(solution)/shard_map/forward_part/pallas_call | solution.py:499
  178.3 78.7 %ff_part.1 = (bf16[3,1024,2304]{2,1,0:T(8,128)(2,1)}, bf16[2,1536,1024]{2,1,0:T(8,128)(2,1)}, bf16[4,256,1536]{2,1,0:T(8,128)(2,1)}, f32[256,1536]{1,0:T(8,128)}) custom-call(bf16[8,3,192,2304]{3,2,1,0:T(8,128)(2,1)} %get-tuple-element.47.ff, bf16[4,256,1536]{2,1,0:T(8,128)(2,1)} %get-tuple-element.48.cot, bf16[4,256,1536]{2,1,0:T(8,128)(2,1)} %get-tuple-element.49.n2), custom_call_target="tpu_custom_call" | custom-call | tf_op jit(solution)/shard_map/ff_part/pallas_call | solution.py:826
  257.0 122.2 %backward_part.1 = (f32[3,192,2304]{2,1,0:T(8,128)}, bf16[3,256,1536]{2,1,0:T(8,128)(2,1)}, bf16[2,3,256,1536]{3,2,1,0:T(8,128)(2,1)}, bf16[256,1536]{1,0:T(8,12...) custom-call(f32[256,1536]{1,0:T(8,128)} %get-tuple-element.40.res, ...), custom_call_target="tpu_custom_call" | custom-call | tf_op jit(solution)/shard_map/backward_part/pallas_call | solution.py:1228
  379.2 4.0 slice.25
  383.2 94.6 %attn_grads.1 = (f32[192,512]{1,0:T(8,128)}, f32[192,384]{1,0:T(8,128)}, f32[192,384]{1,0:T(8,128)}, f32[8,1536]{1,0:T(8,128)}) custom-call(bf16[256,1536]{1,0:T(8,128)(2,1)} %get-tuple-element.60.n1, bf16[256,2048]{1,0:T(8,128)(2,1)} %get-tuple-element.61.d_qkv, bf16[256,1536]{1,0:T(8,128)(2,1)} %get-tuple-element.62.d_branch, ...), custom_call_target="tpu_custom_call" | custom-call | tf_op jit(solution)/shard_map/attn_grads/pallas_call | solution.py:1464
  477.8 1.0 fusion.7
  478.8 0.6 fusion.5
  479.4 0.6 fusion.6
  480.0 0.6 constant_dynamic-slice_fusion
  480.6 2.9 slice_bitcast_fusion
  483.5 0.9 copy.34
  484.4 0.9 copy.35
  485.3 0.7 copy.36
  486.0 0.7 copy.37
  486.7 0.7 copy.38
  (22 shorter events, 0.1 us)
Async XLA Ops:
  0.6 5.1 %copy-start.7 = (bf16[64]{0:T(256)(128)(2,1)S(1)}, bf16[64]{0:T(256)(128)(2,1)}, u32[]{:S(2)}) copy-start(bf16[64]{0:T(256)(128)(2,1)} %param.18) | copy-start | bytes 388
  0.7 5.2 %copy-start.8 = (bf16[192]{0:T(256)(128)(2,1)S(1)}, bf16[192]{0:T(256)(128)(2,1)}, u32[]{:S(2)}) copy-start(bf16[192]{0:T(256)(128)(2,1)} %param.14) | copy-start | bytes 1156
  0.7 5.2 %copy-start.9 = (bf16[192]{0:T(256)(128)(2,1)S(1)}, bf16[192]{0:T(256)(128)(2,1)}, u32[]{:S(2)}) copy-start(bf16[192]{0:T(256)(128)(2,1)} %param.20) | copy-start | bytes 1156
  0.7 5.3 %copy-start.5 = (bf16[192,512]{1,0:T(8,128)(2,1)S(1)}, bf16[192,512]{1,0:T(8,128)(2,1)}, u32[]{:S(2)}) copy-start(bf16[192,512]{1,0:T(8,128)(2,1)} %param.17) | copy-start | bytes 589828
  0.7 6.1 %copy-start.6 = (bf16[48]{0:T(256)(128)(2,1)S(1)}, bf16[48]{0:T(256)(128)(2,1)}, u32[]{:S(2)}) copy-start(bf16[48]{0:T(256)(128)(2,1)} %param.16) | copy-start | bytes 292
  383.2 100.3 %copy-start.1 = (bf16[256,1536]{1,0:T(8,128)(2,1)S(1)}, bf16[256,1536]{1,0:T(8,128)(2,1)}, u32[]{:S(2)}) copy-start(bf16[256,1536]{1,0:T(8,128)(2,1)} %get-tuple-element.86) | copy-start | bytes 2359300
  477.8 6.5 %copy-start = (bf16[256,1536]{1,0:T(8,128)(2,1)S(1)}, bf16[256,1536]{1,0:T(8,128)(2,1)}, u32[]{:S(2)}) copy-start(bf16[256,1536]{1,0:T(8,128)(2,1)} %get-tuple-element.87) | copy-start | bytes 2359300
  480.6 4.6 copy-start.4
  480.6 5.4 %copy-start.2 = (f32[192,512]{1,0:T(8,128)S(1)}, f32[192,512]{1,0:T(8,128)}, u32[]{:S(2)}) copy-start(f32[192,512]{1,0:T(8,128)} %get-tuple-element.91) | copy-start | bytes 1179652
  483.5 3.2 copy-start.3

commit v6 on v5

--- a/solution.py
+++ b/solution.py
@@ -1402,10 +1402,10 @@
     make(0)
     make(1)
     turned_rows[1] = d_branch[...].T
-    for u in range(2, count):
-        make(u)
     for turn in range(count + last):
         work(turn)
+        if turn + 2 < count:
+            make(turn + 2)
         if turn <= last:
             vector_step(turn)
 

time: 497 us -> 496 us (level)
  no operation moved by 1% of the time
where the time goes in v6:
time: 496 us; the launch traced here: 486 us
  Pallas kernels  465 us (94%)
  local copies, waits for them, and re-layouts  16 us (3%)
    pallas_call x1, Pallas kernels, forward_part(): pl.pallas_call(functools.partial(forward_kernel, dp, tp, kvb_count, qb_co...  171 us
    pallas_call x1, Pallas kernels, backward_part(): pl.pallas_call(functools.partial(backward_kernel, dp, tp, chunk), out_sha...  122 us
    pallas_call x1, Pallas kernels, attn_grads(): pl.pallas_call(functools.partial(attn_grad_kernel, dp, tp, widths), out_s...  93 us
    pallas_call x1, Pallas kernels, ff_part(): pl.pallas_call(functools.partial(ff_kernel, dp, tp), out_shape=(shape(FF_...  78.7 us

profile of v6, /device:TPU:24, one launch (start us, length us, event | category | flops | bytes accessed | tf_op | source)
XLA Modules:
  0.0 486.3 jit_solution(15113668183782127703)
XLA Ops:
  0.6 0.0 copy-start.7
  0.7 0.0 copy-start.8
  0.7 0.0 copy-start.9
  0.7 0.8 dynamic_slice.23
  1.5 0.8 copy.28.seg_col
  2.3 3.5 fusion.2.ff
  5.9 0.1 copy.27
  6.0 0.7 fusion.4.kvs
  6.7 0.6 pad.16.zb
  7.3 171.0 %forward_part.1 = (bf16[8,3,192,2304]{3,2,1,0:T(8,128)(2,1)}, bf16[4,256,1536]{2,1,0:T(8,128)(2,1)}, bf16[4,256,1536]{2,1,0:T(8,128)(2,1)}, bf16[4,1536,384]{2,1...) custom-call(bf16[256,1536]{1,0:T(8,128)(2,1)} %x.11, ...), custom_call_target="tpu_custom_call" | custom-call | tf_op jit(solution)/shard_map/forward_part/pallas_call | solution.py:499
  178.3 78.7 %ff_part.1 = (bf16[3,1024,2304]{2,1,0:T(8,128)(2,1)}, bf16[2,1536,1024]{2,1,0:T(8,128)(2,1)}, bf16[4,256,1536]{2,1,0:T(8,128)(2,1)}, f32[256,1536]{1,0:T(8,128)}) custom-call(bf16[8,3,192,2304]{3,2,1,0:T(8,128)(2,1)} %get-tuple-element.47.ff, bf16[4,256,1536]{2,1,0:T(8,128)(2,1)} %get-tuple-element.48.cot, bf16[4,256,1536]{2,1,0:T(8,128)(2,1)} %get-tuple-element.49.n2), custom_call_target="tpu_custom_call" | custom-call | tf_op jit(solution)/shard_map/ff_part/pallas_call | solution.py:826
  257.0 122.2 %backward_part.1 = (f32[3,192,2304]{2,1,0:T(8,128)}, bf16[3,256,1536]{2,1,0:T(8,128)(2,1)}, bf16[2,3,256,1536]{3,2,1,0:T(8,128)(2,1)}, bf16[256,1536]{1,0:T(8,12...) custom-call(f32[256,1536]{1,0:T(8,128)} %get-tuple-element.40.res, ...), custom_call_target="tpu_custom_call" | custom-call | tf_op jit(solution)/shard_map/backward_part/pallas_call | solution.py:1228
  379.2 4.0 slice.25
  383.2 93.0 %attn_grads.1 = (f32[192,512]{1,0:T(8,128)}, f32[192,384]{1,0:T(8,128)}, f32[192,384]{1,0:T(8,128)}, f32[8,1536]{1,0:T(8,128)}) custom-call(bf16[256,1536]{1,0:T(8,128)(2,1)} %get-tuple-element.60.n1, bf16[256,2048]{1,0:T(8,128)(2,1)} %get-tuple-element.61.d_qkv, bf16[256,1536]{1,0:T(8,128)(2,1)} %get-tuple-element.62.d_branch, ...), custom_call_target="tpu_custom_call" | custom-call | tf_op jit(solution)/shard_map/attn_grads/pallas_call | solution.py:1464
  476.2 1.0 fusion.7
  477.2 0.6 fusion.5
  477.8 0.6 fusion.6
  478.4 0.6 constant_dynamic-slice_fusion
  479.0 2.9 slice_bitcast_fusion
  481.9 0.9 copy.34
  482.8 0.9 copy.35
  483.7 0.7 copy.36
  484.4 0.7 copy.37
  485.1 0.7 copy.38
  (22 shorter events, 0.1 us)
Async XLA Ops:
  0.6 5.1 %copy-start.7 = (bf16[64]{0:T(256)(128)(2,1)S(1)}, bf16[64]{0:T(256)(128)(2,1)}, u32[]{:S(2)}) copy-start(bf16[64]{0:T(256)(128)(2,1)} %param.18) | copy-start | bytes 388
  0.7 5.2 %copy-start.8 = (bf16[192]{0:T(256)(128)(2,1)S(1)}, bf16[192]{0:T(256)(128)(2,1)}, u32[]{:S(2)}) copy-start(bf16[192]{0:T(256)(128)(2,1)} %param.14) | copy-start | bytes 1156
  0.7 5.2 %copy-start.9 = (bf16[192]{0:T(256)(128)(2,1)S(1)}, bf16[192]{0:T(256)(128)(2,1)}, u32[]{:S(2)}) copy-start(bf16[192]{0:T(256)(128)(2,1)} %param.20) | copy-start | bytes 1156
  0.7 5.3 %copy-start.5 = (bf16[192,512]{1,0:T(8,128)(2,1)S(1)}, bf16[192,512]{1,0:T(8,128)(2,1)}, u32[]{:S(2)}) copy-start(bf16[192,512]{1,0:T(8,128)(2,1)} %param.17) | copy-start | bytes 589828
  0.7 6.1 %copy-start.6 = (bf16[48]{0:T(256)(128)(2,1)S(1)}, bf16[48]{0:T(256)(128)(2,1)}, u32[]{:S(2)}) copy-start(bf16[48]{0:T(256)(128)(2,1)} %param.16) | copy-start | bytes 292
  383.2 98.7 %copy-start.1 = (bf16[256,1536]{1,0:T(8,128)(2,1)S(1)}, bf16[256,1536]{1,0:T(8,128)(2,1)}, u32[]{:S(2)}) copy-start(bf16[256,1536]{1,0:T(8,128)(2,1)} %get-tuple-element.86) | copy-start | bytes 2359300
  476.2 6.5 %copy-start = (bf16[256,1536]{1,0:T(8,128)(2,1)S(1)}, bf16[256,1536]{1,0:T(8,128)(2,1)}, u32[]{:S(2)}) copy-start(bf16[256,1536]{1,0:T(8,128)(2,1)} %get-tuple-element.87) | copy-start | bytes 2359300
  479.0 4.6 copy-start.4
  479.0 5.4 %copy-start.2 = (f32[192,512]{1,0:T(8,128)S(1)}, f32[192,512]{1,0:T(8,128)}, u32[]{:S(2)}) copy-start(f32[192,512]{1,0:T(8,128)} %get-tuple-element.91) | copy-start | bytes 1179652
  481.9 3.2 copy-start.3
